TPU v7x, 32 devices: a whole 2x2x4 slice. The times are simulated.
32 devices in a mesh: trade: 8 (over z, y), scen: 4 (over x, core).
Axes of the slice: x: 2, y: 2, z: 4, core: 2. Of those that a mesh axis runs over, the one named last changes fastest.
Arguments:
- log_vol: float32 [256, 2048], P('trade'), may hold values from -2.3 to -0.5
- beta: float32 [256], P('trade'), may hold values from 0.5 to 2
- shock_table: bfloat16 [512, 2048], replicated, may hold values from -0.29882812 to 0.3984375
- scen_ids: int32 [8], P('scen'), may hold values from 0 to 511
- hot_index: int32 [16], P('trade'), may hold values from 0 to 31
- dest: int32 [65536, 1], P('trade'), may hold values from 0 to 7; in each aligned block of 2048 rows (0 to 2047, 2048 to 4095, ...) at most 512 rows name the same one
- pick: int32 [65536], P('trade'), may hold values from 0 to 35
- expiry_cell: int32 [65536], P('trade'), may hold values from 1 to 61
- strike_cell: int32 [65536], P('trade'), may hold values from 1 to 29
- frac_e: float32 [65536], P('trade'), may hold values from 0 to 1
- frac_k: float32 [65536], P('trade'), may hold values from 0 to 1
- notional: float32 [65536], P('trade'), may hold values from -12 to 12
- forward: float32 [65536], P('trade'), may hold values from 0.5 to 2
Outputs:
- price_out: float32 [8, 65536], P('scen', 'trade')
- vega_out: float32 [8, 65536], P('scen', 'trade')
- delta_out: float32 [8, 65536], P('scen', 'trade')
Inputs may be any that keep to these rules, and one draw needn't show every extreme that they name: `dest`: within each aligned block of 2048 trades no device is named by more than 512 trades, and some device is named exactly 512 times.
All inputs are finite; a program needn't handle non-finite values.
Results may differ from a plain program's by a relative error of at most 0.0031.
Values may be sent and summed in bfloat16 or wider, within the bound.
No kernel may reach another device: no remote copies, remote signals or barrier semaphores. Data moves between devices by JAX's collectives and lax.ppermute only.
A program may use at most 128 MiB of HBM per device.

v0:
```python
import jax
import jax.numpy as jnp
from jax import lax
from jax.sharding import PartitionSpec as P

NE = 64
NK = 32
HOT = 2


RATE = 0.03
INV_ROOT_TWO = 0.7071067811865476
INV_ROOT_TAU = 0.3989422804014327


def with_halo(cells, sides, width):
    for axis, dim in sides:
        count = lax.axis_size(axis)
        head = lax.slice_in_dim(cells, 0, width, axis=dim)
        tail = lax.slice_in_dim(cells, cells.shape[dim] - width, cells.shape[dim], axis=dim)
        cells = jnp.concatenate(
            [
                lax.ppermute(tail, axis, [(i, (i + 1) % count) for i in range(count)]),
                cells,
                lax.ppermute(head, axis, [((i + 1) % count, i) for i in range(count)]),
            ],
            axis=dim,
        )
    return cells


def spline_weights(offset):
    square = offset * offset
    offset_cube = square * offset
    return (
        0.5 * (2.0 * square - offset_cube - offset),
        0.5 * (3.0 * offset_cube - 5.0 * square + 2.0),
        0.5 * (4.0 * square - 3.0 * offset_cube + offset),
        0.5 * (offset_cube - square),
    )


def black_model(log_sigma, expiry_cell, frac_e, strike_cell, frac_k, notional, forward):
    maturity = (expiry_cell + frac_e + 1.0) * (4.0 / NE)
    moneyness = (strike_cell + frac_k - 0.5 * (NK - 1)) / NK
    root_time = jnp.sqrt(maturity)
    spread = jnp.exp(log_sigma) * root_time
    upper_d = -moneyness / spread + 0.5 * spread
    minus_term_black = upper_d - spread
    discount_factor = jnp.exp(-RATE * maturity)
    cdf_upper = 0.5 * lax.erfc(-upper_d * INV_ROOT_TWO)
    cdf_lower = 0.5 * lax.erfc(-minus_term_black * INV_ROOT_TWO)
    scaled = notional * discount_factor
    price_out = scaled * forward * (cdf_upper - jnp.exp(moneyness) * cdf_lower)
    vega_out = scaled * forward * INV_ROOT_TAU * jnp.exp(-0.5 * upper_d * upper_d) * root_time
    delta_out = scaled * cdf_upper
    return (price_out, vega_out, delta_out)


def place_rows(row_total, centre, weights):
    row_grid = lax.broadcasted_iota(jnp.float32, (row_total, centre.shape[0]), 0)
    placed = jnp.zeros(row_grid.shape, weights[0].dtype)
    for position in range(4):
        matched_rows = row_grid == (centre - 1.0 + position)[None, :]
        placed = placed + jnp.where(
            matched_rows, weights[position][None, :], jnp.zeros((), weights[0].dtype)
        )
    return placed


def held_surfaces(log_vol, beta, shock_table, scenario_ids, hot_index):
    choose = (
        scenario_ids[:, None] == jnp.arange(shock_table.shape[0], dtype=jnp.int32)[None, :]
    ).astype(jnp.bfloat16)
    shifts = jnp.dot(choose, shock_table, preferred_element_type=jnp.float32)
    shocked = (log_vol[None] + beta[None, :, None] * shifts[:, None, :]).astype(jnp.bfloat16)
    hot_rows = jnp.take(shocked, hot_index, axis=1)
    extended = with_halo(hot_rows, (("trade", 1),), HOT)
    held_rows = jnp.concatenate([shocked, extended[:, :HOT], extended[:, 2 * HOT :]], axis=1)
    stress_case_number = held_rows.shape[0]
    held_count = held_rows.shape[1]
    return held_rows.reshape(stress_case_number, held_count * NE, NK)


def evaluate(held_surface, columns):
    packed = columns[0]
    frac_e = columns[1]
    frac_k = columns[2]
    row_code = jnp.floor(packed / NK)
    strike_cell = packed - row_code * NK
    expiry_cell = row_code - jnp.floor(row_code / NE) * NE
    weights_e = tuple((weight.astype(jnp.bfloat16) for weight in spline_weights(frac_e)))
    right_side = place_rows(held_surface.shape[1], row_code, weights_e)
    mixed_rows = jnp.einsum(
        "shk,hn->skn", held_surface, right_side, preferred_element_type=jnp.float32
    )
    strike_interp_coefs = place_rows(NK, strike_cell, spline_weights(frac_k))
    log_sigma = jnp.sum(mixed_rows * strike_interp_coefs[None], axis=1)
    return jnp.stack(
        black_model(log_sigma, expiry_cell, frac_e, strike_cell, frac_k, columns[3], columns[4])
    )


def evaluate_items(held_surface, stress_case_number, received):
    field_count = received.shape[0]
    slot_total = received.shape[1] * received.shape[2]
    block_size = 512
    flat_fields = received.reshape(field_count, slot_total)
    result_rows = 3 * stress_case_number

    def run_block(block, results):
        columns = lax.dynamic_slice_in_dim(flat_fields, block * block_size, block_size, 1)
        values = evaluate(held_surface, columns).reshape(result_rows, block_size)
        return lax.dynamic_update_slice_in_dim(results, values, block * block_size, 1)

    results = lax.fori_loop(
        0, slot_total // block_size, run_block, jnp.zeros((result_rows, slot_total), jnp.float32)
    )
    return results.reshape(result_rows, received.shape[1], received.shape[2])


def shards(
    log_vol,
    beta,
    shock_table,
    scen_ids,
    hot_index,
    dest,
    pick,
    expiry_cell,
    strike_cell,
    frac_e,
    frac_k,
    notional,
    forward,
):
    partner_number = lax.axis_size("trade")
    scenario_ids = lax.all_gather(scen_ids, "scen", axis=0, tiled=True)
    blocks = 1
    overall_extent = dest.shape[0] // lax.axis_size("scen")
    first_row = lax.axis_index("scen") * overall_extent
    trade_rows = [
        lax.dynamic_slice_in_dim(column_data, first_row, overall_extent, 0)
        for column_data in (
            dest[:, 0],
            pick,
            expiry_cell,
            strike_cell,
            frac_e,
            frac_k,
            notional,
            forward,
        )
    ]
    (
        target,
        pick_rows,
        expiry_rows,
        strike_rows,
        frac_e_rows,
        frac_k_rows,
        notional_rows,
        forward_rows,
    ) = trade_rows
    held_surface = held_surfaces(log_vol, beta, shock_table, scenario_ids, hot_index)
    stress_case_number = scenario_ids.shape[0]
    sub_length = overall_extent // blocks
    capacity = 2 * sub_length // partner_number
    slot_width = blocks * capacity
    member = (target[:, None] == jnp.arange(partner_number, dtype=jnp.int32)[None, :]).astype(
        jnp.int32
    )
    running = (
        jnp.cumsum(member.reshape(blocks, sub_length, partner_number), axis=1).reshape(
            overall_extent, partner_number
        )
        - member
    )
    rank_index = jnp.sum(running * member, axis=1)
    slot_index = jnp.arange(overall_extent, dtype=jnp.int32) // sub_length * capacity + rank_index
    flat_slot = target * slot_width + slot_index
    packed = ((pick_rows * NE + expiry_rows) * NK + strike_rows).astype(jnp.float32)
    fields = jnp.stack([packed, frac_e_rows, frac_k_rows, notional_rows, forward_rows])
    buffer = (
        jnp.zeros((fields.shape[0], partner_number * slot_width), jnp.float32)
        .at[:, flat_slot]
        .set(fields)
    )
    buffer = buffer.reshape(fields.shape[0], partner_number, slot_width)
    answers = evaluate_items(
        held_surface,
        stress_case_number,
        lax.all_to_all(buffer, "trade", split_axis=1, concat_axis=1, tiled=True),
    )
    returned = lax.all_to_all(answers, "trade", split_axis=1, concat_axis=1, tiled=True)
    premium_entries = returned.reshape(returned.shape[0], partner_number * slot_width)[:, flat_slot]
    valued_entries = premium_entries.reshape(3, stress_case_number, overall_extent)
    valued_entries = lax.all_to_all(valued_entries, "scen", split_axis=1, concat_axis=2, tiled=True)
    return (valued_entries[0], valued_entries[1], valued_entries[2])


def solution(mesh):
    in_specs = (
        P("trade", None),
        P("trade"),
        P(),
        P("scen"),
        P("trade"),
        P("trade", None),
        P("trade"),
        P("trade"),
        P("trade"),
        P("trade"),
        P("trade"),
        P("trade"),
        P("trade"),
    )
    out_specs = (P("scen", "trade"), P("scen", "trade"), P("scen", "trade"))
    return jax.shard_map(shards, mesh=mesh, in_specs=in_specs, out_specs=out_specs, check_vma=False)
```

profile of v0, /device:TPU:0, one launch (start us, length us, event | category | flops | bytes accessed | tf_op | source)
XLA Modules:
  0.0 120.4 jit_solution(17656094455642899059)
XLA Ops:
  0.7 0.8 compare_select_fusion.1
  1.5 1.2 %dynamic-slice.1 = u32[1]{0:T(128)} dynamic-slice(u32[32]{0:T(128)} %constant.693, u32[]{:T(128)S(6)} %add.562), dynamic_slice_sizes={1} | dynamic-slice | bytes 12
  3.4 0.9 dynamic-update-slice
  4.9 6.4 %all-reduce = s32[8]{0:T(128)S(1)} all-reduce(s32[8]{0:T(128)S(1)} %dynamic-update-slice), channel_id=1, replica_groups=mesh['trade'=8,'scen'=4] {'scen'}, use_global_device_ids=true, to_apply=%add | all-reduce | flops 8 | bytes 64
  12.5 0.7 select_bitcast_fusion
  13.2 1.5 %collective-permute-start = (bf16[8,2,2048]{2,0,1:T(8,128)(2,1)}, bf16[8,2,2048]{2,0,1:T(8,128)(2,1)S(1)}, u32[]{:S(2)}, u32[]{:S(2)}) collective-permute-start(bf16[8,2,2048]{2,0,1:T(8,128)(2,1)} %select_bitcast_fusion), channel_id=1, source_target_pairs={{0,4},{4,8},{8,12},{12,16},{16,20},{20,24},{24,28},{28,0},{1,5},{5... | collective-permute-start | bytes 196616 | tf_op jit(solution)/shard_map/ppermute | solution.py:23
  14.8 3.2 %collective-permute-start.1 = (bf16[8,2,2048]{2,0,1:T(8,128)(2,1)}, bf16[8,2,2048]{2,0,1:T(8,128)(2,1)}, u32[]{:S(2)}, u32[]{:S(2)}) collective-permute-start(bf16[8,2,2048]{2,0,1:T(8,128)(2,1)} %select_bitcast_fusion), channel_id=1, source_target_pairs={{4,0},{8,4},{12,8},{16,12},{20,16},{24,20},{28,24},{0,28},{5,1},{9... | collective-permute-start | bytes 196616 | tf_op jit(solution)/shard_map/ppermute | solution.py:25
  18.0 2.3 %reduce-window.6 = s32[1,8,16,128]{3,2,1,0:T(8,128)S(1)} reduce-window(s32[1,8,16,128]{3,2,1,0:T(8,128)S(1)} %copy.54, s32[]{:T(128)} %constant.674.clone.1), window={size=1x1x1x128 pad=0_0x0_0x0_0x127_0}, to_apply=%region_0.1 | reduce-window | flops 2080768 | bytes 131076 | tf_op jit(solution)/shard_map/reduce-window
  20.6 0.7 dynamic_slice.42
  23.8 0.7 add_convert_fusion.1
  24.6 1.4 %copy.37 = f32[2048,5]{1,0:T(8,128)} copy(f32[2048,5]{0,1:T(8,128)S(1)} %bitcast.156) | data formatting | bytes 81920 | tf_op jit(solution)/shard_map/stack | solution.py:183
  26.0 7.4 %scatter_custom_fusion = f32[5,4096]{0,1:T(8,128)} fusion(s32[2048]{0:T(1024)S(1)} %bitcast.179, f32[2048,5]{1,0:T(8,128)} %copy.37, f32[]{:T(128)} %constant.675.clone.1), kind=kCustom, calls=%fused_computation.101 | custom fusion | bytes 82432 | tf_op jit(solution)/shard_map/scatter | solution.py:187
  33.3 2.9 %copy.38 = f32[5,8,512]{2,0,1:T(8,128)} copy(f32[5,8,512]{0,2,1:T(8,128)} %bitcast.146) | data formatting | bytes 163840 | tf_op jit(solution)/shard_map/reshape | solution.py:189
  36.2 3.4 %all-to-all-start = ((f32[5,8,512]{2,0,1:T(8,128)}), f32[5,8,512]{2,0,1:T(8,128)S(1)}, u32[]{:S(2)}, u32[]{:S(2)}) async-start(f32[5,8,512]{2,0,1:T(8,128)} %copy.38), calls=%async_computation | async-start | bytes 262144 | tf_op jit(solution)/shard_map/all_to_all | solution.py:193
  39.6 1.0 pad_maximum_fusion
  41.3 4.8 %reshape.1212 = bf16[8,2304,32]{2,1,0:T(8,128)(2,1)} reshape(bf16[8,36,2048]{2,1,0:T(8,128)(2,1)S(1)} %copy.39) | data formatting | bytes 2359296 | tf_op jit(solution)/shard_map/reshape | solution.py:82
  46.1 4.7 %copy.40 = bf16[8,2304,32]{1,2,0:T(8,128)(2,1)} copy(bf16[8,2304,32]{2,1,0:T(8,128)(2,1)} %reshape.1212) | data formatting | bytes 2359296 | tf_op jit(solution)/shard_map/while | solution.py:116
  50.9 33.8 %while.18 = (s32[]{:T(128)}, f32[24,4096]{1,0:T(8,128)S(1)}, f32[5,4096]{1,0:T(8,128)S(1)}, bf16[8,2304,32]{1,2,0:T(8,128)(2,1)}, s32[]{:T(128)}, /*index=5*/s32...) while((s32[]{:T(128)}, f32[24,4096]{1,0:T(8,128)S(1)}, f32[5,4096]{1,0:T(8,128)S(1)}, ...), condition=%wide.region_6.7_spmd, body=%wide.region_4.6_spmd.sunk | while | flops 623915520 | bytes 1603835 | solution.py:116
  51.2 3.7 %multiply_reduce_fusion.2 = f32[8,512]{1,0:T(8,128)S(1)} fusion(f32[32,512]{1,0:T(8,128)S(1)} %select_add_fusion.2, bf16[2304,256]{0,1:T(8,128)(2,1)} %bitcast.150, f32[512]{0:T(512)S(1)} %bitcast.178, f32[512]{0:T(512)S(1)} %bitcast.177, f32[512]{0:T(512)S(1)} %bitcast.170, f32[512]{0:T(512)S(1)} %bitcast.176, ...), kind=kOutput, calls=%fused_computation.24.clone.1 | convolution fusion | flops 623112192 | bytes 1273856 | tf_op jit(solution)/shard_map/while
  55.5 3.7 %multiply_reduce_fusion.2 = f32[8,512]{1,0:T(8,128)S(1)} fusion(f32[32,512]{1,0:T(8,128)S(1)} %select_add_fusion.2, bf16[2304,256]{0,1:T(8,128)(2,1)} %bitcast.150, f32[512]{0:T(512)S(1)} %bitcast.178, f32[512]{0:T(512)S(1)} %bitcast.177, f32[512]{0:T(512)S(1)} %bitcast.170, f32[512]{0:T(512)S(1)} %bitcast.176, ...), kind=kOutput, calls=%fused_computation.24.clone.1 | convolution fusion | flops 623112192 | bytes 1273856 | tf_op jit(solution)/shard_map/while
  59.7 3.7 %multiply_reduce_fusion.2 = f32[8,512]{1,0:T(8,128)S(1)} fusion(f32[32,512]{1,0:T(8,128)S(1)} %select_add_fusion.2, bf16[2304,256]{0,1:T(8,128)(2,1)} %bitcast.150, f32[512]{0:T(512)S(1)} %bitcast.178, f32[512]{0:T(512)S(1)} %bitcast.177, f32[512]{0:T(512)S(1)} %bitcast.170, f32[512]{0:T(512)S(1)} %bitcast.176, ...), kind=kOutput, calls=%fused_computation.24.clone.1 | convolution fusion | flops 623112192 | bytes 1273856 | tf_op jit(solution)/shard_map/while
  63.9 3.7 %multiply_reduce_fusion.2 = f32[8,512]{1,0:T(8,128)S(1)} fusion(f32[32,512]{1,0:T(8,128)S(1)} %select_add_fusion.2, bf16[2304,256]{0,1:T(8,128)(2,1)} %bitcast.150, f32[512]{0:T(512)S(1)} %bitcast.178, f32[512]{0:T(512)S(1)} %bitcast.177, f32[512]{0:T(512)S(1)} %bitcast.170, f32[512]{0:T(512)S(1)} %bitcast.176, ...), kind=kOutput, calls=%fused_computation.24.clone.1 | convolution fusion | flops 623112192 | bytes 1273856 | tf_op jit(solution)/shard_map/while
  68.2 3.7 %multiply_reduce_fusion.2 = f32[8,512]{1,0:T(8,128)S(1)} fusion(f32[32,512]{1,0:T(8,128)S(1)} %select_add_fusion.2, bf16[2304,256]{0,1:T(8,128)(2,1)} %bitcast.150, f32[512]{0:T(512)S(1)} %bitcast.178, f32[512]{0:T(512)S(1)} %bitcast.177, f32[512]{0:T(512)S(1)} %bitcast.170, f32[512]{0:T(512)S(1)} %bitcast.176, ...), kind=kOutput, calls=%fused_computation.24.clone.1 | convolution fusion | flops 623112192 | bytes 1273856 | tf_op jit(solution)/shard_map/while
  72.4 3.7 %multiply_reduce_fusion.2 = f32[8,512]{1,0:T(8,128)S(1)} fusion(f32[32,512]{1,0:T(8,128)S(1)} %select_add_fusion.2, bf16[2304,256]{0,1:T(8,128)(2,1)} %bitcast.150, f32[512]{0:T(512)S(1)} %bitcast.178, f32[512]{0:T(512)S(1)} %bitcast.177, f32[512]{0:T(512)S(1)} %bitcast.170, f32[512]{0:T(512)S(1)} %bitcast.176, ...), kind=kOutput, calls=%fused_computation.24.clone.1 | convolution fusion | flops 623112192 | bytes 1273856 | tf_op jit(solution)/shard_map/while
  76.6 3.7 %multiply_reduce_fusion.2 = f32[8,512]{1,0:T(8,128)S(1)} fusion(f32[32,512]{1,0:T(8,128)S(1)} %select_add_fusion.2, bf16[2304,256]{0,1:T(8,128)(2,1)} %bitcast.150, f32[512]{0:T(512)S(1)} %bitcast.178, f32[512]{0:T(512)S(1)} %bitcast.177, f32[512]{0:T(512)S(1)} %bitcast.170, f32[512]{0:T(512)S(1)} %bitcast.176, ...), kind=kOutput, calls=%fused_computation.24.clone.1 | convolution fusion | flops 623112192 | bytes 1273856 | tf_op jit(solution)/shard_map/while
  80.8 3.7 %multiply_reduce_fusion.2 = f32[8,512]{1,0:T(8,128)S(1)} fusion(f32[32,512]{1,0:T(8,128)S(1)} %select_add_fusion.2, bf16[2304,256]{0,1:T(8,128)(2,1)} %bitcast.150, f32[512]{0:T(512)S(1)} %bitcast.178, f32[512]{0:T(512)S(1)} %bitcast.177, f32[512]{0:T(512)S(1)} %bitcast.170, f32[512]{0:T(512)S(1)} %bitcast.176, ...), kind=kOutput, calls=%fused_computation.24.clone.1 | convolution fusion | flops 623112192 | bytes 1273856 | tf_op jit(solution)/shard_map/while
  84.7 0.8 copy.52
  85.5 5.9 %all-to-all-start.1 = ((f32[24,8,512]{2,0,1:T(8,128)}), f32[24,8,512]{2,0,1:T(8,128)S(1)}, u32[]{:S(2)}, u32[]{:S(2)}) async-start(f32[24,8,512]{2,0,1:T(8,128)} %bitcast.97), calls=%async_computation.1 | async-start | bytes 786432 | tf_op jit(solution)/shard_map/all_to_all | solution.py:195
  91.4 10.3 %all-to-all-done.1 = f32[24,8,512]{2,0,1:T(8,128)S(1)} async-done(((f32[24,8,512]{2,0,1:T(8,128)}), f32[24,8,512]{2,0,1:T(8,128)S(1)}, u32[]{:S(2)}, u32[]{:S(2)}) %all-to-all-start.1) | async-done | bytes 393248 | tf_op jit(solution)/shard_map/all_to_all | solution.py:195
  101.7 2.0 %copy.42 = f32[24,8,512]{0,2,1:T(8,128)} copy(f32[24,8,512]{2,0,1:T(8,128)S(1)} %all-to-all-done.1) | data formatting | bytes 786432 | tf_op jit(solution)/shard_map/all_to_all | solution.py:195
  103.6 7.0 %gather_fusion.1 = f32[2048,24]{1,0:T(8,128)S(1)} fusion(f32[24,4096]{0,1:T(8,128)} %bitcast.147, s32[2048]{0:T(1024)S(1)} %broadcast_clamp_fusion), kind=kCustom, calls=%fused_computation.1 | custom fusion | bytes 401408 | tf_op jit(solution)/shard_map/gather | solution.py:196
  111.1 8.4 %all_to_all.25 = f32[3,8,2048]{2,0,1:T(4,128)S(1)} all-to-all(f32[3,8,2048]{2,0,1:T(4,128)S(1)} %copy.44), channel_id=1, replica_groups=mesh['trade'=8,'scen'=4] {'scen'}, dimensions={1} | all-to-all | bytes 393216 | tf_op jit(solution)/shard_map/all_to_all | solution.py:198
  (110 shorter events, 10.6 us)
Async XLA Ops:
  0.6 10.6 %copy-start = (bf16[512,2048]{1,0:T(8,128)(2,1)S(1)}, bf16[512,2048]{1,0:T(8,128)(2,1)}, u32[]{:S(2)}) copy-start(bf16[512,2048]{1,0:T(8,128)(2,1)} %param.17) | copy-start | bytes 6291460
  0.6 11.1 %copy-start.1 = (f32[32,2048]{1,0:T(8,128)S(1)}, f32[32,2048]{1,0:T(8,128)}, u32[]{:S(2)}) copy-start(f32[32,2048]{1,0:T(8,128)} %param.15) | copy-start | bytes 786436
  0.7 11.0 %copy-start.3 = (f32[32]{0:T(128)S(1)}, f32[32]{0:T(128)}, u32[]{:S(2)}) copy-start(f32[32]{0:T(128)} %param.16) | copy-start | bytes 388
  0.7 17.3 %copy-start.2 = (s32[8192,1]{0,1:T(1,128)S(1)}, s32[8192,1]{0,1:T(1,128)}, u32[]{:S(2)}) copy-start(s32[8192,1]{0,1:T(1,128)} %param.20) | copy-start | bytes 98308
  13.2 26.4 %collective-permute-start = (bf16[8,2,2048]{2,0,1:T(8,128)(2,1)}, bf16[8,2,2048]{2,0,1:T(8,128)(2,1)S(1)}, u32[]{:S(2)}, u32[]{:S(2)}) collective-permute-start(bf16[8,2,2048]{2,0,1:T(8,128)(2,1)} %select_bitcast_fusion), channel_id=1, source_target_pairs={{0,4},{4,8},{8,12},{12,16},{16,20},{20,24},{24,28},{28,0},{1,5},{5... | collective-permute-start | bytes 196616 | tf_op jit(solution)/shard_map/ppermute | solution.py:23
  14.8 24.8 %collective-permute-start.1 = (bf16[8,2,2048]{2,0,1:T(8,128)(2,1)}, bf16[8,2,2048]{2,0,1:T(8,128)(2,1)}, u32[]{:S(2)}, u32[]{:S(2)}) collective-permute-start(bf16[8,2,2048]{2,0,1:T(8,128)(2,1)} %select_bitcast_fusion), channel_id=1, source_target_pairs={{4,0},{8,4},{12,8},{16,12},{20,16},{24,20},{28,24},{0,28},{5,1},{9... | collective-permute-start | bytes 196616 | tf_op jit(solution)/shard_map/ppermute | solution.py:25
  36.2 14.6 %all-to-all-start = ((f32[5,8,512]{2,0,1:T(8,128)}), f32[5,8,512]{2,0,1:T(8,128)S(1)}, u32[]{:S(2)}, u32[]{:S(2)}) async-start(f32[5,8,512]{2,0,1:T(8,128)} %copy.38), calls=%async_computation | async-start | bytes 262144 | tf_op jit(solution)/shard_map/all_to_all | solution.py:193
  85.5 16.2 %all-to-all-start.1 = ((f32[24,8,512]{2,0,1:T(8,128)}), f32[24,8,512]{2,0,1:T(8,128)S(1)}, u32[]{:S(2)}, u32[]{:S(2)}) async-start(f32[24,8,512]{2,0,1:T(8,128)} %bitcast.97), calls=%async_computation.1 | async-start | bytes 786432 | tf_op jit(solution)/shard_map/all_to_all | solution.py:195
where the time goes:
time: 122 us; the launch traced here: 120 us
  local copies, waits for them, and re-layouts  38.8 us (32%)
  matrix products  29.8 us (24%)
  blocking collectives  14.8 us (12%)
  starting transfers between devices  14 us (11%)
  other arithmetic  10.6 us (9%)
  waiting for transfers between devices  10.3 us (8%)
  between operations  1.47 us (1%)
    while x8, matrix products  29.4 us
    all_to_all x1, waiting for transfers between devices, shards(): lax.all_to_all(answers, 'trade', split_axis=1, concat_axis=1, tiled=True)  10.3 us
    all_to_all x1, blocking collectives, shards(): lax.all_to_all(valued_entries, 'scen', split_axis=1, concat_axis=2, tiled...  8.42 us
    scatter x1, local copies, waits for them, and re-layouts, shards(): buffer = jnp.zeros((fields.shape[0], partner_number * slot_width), jnp.fl...  7.39 us
    gather x2, local copies, waits for them, and re-layouts, shards(): returned.reshape(returned.shape[0], partner_number * slot_width)  7.35 us
    unnamed x1, blocking collectives  6.35 us
    all_to_all x1, starting transfers between devices, shards(): lax.all_to_all(answers, 'trade', split_axis=1, concat_axis=1, tiled=True)  5.92 us
    reshape x1, local copies, waits for them, and re-layouts, held_surfaces(): return held_rows.reshape(stress_case_number, held_count * NE, NK)  4.83 us
  transfers between devices with their start and end apart: 4, of which 1 were waited for; matrix products, arithmetic and copies ran while one was open for 24% of the time, Pallas kernels for 0%

commit v1 on v0

v1 whole, which is shorter than its diff:
```python
import functools

import jax
import jax.numpy as jnp
from jax import lax
from jax.experimental import pallas as pl
from jax.experimental.pallas import tpu as pltpu
from jax.sharding import PartitionSpec as P

NE = 64
NK = 32
HOT = 2
LANES = 128
BAND = LANES // NK
BLOCKS = NE // BAND
EXTRA = 16
CENTRE = 1.4

RATE = 0.03
INV_ROOT_TWO = 0.7071067811865476
INV_ROOT_TAU = 0.3989422804014327

VMEM = pl.BlockSpec(memory_space=pltpu.VMEM)
SMEM = pl.BlockSpec(memory_space=pltpu.SMEM)
F32 = jnp.float32
BF16 = jnp.bfloat16

(WE, WK, ROW, COL, BLK, SLOT, PICK) = (0, 4, 8, 9, 10, 11, 12)
PREPARED = 13


def spline_weights(offset):
    square = offset * offset
    offset_cube = square * offset
    return (
        0.5 * (2.0 * square - offset_cube - offset),
        0.5 * (3.0 * offset_cube - 5.0 * square + 2.0),
        0.5 * (4.0 * square - 3.0 * offset_cube + offset),
        0.5 * (offset_cube - square),
    )


def params(megabytes=None):
    limit = None if megabytes is None else megabytes << 20
    return pltpu.CompilerParams(vmem_limit_bytes=limit)


def pack_kernel(hot_ref, log_vol_ref, beta_ref, out_ref):
    owned = log_vol_ref.shape[0]
    per_tile = LANES // owned
    for tile in range(BLOCKS // per_tile):
        stacked = jnp.concatenate(
            [
                log_vol_ref[:, (tile * per_tile + i) * LANES : (tile * per_tile + i + 1) * LANES]
                for i in range(per_tile)
            ],
            axis=0,
        )
        out_ref[0:LANES, tile * LANES : (tile + 1) * LANES] = (
            jnp.transpose(stacked) + CENTRE
        ).astype(BF16)
    row = lax.broadcasted_iota(jnp.int32, (EXTRA, LANES), 0)
    beta = jnp.broadcast_to(beta_ref[...], (EXTRA, LANES))
    high = beta.astype(BF16).astype(F32)
    middle = (beta - high).astype(BF16).astype(F32)
    low = beta - high - middle
    zero = jnp.zeros((EXTRA, LANES), F32)
    pieces = jnp.where(row == 0, high, jnp.where(row == 1, middle, jnp.where(row == 2, low, zero)))
    hots = zero
    for i in range(HOT):
        hots = jnp.where(row == i, hot_ref[i].astype(F32), hots)
    out_ref[LANES : LANES + EXTRA, 0:LANES] = pieces.astype(BF16)
    out_ref[LANES : LANES + EXTRA, LANES : 2 * LANES] = hots.astype(BF16)
    for tile in range(2, BLOCKS // per_tile):
        out_ref[LANES : LANES + EXTRA, tile * LANES : (tile + 1) * LANES] = zero.astype(BF16)


def placed(position, weights, first, shape):
    distance = position - jnp.broadcast_to(first, shape)
    result = jnp.zeros(shape, F32)
    for tap in range(4):
        result = jnp.where(distance == float(tap), jnp.broadcast_to(weights[tap], shape), result)
    return result


def prepare_kernel(
    device_count,
    per_step,
    place_ref,
    shift_ref,
    dest_ref,
    pick_ref,
    expiry_ref,
    strike_ref,
    frac_e_ref,
    frac_k_ref,
    out_ref,
    high_ref,
):
    groups = dest_ref.shape[0]
    owned = place_ref[2]
    n_scen = place_ref[3]
    weights = spline_weights(frac_e_ref[...])
    for tap in range(4):
        out_ref[WE + tap] = weights[tap].astype(BF16).astype(F32)
    weights = spline_weights(frac_k_ref[...])
    for tap in range(4):
        out_ref[WK + tap] = weights[tap]
    first_row = expiry_ref[...] - 1
    block = lax.shift_right_logical(first_row, BAND.bit_length() - 1)
    out_ref[ROW] = (first_row - block * BAND).astype(F32)
    out_ref[BLK] = block.astype(F32)
    out_ref[COL] = (strike_ref[...] - 1).astype(F32)
    dest = dest_ref[...]
    pick = pick_ref[...]
    hot = pick - owned
    step = jnp.where(hot < 0, 0, jnp.where(hot < HOT, device_count - 1, 1))
    owner = (dest + step) & (device_count - 1)
    offset = owner ^ place_ref[0]
    mine = (offset & (n_scen - 1)) == place_ref[1]
    slot = lax.shift_right_logical(offset, place_ref[4])
    out_ref[SLOT] = jnp.where(mine, slot, -1).astype(F32)
    out_ref[PICK] = jnp.where(hot < HOT, pick, pick - HOT).astype(F32)

    shift = shift_ref[...]
    scenarios = high_ref.shape[0]
    expiries = lax.broadcasted_iota(jnp.int32, (NE, LANES), 0).astype(F32)
    strikes = lax.broadcasted_iota(jnp.int32, (NK, LANES), 0).astype(F32)

    def some(i, carry):
        sides = []
        for part in range(per_step):
            g = i * per_step + part
            first = out_ref[BLK, pl.ds(g, 1), :] * float(BAND) + out_ref[ROW, pl.ds(g, 1), :]
            taps = [out_ref[WE + tap, pl.ds(g, 1), :] for tap in range(4)]
            sides.append(placed(expiries, taps, first, (NE, LANES)).astype(BF16))
        mixed = jnp.dot(shift, jnp.concatenate(sides, axis=1), preferred_element_type=F32)
        for part in range(per_step):
            g = i * per_step + part
            taps = [out_ref[WK + tap, pl.ds(g, 1), :] for tap in range(4)]
            coefs = placed(strikes, taps, out_ref[COL, pl.ds(g, 1), :], (NK, LANES))
            for s in range(scenarios):
                piece = mixed[s * NK : (s + 1) * NK, part * LANES : (part + 1) * LANES]
                high_ref[s, pl.ds(g, 1), :] = jnp.sum(piece * coefs, axis=0, keepdims=True)
        return carry

    lax.fori_loop(0, groups // per_step, some, 0)


def surface_kernel(slots, owned, per_step, *refs):
    messages = refs[:slots]
    pre_ref, out_ref, table_ref, index_ref = refs[slots:]
    groups = pre_ref.shape[1]
    depth = BLOCKS * owned
    for k in range(slots):
        here = messages[k][0:LANES, :]
        table_ref[k, 0:LANES, :] = here
        table_ref[k, LANES : 2 * LANES, :] = pltpu.roll(
            here.astype(F32), depth - owned, 1
        ).astype(BF16)
    sub = 8
    extras = [messages[k][LANES : LANES + EXTRA, 0 : 2 * LANES].astype(F32) for k in range(slots)]

    for i in range(groups // sub):
        rows = pl.ds(i * sub, sub)
        slot = pre_ref[SLOT, rows, :]
        pick = pre_ref[PICK, rows, :]
        index = jnp.full((sub, LANES), -1.0, F32)
        beta = jnp.zeros((sub, LANES), F32)
        for k in range(slots):
            local = pick
            for h in range(HOT):
                hot = jnp.broadcast_to(extras[k][h : h + 1, LANES : 2 * LANES], (sub, LANES))
                local = jnp.where(pick == float(owned + h), hot, local)
            row = extras[k][0:1, 0:LANES] + extras[k][1:2, 0:LANES] + extras[k][2:3, 0:LANES]
            looked = jnp.take_along_axis(
                jnp.broadcast_to(row, (sub, LANES)),
                local.astype(jnp.int32),
                axis=1,
                mode="promise_in_bounds",
            )
            index = jnp.where(slot == float(k), local + float(k * owned), index)
            beta = jnp.where(slot == float(k), looked, beta)
        index_ref[rows, :] = index
        out_ref[pl.ds(groups + i * sub, sub), :] = beta

    height = slots * owned
    underlyings = lax.broadcasted_iota(jnp.int32, (height, LANES), 0).astype(F32)
    strikes = lax.broadcasted_iota(jnp.int32, (NK, LANES), 0).astype(F32)
    expiries = lax.broadcasted_iota(jnp.int32, (2 * BAND, LANES), 0).astype(F32)

    def some(i, carry):
        chosen, block = [], []
        for part in range(per_step):
            g = i * per_step + part
            index = jnp.broadcast_to(index_ref[pl.ds(g, 1), :], (height, LANES))
            chosen.append(jnp.where(underlyings == index, 1.0, 0.0).astype(BF16))
            block.append(
                jnp.broadcast_to(pre_ref[BLK, pl.ds(g, 1), :], (owned, LANES)).astype(BF16)
            )
        total = None
        zero = jnp.zeros((owned, LANES), BF16)
        for k in range(slots):
            side = jnp.concatenate(
                [
                    jnp.concatenate(
                        [
                            jnp.where(
                                block[part] == jnp.asarray(j, BF16),
                                chosen[part][k * owned : (k + 1) * owned],
                                zero,
                            )
                            for j in range(BLOCKS)
                        ],
                        axis=0,
                    )
                    for part in range(per_step)
                ],
                axis=1,
            )
            product = jnp.dot(table_ref[k], side, preferred_element_type=F32)
            total = product if total is None else total + product
        for part in range(per_step):
            g = i * per_step + part
            columns = slice(part * LANES, (part + 1) * LANES)
            taps = [pre_ref[WE + tap, pl.ds(g, 1), :] for tap in range(4)]
            mix = placed(expiries, taps, pre_ref[ROW, pl.ds(g, 1), :], (2 * BAND, LANES))
            curve = jnp.zeros((NK, LANES), F32)
            for a in range(2 * BAND):
                curve = curve + total[a * NK : (a + 1) * NK, columns] * mix[a : a + 1, :]
            taps = [pre_ref[WK + tap, pl.ds(g, 1), :] for tap in range(4)]
            coefs = placed(strikes, taps, pre_ref[COL, pl.ds(g, 1), :], (NK, LANES))
            level = jnp.sum(curve * coefs, axis=0, keepdims=True)
            weight = (taps[0] + taps[1] + taps[2] + taps[3]) * jnp.sum(mix, axis=0, keepdims=True)
            held = index_ref[pl.ds(g, 1), :] >= 0.0
            out_ref[pl.ds(g, 1), :] = jnp.where(held, level - CENTRE * weight, 0.0)
        return carry

    lax.fori_loop(0, groups // per_step, some, 0)


def black_model(log_sigma, expiry_cell, frac_e, strike_cell, frac_k, notional, forward):
    maturity = (expiry_cell + frac_e + 1.0) * (4.0 / NE)
    moneyness = (strike_cell + frac_k - 0.5 * (NK - 1)) / NK
    root_time = jnp.sqrt(maturity)
    spread = jnp.exp(log_sigma) * root_time
    upper_d = -moneyness / spread + 0.5 * spread
    minus_term_black = upper_d - spread
    discount_factor = jnp.exp(-RATE * maturity)
    cdf_upper = 0.5 * lax.erfc(-upper_d * INV_ROOT_TWO)
    cdf_lower = 0.5 * lax.erfc(-minus_term_black * INV_ROOT_TWO)
    scaled = notional * discount_factor
    price_out = scaled * forward * (cdf_upper - jnp.exp(moneyness) * cdf_lower)
    vega_out = scaled * forward * INV_ROOT_TAU * jnp.exp(-0.5 * upper_d * upper_d) * root_time
    delta_out = scaled * cdf_upper
    return (price_out, vega_out, delta_out)


def shards(
    log_vol,
    beta,
    shock_table,
    scen_ids,
    hot_index,
    dest,
    pick,
    expiry_cell,
    strike_cell,
    frac_e,
    frac_k,
    notional,
    forward,
):
    n_trade = lax.axis_size("trade")
    n_scen = lax.axis_size("scen")
    slots = n_trade // n_scen
    owned = log_vol.shape[0]
    trades = pick.shape[0]
    groups = trades // LANES
    scenarios = scen_ids.shape[0]

    beta_row = jnp.pad(beta[None, :], ((0, 0), (0, LANES - owned)))
    message = pl.pallas_call(
        pack_kernel,
        out_shape=jax.ShapeDtypeStruct((LANES + EXTRA, BLOCKS * owned), BF16),
        in_specs=[SMEM, VMEM, VMEM],
        out_specs=VMEM,
        compiler_params=params(),
    )(hot_index, log_vol, beta_row)

    received = [None] * slots
    for k in reversed(range(slots)):
        pairs = [
            ((d ^ (q + k * n_scen)) * n_scen + q, d * n_scen + q)
            for d in range(n_trade)
            for q in range(n_scen)
        ]
        received[k] = lax.ppermute(message, ("trade", "scen"), pairs)

    shift = jnp.concatenate(
        [
            lax.dynamic_slice(shock_table, (scen_ids[s], 0), (1, NE * NK))
            for s in range(scenarios)
        ],
        axis=0,
    )
    shift = shift.reshape(scenarios, NE, NK).transpose(0, 2, 1).reshape(scenarios * NK, NE)
    dense = [
        column.reshape(groups, LANES)
        for column in (dest, pick, expiry_cell, strike_cell, frac_e, frac_k)
    ]
    place = jnp.stack(
        [
            lax.axis_index("trade"),
            lax.axis_index("scen"),
            jnp.int32(owned),
            jnp.int32(n_scen),
            jnp.int32(n_scen.bit_length() - 1),
        ]
    )
    prepared, shift_level = pl.pallas_call(
        functools.partial(prepare_kernel, n_trade, 4),
        out_shape=(
            jax.ShapeDtypeStruct((PREPARED, groups, LANES), F32),
            jax.ShapeDtypeStruct((scenarios, groups, LANES), F32),
        ),
        in_specs=[SMEM] + [VMEM] * 7,
        out_specs=(VMEM, VMEM),
        cost_estimate=pl.CostEstimate(flops=40_000_000, bytes_accessed=6_000_000, transcendentals=0),
        compiler_params=params(),
    )(place, shift, *dense)

    partial_levels = pl.pallas_call(
        functools.partial(surface_kernel, slots, owned, 4),
        out_shape=jax.ShapeDtypeStruct((2 * groups, LANES), F32),
        in_specs=[VMEM] * (slots + 1),
        out_specs=VMEM,
        scratch_shapes=[
            pltpu.VMEM((slots, 2 * LANES, BLOCKS * owned), BF16),
            pltpu.VMEM((groups, LANES), F32),
        ],
        compiler_params=params(48),
    )(*received, prepared)

    total = partial_levels
    hop = n_scen // 2
    while hop:
        total = total + lax.ppermute(total, "scen", [(i, i ^ hop) for i in range(n_scen)])
        hop //= 2
    level = total[:groups].reshape(trades)
    slope = total[groups:].reshape(trades)
    log_sigma = level[None, :] + slope[None, :] * shift_level.reshape(scenarios, trades)
    return black_model(
        log_sigma,
        expiry_cell.astype(F32),
        frac_e,
        strike_cell.astype(F32),
        frac_k,
        notional,
        forward,
    )


def solution(mesh):
    in_specs = (
        P("trade", None),
        P("trade"),
        P(),
        P("scen"),
        P("trade"),
        P("trade", None),
        P("trade"),
        P("trade"),
        P("trade"),
        P("trade"),
        P("trade"),
        P("trade"),
        P("trade"),
    )
    out_specs = (P("scen", "trade"), P("scen", "trade"), P("scen", "trade"))
    return jax.shard_map(shards, mesh=mesh, in_specs=in_specs, out_specs=out_specs, check_vma=False)
```

time: 122 us -> 41.1 us (0.34)
  local copies, waits for them, and re-layouts: 38.8 us -> 5.8 us
  matrix products: 29.8 us -> 0 us
  blocking collectives: 14.8 us -> 0 us
  Pallas kernels: 0 us -> 14 us
  waiting for transfers between devices: 10.3 us -> 2.79 us
  other arithmetic: 10.6 us -> 4.38 us
  starting transfers between devices: 14 us -> 9.04 us
  between operations: 1.47 us -> 4.58 us
    while x8 -> x0, matrix products: 29.4 us -> none
    pallas_call x0 -> x3, Pallas kernels: none -> 14 us  [the longest x1 7.53 us: shards(): pl.pallas_call(functools.partial(surface_kernel, slots, owned, 4), out_sh...]
    all_to_all x2 -> x0, waiting for transfers between devices: 10.3 us -> none  [the longest x1 10.3 us: shards(): lax.all_to_all(answers, 'trade', split_axis=1, concat_axis=1, tiled=True)]
    all_to_all x2 -> x0, starting transfers between devices: 9.29 us -> none  [the longest x1 5.92 us: shards(): lax.all_to_all(answers, 'trade', split_axis=1, concat_axis=1, tiled=True)]
    reshape x4 -> x1, local copies, waits for them, and re-layouts: 8.6 us -> 0.09 us  [shards(): shift.reshape(scenarios, NE, NK).transpose(0, 2, 1)]
    all_to_all x1 -> x0, blocking collectives: 8.42 us -> none  [shards(): lax.all_to_all(valued_entries, 'scen', split_axis=1, concat_axis=2, tiled...]
    gather x3 -> x0, local copies, waits for them, and re-layouts: 7.9 us -> none  [the longest x2 7.35 us: shards(): returned.reshape(returned.shape[0], partner_number * slot_width)]
    scatter x1 -> x0, local copies, waits for them, and re-layouts: 7.39 us -> none  [shards(): buffer = jnp.zeros((fields.shape[0], partner_number * slot_width), jnp.fl...]
  transfers between devices with their start and end apart: 4 -> 4, of which waited for: 1 -> 2; matrix products, arithmetic and copies ran while one was open for 24% -> 11% of each run, Pallas kernels for 0% -> 12%
where the time goes in v1:
time: 41.1 us; the launch traced here: 40.6 us
  Pallas kernels  14 us (34%)
  starting transfers between devices  9.04 us (22%)
  local copies, waits for them, and re-layouts  5.8 us (14%)
  between operations  4.58 us (11%)
  other arithmetic  4.38 us (11%)
  waiting for transfers between devices  2.79 us (7%)
    pallas_call x1, Pallas kernels, shards(): pl.pallas_call(functools.partial(surface_kernel, slots, owned, 4), out_sh...  7.53 us
    ppermute x2, starting transfers between devices, shards(): received[k] = lax.ppermute(message, ('trade', 'scen'), pairs)  5.59 us
    pallas_call x1, Pallas kernels, shards(): pl.pallas_call(functools.partial(prepare_kernel, n_trade, 4), out_shape=(...  4.71 us
    ppermute x2, starting transfers between devices, shards(): lax.ppermute(total, 'scen', [(i, i ^ hop) for i in range(n_scen)])  3.44 us
    ppermute x2, waiting for transfers between devices, shards(): lax.ppermute(total, 'scen', [(i, i ^ hop) for i in range(n_scen)])  2.79 us
    mul x1, other arithmetic, black_model(): delta_out = scaled * cdf_upper  2.12 us
    pallas_call x1, Pallas kernels, shards(): pl.pallas_call(pack_kernel, out_shape=jax.ShapeDtypeStruct((LANES + EXTRA...  1.74 us
    mul x1, other arithmetic, black_model(): scaled * forward * INV_ROOT_TAU * jnp.exp(-0.5 * upper_d * upper_d)  1.33 us
  transfers between devices with their start and end apart: 4, of which 2 were waited for; matrix products, arithmetic and copies ran while one was open for 11% of the time, Pallas kernels for 12%

profile of v1, /device:TPU:0, one launch (start us, length us, event | category | flops | bytes accessed | tf_op | source)
XLA Modules:
  0.0 40.6 jit_solution(11640731981740869687)
XLA Ops:
  0.6 1.2 %pad.4.beta_ref = f32[1,128]{1,0:T(1,128)} pad(f32[1,32]{1,0:T(1,128)} %bitcast.41, f32[]{:T(128)} %constant.10.clone.1), padding=0_0x0_96 | pad | bytes 644 | tf_op jit(solution)/shard_map/jit(_pad)/pad | solution.py:282
  1.8 1.7 %shard_map.148 = bf16[144,512]{1,0:T(8,128)(2,1)} custom-call(s32[2]{0:T(128)} %hot_ref.1, f32[32,2048]{1,0:T(8,128)} %log_vol_ref.1, f32[1,128]{1,0:T(1,128)} %pad.4.beta_ref), custom_call_target="tpu_custom_call" | custom-call | tf_op jit(solution)/shard_map/pallas_call | solution.py:283
  3.5 1.6 %collective-permute-start = (bf16[144,512]{1,0:T(8,128)(2,1)}, bf16[144,512]{1,0:T(8,128)(2,1)S(1)}, u32[]{:S(2)}, u32[]{:S(2)}) collective-permute-start(bf16[144,512]{1,0:T(8,128)(2,1)} %shard_map.148), channel_id=1, source_target_pairs={{0,0},{5,1},{10,2},{15,3},{4,4},{1,5},{14,6},{11,7},{8,8},{13,9},{... | collective-permute-start | bytes 442376 | tf_op jit(solution)/shard_map/ppermute | solution.py:298
  5.1 4.0 %collective-permute-start.1 = (bf16[144,512]{1,0:T(8,128)(2,1)}, bf16[144,512]{1,0:T(8,128)(2,1)S(1)}, u32[]{:S(2)}, u32[]{:S(2)}) collective-permute-start(bf16[144,512]{1,0:T(8,128)(2,1)} %shard_map.148), channel_id=1, source_target_pairs={{16,0},{21,1},{26,2},{31,3},{20,4},{17,5},{30,6},{27,7},{24,8},{29... | collective-permute-start | bytes 442376 | tf_op jit(solution)/shard_map/ppermute | solution.py:298
  9.1 1.3 %fusion.18 = (s32[1]{0:T(128)}, s32[1]{0:T(128)}) fusion(s32[2]{0:T(128)} %param.16), kind=kLoop, calls=%fused_computation.47 | loop fusion | bytes 16 | tf_op jit(solution)/shard_map/slice | solution.py:302
  14.3 0.9 %constant_dynamic-slice_fusion.1 = (bf16[1,2048]{1,0:T(2,128)(2,1)S(1)}, bf16[1,2048]{1,0:T(2,128)(2,1)S(1)}) fusion(bf16[512,2048]{1,0:T(8,128)(2,1)} %param.15, s32[]{:T(128)S(6)} %select_n.6, s32[]{:T(128)S(6)} %select_n.7), kind=kLoop, calls=%fused_computation.45 | loop fusion | bytes 16392 | tf_op jit(solution)/shard_map/dynamic_slice | solution.py:302
  15.2 0.1 reshape.41
  15.3 0.7 %copy.17 = bf16[2,32,64]{2,1,0:T(8,128)(2,1)} copy(bf16[2,32,64]{1,2,0:T(8,128)(2,1)S(1)} %bitcast.33) | data formatting | bytes 16384 | tf_op jit(solution)/shard_map/transpose | solution.py:307
  16.0 0.7 %stack.11.place_ref = s32[5]{0:T(128)} concatenate(s32[1]{0:T(128)} %bitcast.1, s32[1]{0:T(128)} %bitcast.2, s32[1]{0:T(128)} %constant.14.clone.1, s32[1]{0:T(128)} %constant.15.clone.1, s32[1]{0:T(128)} %constant.16.clone.1), dimensions={0} | concatenate | bytes 40 | tf_op jit(solution)/shard_map/stack | solution.py:312
  16.7 4.7 %shard_map.149 = (f32[13,64,128]{2,1,0:T(8,128)}, f32[2,64,128]{2,1,0:T(8,128)}) custom-call(s32[5]{0:T(128)} %stack.11.place_ref, bf16[64,64]{1,0:T(8,128)(2,1)} %bitcast.38, s32[64,128]{1,0:T(8,128)} %bitcast.39, s32[64,128]{1,0:T(8,128)} %bitcast.40, s32[64,128]{1,0:T(8,128)} %bitcast.37, s32[64,128]{1,0:T(8,128)} %bitcast.35, f32[64,128]{1,0:T(8,128)} %bitcast.36, ...), custom_call_target="tpu_custom_call" | custom-call | flops 40000000 | bytes 6000000 | tf_op jit(solution)/shard_map/pallas_call | solution.py:321
  21.4 0.0 collective-permute-done.refs_0_
  21.4 0.0 collective-permute-done.1.refs_1_
  21.4 0.0 copy-start
  21.4 1.0 %copy-done = f32[13,64,128]{2,1,0:T(8,128)S(1)} copy-done((f32[13,64,128]{2,1,0:T(8,128)S(1)}, f32[13,64,128]{2,1,0:T(8,128)}, u32[]{:S(2)}) %copy-start) | copy-done | bytes 426008
  22.4 0.0 copy-start.1
  22.4 7.5 %shard_map.150 = f32[128,128]{1,0:T(8,128)S(1)} custom-call(bf16[144,512]{1,0:T(8,128)(2,1)S(1)} %collective-permute-done.refs_0_, bf16[144,512]{1,0:T(8,128)(2,1)S(1)} %collective-permute-done.1.refs_1_, f32[13,64,128]{2,1,0:T(8,128)S(1)} %copy-done), custom_call_target="tpu_custom_call" | custom-call | tf_op jit(solution)/shard_map/pallas_call | solution.py:333
  30.0 3.4 %collective-permute-start.2 = (f32[128,128]{1,0:T(8,128)S(1)}, f32[128,128]{1,0:T(8,128)S(1)}, u32[]{:S(2)}, u32[]{:S(2)}) collective-permute-start(f32[128,128]{1,0:T(8,128)S(1)} %shard_map.150), channel_id=1, source_target_pairs={{0,2},{1,3},{2,0},{3,1},{4,6},{5,7},{6,4},{7,5},{8,10},{9,11},{10,... | collective-permute-start | bytes 196616 | tf_op jit(solution)/shard_map/ppermute | solution.py:348
  33.3 2.4 %collective-permute-done.2 = f32[128,128]{1,0:T(8,128)S(1)} collective-permute-done((f32[128,128]{1,0:T(8,128)S(1)}, f32[128,128]{1,0:T(8,128)S(1)}, u32[]{:S(2)}, u32[]{:S(2)}) %collective-permute-start.2) | collective-permute-done | bytes 65568 | tf_op jit(solution)/shard_map/ppermute | solution.py:348
  35.8 0.1 collective-permute-start.3
  35.8 0.9 %exponential_multiply_fusion = (f32[8192]{0:T(1024)S(1)}, f32[8192]{0:T(1024)S(1)}, f32[8192]{0:T(1024)S(1)}, f32[8192]{0:T(1024)S(1)}, f32[8192]{0:T(1024)S(1)}, /*index=5*/f32[8192]{0:T(1024)S(1)}) fusion(f32[8192]{0:T(1024)} %param.23, s32[8192]{0:T(1024)} %param.21, f32[8192]{0:T(1024)} %param.22, s32[8192]{0:T(1024)} %param.20, f32[8192]{0:T(1024)} %param.24, ...), kind=kLoop, calls=%fused_computation.35 | loop fusion | flops 122880 | bytes 393216 | tf_op jit(solution)/shard_map/mul | solution.py:253
  36.7 0.4 collective-permute-done.3
  37.1 2.1 %broadcast_multiply_fusion = (f32[2,8192]{1,0:T(2,128)}, f32[2,8192]{1,0:T(2,128)S(1)}, f32[2,8192]{1,0:T(2,128)S(1)}) fusion(f32[8192]{0:T(1024)S(1)} %get-tuple-element.25, f32[8192]{0:T(1024)S(1)} %get-tuple-element.24, f32[1,2,64,128]{3,2,1,0:T(8,128)} %bitcast.31, f32[8192]{0:T(1024)S(1)} %get-tuple-element.21, f32[8192]{0:T(1024)S(1)} %get-tuple-element.20, ...), kind=kLoop, calls=%fused_computation.34 | loop fusion | flops 1130496 | bytes 425984 | tf_op jit(solution)/shard_map/mul | solution.py:255
  39.2 0.0 copy-done.1
  39.2 1.3 %fusion.4 = (f32[2,8192]{1,0:T(2,128)}, f32[2,8192]{1,0:T(2,128)}) fusion(f32[2,8192]{1,0:T(2,128)S(1)} %get-tuple-element.9, f32[8192]{0:T(1024)S(1)} %get-tuple-element.26, f32[8192]{0:T(1024)S(1)} %get-tuple-element.24, f32[8192]{0:T(1024)S(1)} %get-tuple-element.18, f32[1,2,64,128]{3,2,1,0:T(8,128)S(1)} %bitcast.32, f32[8192]{0:T(1024)S(1)} %get-tuple-element.21, ...), kind=kLoop, calls=%fused_computation.16 | loop fusion | flops 1212416 | bytes 524288 | tf_op jit(solution)/shard_map/mul | solution.py:254
  (4 shorter events, 0.1 us)
Async XLA Ops:
  3.5 17.9 %collective-permute-start = (bf16[144,512]{1,0:T(8,128)(2,1)}, bf16[144,512]{1,0:T(8,128)(2,1)S(1)}, u32[]{:S(2)}, u32[]{:S(2)}) collective-permute-start(bf16[144,512]{1,0:T(8,128)(2,1)} %shard_map.148), channel_id=1, source_target_pairs={{0,0},{5,1},{10,2},{15,3},{4,4},{1,5},{14,6},{11,7},{8,8},{13,9},{... | collective-permute-start | bytes 442376 | tf_op jit(solution)/shard_map/ppermute | solution.py:298
  5.1 16.3 %collective-permute-start.1 = (bf16[144,512]{1,0:T(8,128)(2,1)}, bf16[144,512]{1,0:T(8,128)(2,1)S(1)}, u32[]{:S(2)}, u32[]{:S(2)}) collective-permute-start(bf16[144,512]{1,0:T(8,128)(2,1)} %shard_map.148), channel_id=1, source_target_pairs={{16,0},{21,1},{26,2},{31,3},{20,4},{17,5},{30,6},{27,7},{24,8},{29... | collective-permute-start | bytes 442376 | tf_op jit(solution)/shard_map/ppermute | solution.py:298
  21.4 1.0 %copy-start = (f32[13,64,128]{2,1,0:T(8,128)S(1)}, f32[13,64,128]{2,1,0:T(8,128)}, u32[]{:S(2)}) copy-start(f32[13,64,128]{2,1,0:T(8,128)} %get-tuple-element.5.refs_2_) | copy-start | bytes 1277956
  22.4 16.8 %copy-start.1 = (f32[2,64,128]{2,1,0:T(8,128)S(1)}, f32[2,64,128]{2,1,0:T(8,128)}, u32[]{:S(2)}) copy-start(f32[2,64,128]{2,1,0:T(8,128)} %get-tuple-element.6) | copy-start | bytes 196612
  30.0 5.8 %collective-permute-start.2 = (f32[128,128]{1,0:T(8,128)S(1)}, f32[128,128]{1,0:T(8,128)S(1)}, u32[]{:S(2)}, u32[]{:S(2)}) collective-permute-start(f32[128,128]{1,0:T(8,128)S(1)} %shard_map.150), channel_id=1, source_target_pairs={{0,2},{1,3},{2,0},{3,1},{4,6},{5,7},{6,4},{7,5},{8,10},{9,11},{10,... | collective-permute-start | bytes 196616 | tf_op jit(solution)/shard_map/ppermute | solution.py:348
  35.8 1.3 %collective-permute-start.3 = (f32[128,128]{1,0:T(8,128)S(1)}, f32[128,128]{1,0:T(8,128)S(1)}, u32[]{:S(2)}, u32[]{:S(2)}) collective-permute-start(f32[128,128]{1,0:T(8,128)S(1)} %add.46), channel_id=1, source_target_pairs={{0,1},{1,0},{2,3},{3,2},{4,5},{5,4},{6,7},{7,6},{8,9},{9,8},{10,11... | collective-permute-start | bytes 196616 | tf_op jit(solution)/shard_map/ppermute | solution.py:348

commit v2 on v1

v2 whole, which is shorter than its diff:
```python
import functools

import jax
import jax.numpy as jnp
from jax import lax
from jax.experimental import pallas as pl
from jax.experimental.pallas import tpu as pltpu
from jax.sharding import PartitionSpec as P

NE = 64
NK = 32
HOT = 2
LANES = 128
BAND = 8
BLOCKS = NE // BAND
TILES = BAND * NK // LANES
WIDE = BAND * NK
REACH = BAND + 3
EXTRA = 16
CENTRE = 1.4
PREPARE_STEP = 16
SURFACE_STEP = 16

RATE = 0.03
INV_ROOT_TWO = 0.7071067811865476
INV_ROOT_TAU = 0.3989422804014327

VMEM = pl.BlockSpec(memory_space=pltpu.VMEM)
HBM = pl.BlockSpec(memory_space=pltpu.HBM)
F32 = jnp.float32
BF16 = jnp.bfloat16

(WE, WK, ROW, COL, BLK, SLOT, PICK) = (0, 4, 8, 9, 10, 11, 12)
(ROOT, MONEY, GROWTH, CASH, VALUE) = (13, 14, 15, 16, 17)
PREPARED = 18


def spline_weights(offset):
    square = offset * offset
    offset_cube = square * offset
    return (
        0.5 * (2.0 * square - offset_cube - offset),
        0.5 * (3.0 * offset_cube - 5.0 * square + 2.0),
        0.5 * (4.0 * square - 3.0 * offset_cube + offset),
        0.5 * (offset_cube - square),
    )


def params(kilobytes):
    return pltpu.CompilerParams(vmem_limit_bytes=kilobytes << 10)


def pack_kernel(hot_in, log_vol_in, beta_in, out_ref, log_vol_ref, beta_ref, hot_ref, sems, small):
    owned = log_vol_ref.shape[0]
    per_tile = LANES // owned
    steps = BLOCKS // per_tile
    width = log_vol_ref.shape[1] // steps
    copies = []
    for tile in range(steps):
        columns = pl.ds(tile * width, width)
        copies.append(
            pltpu.make_async_copy(
                log_vol_in.at[:, columns], log_vol_ref.at[:, columns], sems.at[tile]
            )
        )
    copies.append(pltpu.make_async_copy(beta_in, beta_ref, small.at[0]))
    copies.append(pltpu.make_async_copy(hot_in, hot_ref, small.at[1]))
    for copy in copies:
        copy.start()
    for tile in range(steps):
        copies[tile].wait()
        for half in range(TILES):
            first = [((tile * per_tile + i) * TILES + half) * LANES for i in range(per_tile)]
            stacked = jnp.concatenate([log_vol_ref[:, c : c + LANES] for c in first], axis=0)
            out_ref[half * LANES : (half + 1) * LANES, tile * LANES : (tile + 1) * LANES] = (
                jnp.transpose(stacked) + CENTRE
            ).astype(BF16)
    copies[steps].wait()
    copies[steps + 1].wait()
    row = lax.broadcasted_iota(jnp.int32, (EXTRA, LANES), 0)
    beta = jnp.broadcast_to(beta_ref[...], (EXTRA, owned))
    high = beta.astype(BF16).astype(F32)
    middle = (beta - high).astype(BF16).astype(F32)
    low = beta - high - middle
    zero = jnp.zeros((EXTRA, LANES), F32)
    row_b = row[:, 0:owned]
    pieces = jnp.where(row_b == 0, high, jnp.where(row_b == 1, middle, jnp.where(row_b == 2, low, 0.0)))
    hots = zero
    for i in range(HOT):
        hots = jnp.where(row == i, hot_ref[i].astype(F32), hots)
    out_ref[WIDE : WIDE + EXTRA, 0:LANES] = zero.astype(BF16)
    out_ref[WIDE : WIDE + EXTRA, 0:owned] = pieces.astype(BF16)
    out_ref[WIDE : WIDE + EXTRA, LANES : 2 * LANES] = hots.astype(BF16)
    for tile in range(2, BLOCKS // per_tile):
        out_ref[WIDE : WIDE + EXTRA, tile * LANES : (tile + 1) * LANES] = zero.astype(BF16)


def placed(position, weights, first, shape):
    distance = position - jnp.broadcast_to(first, shape)
    result = jnp.zeros(shape, F32)
    for tap in range(4):
        result = jnp.where(distance == float(tap), jnp.broadcast_to(weights[tap], shape), result)
    return result


def prepare_kernel(
    device_count,
    n_scen,
    owned,
    per_step,
    scen_in,
    shock_ref,
    *refs,
):
    whole, reals = refs[:4], refs[4:8]
    out_ref, shift_ref, scen_ref, whole_ref, real_ref, rows_ref, matrix_ref, sems, sem = refs[8:]
    groups = out_ref.shape[1]
    scenarios = shift_ref.shape[0]
    ids = pltpu.make_async_copy(scen_in, scen_ref, sems.at[8])
    ids.start()
    columns = []
    for i in range(4):
        columns.append(pltpu.make_async_copy(whole[i], whole_ref.at[i], sems.at[i]))
        columns.append(pltpu.make_async_copy(reals[i], real_ref.at[i], sems.at[4 + i]))
    for copy in columns:
        copy.start()
    ids.wait()
    copies = []
    for s in range(scenarios):
        first = pl.multiple_of(lax.shift_right_logical(scen_ref[s], 4) * 16, 16)
        copies.append(
            pltpu.make_async_copy(shock_ref.at[pl.ds(first, 16), :], rows_ref.at[s], sem.at[s])
        )
        copies[-1].start()
    for copy in columns:
        copy.wait()
    dest, pick, expiry, strike = [whole_ref[i] for i in range(4)]
    frac_e, frac_k, notional, forward = [real_ref[i] for i in range(4)]
    weights = spline_weights(frac_e)
    for tap in range(4):
        out_ref[WE + tap] = weights[tap].astype(BF16).astype(F32)
    weights = spline_weights(frac_k)
    for tap in range(4):
        out_ref[WK + tap] = weights[tap]
    first_row = expiry - 1
    block = lax.shift_right_logical(first_row, BAND.bit_length() - 1)
    out_ref[ROW] = (first_row - block * BAND).astype(F32)
    out_ref[BLK] = block.astype(F32)
    out_ref[COL] = (strike - 1).astype(F32)
    hot = pick - owned
    step = jnp.where(hot < 0, 0, jnp.where(hot < HOT, device_count - 1, 1))
    owner = (dest + step) & (device_count - 1)
    offset = owner ^ lax.axis_index("trade")
    mine = (offset & (n_scen - 1)) == lax.axis_index("scen")
    slot = lax.shift_right_logical(offset, n_scen.bit_length() - 1)
    out_ref[SLOT] = jnp.where(mine, slot, -1).astype(F32)
    out_ref[PICK] = jnp.where(hot < HOT, pick, pick - HOT).astype(F32)

    maturity = (expiry.astype(F32) + frac_e + 1.0) * (4.0 / NE)
    moneyness = (strike.astype(F32) + frac_k - 0.5 * (NK - 1)) / NK
    scaled = notional * jnp.exp(-RATE * maturity)
    out_ref[ROOT] = jnp.sqrt(maturity)
    out_ref[MONEY] = moneyness
    out_ref[GROWTH] = jnp.exp(moneyness)
    out_ref[CASH] = scaled
    out_ref[VALUE] = scaled * forward

    tiles = NE * NK // LANES
    in_tile = LANES // NK
    line = lax.broadcasted_iota(jnp.int32, (16, NE * NK), 0)
    for s in range(scenarios):
        copies[s].wait()
        wanted = jnp.where(line == (scen_ref[s] & 15), rows_ref[s].astype(F32), 0.0)
        wanted = jnp.sum(wanted, axis=0, keepdims=True)
        stacked = jnp.concatenate(
            [wanted[:, i * LANES : (i + 1) * LANES] for i in range(tiles)], axis=0
        )
        turned = jnp.transpose(stacked)
        for i in range(in_tile):
            matrix_ref[s * NK : (s + 1) * NK, i * tiles : (i + 1) * tiles] = turned[
                i * NK : (i + 1) * NK, :
            ]
    shift = matrix_ref[...].astype(BF16)
    place = lax.broadcasted_iota(jnp.int32, (NE, LANES), 0)
    expiries = (
        (place & (tiles - 1)) * in_tile + lax.shift_right_logical(place, tiles.bit_length() - 1)
    ).astype(F32)
    strikes = lax.broadcasted_iota(jnp.int32, (NK, LANES), 0).astype(F32)

    def some(i, carry):
        sides = []
        for part in range(per_step):
            g = i * per_step + part
            first = out_ref[BLK, pl.ds(g, 1), :] * float(BAND) + out_ref[ROW, pl.ds(g, 1), :]
            taps = [out_ref[WE + tap, pl.ds(g, 1), :] for tap in range(4)]
            sides.append(placed(expiries, taps, first, (NE, LANES)).astype(BF16))
        mixed = jnp.dot(shift, jnp.concatenate(sides, axis=1), preferred_element_type=F32)
        for part in range(per_step):
            g = i * per_step + part
            taps = [out_ref[WK + tap, pl.ds(g, 1), :] for tap in range(4)]
            coefs = placed(strikes, taps, out_ref[COL, pl.ds(g, 1), :], (NK, LANES))
            for s in range(scenarios):
                piece = mixed[s * NK : (s + 1) * NK, part * LANES : (part + 1) * LANES]
                shift_ref[s, pl.ds(g, 1), :] = jnp.sum(piece * coefs, axis=0, keepdims=True)
        return carry

    lax.fori_loop(0, groups // per_step, some, 0)


def surface_kernel(slot, owned, per_step, message_ref, pre_ref, *refs):
    before_ref = refs[0] if len(refs) == 4 else None
    out_ref, table_ref, index_ref = refs[-3:]
    groups = pre_ref.shape[1]
    table_ref[0:WIDE, :] = message_ref[0:WIDE, :]
    table_ref[WIDE : WIDE + 3 * NK, :] = pltpu.roll(
        message_ref[0 : 3 * NK, :].astype(F32), (BLOCKS - 1) * owned, 1
    ).astype(BF16)
    extra = message_ref[WIDE : WIDE + EXTRA, 0 : 2 * LANES].astype(F32)
    betas = extra[0:1, 0:LANES] + extra[1:2, 0:LANES] + extra[2:3, 0:LANES]
    sub = 8
    for i in range(groups // sub):
        rows = pl.ds(i * sub, sub)
        held = pre_ref[SLOT, rows, :] == float(slot)
        local = pre_ref[PICK, rows, :]
        for h in range(HOT):
            hot = jnp.broadcast_to(extra[h : h + 1, LANES : 2 * LANES], (sub, LANES))
            local = jnp.where(local == float(owned + h), hot, local)
        looked = jnp.take_along_axis(
            jnp.broadcast_to(betas, (sub, LANES)),
            local.astype(jnp.int32),
            axis=1,
            mode="promise_in_bounds",
        )
        index_ref[rows, :] = jnp.where(held, local, -1.0)
        later = pl.ds(groups + i * sub, sub)
        other = 0.0 if before_ref is None else before_ref[later, :]
        out_ref[later, :] = jnp.where(held, looked, other)

    underlyings = lax.broadcasted_iota(jnp.int32, (owned, LANES), 0).astype(F32)
    strikes = lax.broadcasted_iota(jnp.int32, (NK, LANES), 0).astype(F32)
    expiries = lax.broadcasted_iota(jnp.int32, (2 * BAND, LANES), 0).astype(F32)
    zero = jnp.zeros((owned, LANES), BF16)

    def some(i, carry):
        sides = []
        for part in range(per_step):
            g = i * per_step + part
            index = jnp.broadcast_to(index_ref[pl.ds(g, 1), :], (owned, LANES))
            chosen = jnp.where(underlyings == index, 1.0, 0.0).astype(BF16)
            block = jnp.broadcast_to(pre_ref[BLK, pl.ds(g, 1), :], (owned, LANES)).astype(BF16)
            sides.append(
                jnp.concatenate(
                    [
                        jnp.where(block == jnp.asarray(j, BF16), chosen, zero)
                        for j in range(BLOCKS)
                    ],
                    axis=0,
                )
            )
        product = jnp.dot(
            table_ref[...], jnp.concatenate(sides, axis=1), preferred_element_type=F32
        )
        for part in range(per_step):
            g = i * per_step + part
            columns = slice(part * LANES, (part + 1) * LANES)
            taps = [pre_ref[WE + tap, pl.ds(g, 1), :] for tap in range(4)]
            mix = placed(expiries, taps, pre_ref[ROW, pl.ds(g, 1), :], (2 * BAND, LANES))
            curve = jnp.zeros((NK, LANES), F32)
            for a in range(REACH):
                curve = curve + product[a * NK : (a + 1) * NK, columns] * mix[a : a + 1, :]
            taps_k = [pre_ref[WK + tap, pl.ds(g, 1), :] for tap in range(4)]
            coefs = placed(strikes, taps_k, pre_ref[COL, pl.ds(g, 1), :], (NK, LANES))
            level = jnp.sum(curve * coefs, axis=0, keepdims=True)
            weight = (taps[0] + taps[1] + taps[2] + taps[3]) * (
                taps_k[0] + taps_k[1] + taps_k[2] + taps_k[3]
            )
            held = index_ref[pl.ds(g, 1), :] >= 0.0
            other = 0.0 if before_ref is None else before_ref[pl.ds(g, 1), :]
            out_ref[pl.ds(g, 1), :] = jnp.where(held, level - CENTRE * weight, other)
        return carry

    lax.fori_loop(0, groups // per_step, some, 0)


def value_kernel(part_ref, rest_ref, shift_ref, pre_ref, price_ref, vega_ref, delta_ref):
    scenarios, groups = shift_ref.shape[0], shift_ref.shape[1]
    sub = 8
    for i in range(groups // sub):
        rows = pl.ds(i * sub, sub)
        later = pl.ds(groups + i * sub, sub)
        level = part_ref[rows, :] + rest_ref[rows, :]
        slope = part_ref[later, :] + rest_ref[later, :]
        root_time = pre_ref[ROOT, rows, :]
        moneyness = pre_ref[MONEY, rows, :]
        growth = pre_ref[GROWTH, rows, :]
        scaled = pre_ref[CASH, rows, :]
        value = pre_ref[VALUE, rows, :]
        results = ([], [], [])
        for s in range(scenarios):
            spread = jnp.exp(level + slope * shift_ref[s, rows, :]) * root_time
            upper_d = -moneyness / spread + 0.5 * spread
            lower_d = upper_d - spread
            cdf_upper = 0.5 + 0.5 * lax.erf(upper_d * INV_ROOT_TWO)
            cdf_lower = 0.5 + 0.5 * lax.erf(lower_d * INV_ROOT_TWO)
            results[0].append(value * (cdf_upper - growth * cdf_lower))
            results[1].append(value * INV_ROOT_TAU * jnp.exp(-0.5 * upper_d * upper_d) * root_time)
            results[2].append(scaled * cdf_upper)
        for r in range(sub):
            columns = pl.ds((i * sub + r) * LANES, LANES)
            for ref, result in zip((price_ref, vega_ref, delta_ref), results):
                ref[:, columns] = jnp.concatenate([x[r : r + 1, :] for x in result], axis=0)


def shards(
    log_vol,
    beta,
    shock_table,
    scen_ids,
    hot_index,
    dest,
    pick,
    expiry_cell,
    strike_cell,
    frac_e,
    frac_k,
    notional,
    forward,
):
    n_trade = lax.axis_size("trade")
    n_scen = lax.axis_size("scen")
    slots = n_trade // n_scen
    owned = log_vol.shape[0]
    trades = pick.shape[0]
    groups = trades // LANES
    scenarios = scen_ids.shape[0]

    message = pl.pallas_call(
        pack_kernel,
        out_shape=jax.ShapeDtypeStruct((WIDE + EXTRA, BLOCKS * owned), BF16),
        in_specs=[HBM] * 3,
        out_specs=VMEM,
        scratch_shapes=[
            pltpu.VMEM(log_vol.shape, F32),
            pltpu.VMEM((1, owned), F32),
            pltpu.SMEM(hot_index.shape, jnp.int32),
            pltpu.SemaphoreType.DMA((BLOCKS * owned // LANES,)),
            pltpu.SemaphoreType.DMA((2,)),
        ],
        compiler_params=params(60000),
    )(hot_index, log_vol, beta.reshape(1, owned))

    received = [None] * slots
    for k in reversed(range(slots)):
        pairs = [
            ((d ^ (q + k * n_scen)) * n_scen + q, d * n_scen + q)
            for d in range(n_trade)
            for q in range(n_scen)
        ]
        received[k] = lax.ppermute(message, ("trade", "scen"), pairs)

    dense = [
        column.reshape(groups, LANES)
        for column in (
            dest,
            pick,
            expiry_cell,
            strike_cell,
            frac_e,
            frac_k,
            notional,
            forward,
        )
    ]
    prepared, shift_level = pl.pallas_call(
        functools.partial(prepare_kernel, n_trade, n_scen, owned, PREPARE_STEP),
        out_shape=(
            jax.ShapeDtypeStruct((PREPARED, groups, LANES), F32),
            jax.ShapeDtypeStruct((scenarios, groups, LANES), F32),
        ),
        in_specs=[HBM] * 10,
        out_specs=(VMEM, VMEM),
        scratch_shapes=[
            pltpu.SMEM(scen_ids.shape, jnp.int32),
            pltpu.VMEM((4, groups, LANES), jnp.int32),
            pltpu.VMEM((4, groups, LANES), F32),
            pltpu.VMEM((scenarios, 16, NE * NK), BF16),
            pltpu.VMEM((scenarios * NK, NE), F32),
            pltpu.SemaphoreType.DMA((9,)),
            pltpu.SemaphoreType.DMA((scenarios,)),
        ],
        cost_estimate=pl.CostEstimate(flops=40_000_000, bytes_accessed=6_000_000, transcendentals=0),
        compiler_params=params(60000),
    )(scen_ids, shock_table, *dense)

    partial_levels = None
    for k in range(slots):
        before = [] if partial_levels is None else [partial_levels]
        partial_levels = pl.pallas_call(
            functools.partial(surface_kernel, k, owned, SURFACE_STEP),
            out_shape=jax.ShapeDtypeStruct((2 * groups, LANES), F32),
            in_specs=[VMEM] * (2 + len(before)),
            out_specs=VMEM,
            scratch_shapes=[
                pltpu.VMEM((WIDE + 3 * NK, BLOCKS * owned), BF16),
                pltpu.VMEM((groups, LANES), F32),
            ],
            compiler_params=params(24576),
        )(received[k], prepared, *before)

    rest = jnp.zeros_like(partial_levels) if n_scen == 1 else None
    hop = n_scen // 2
    while hop:
        if rest is not None:
            partial_levels = partial_levels + rest
        rest = lax.ppermute(partial_levels, "scen", [(i, i ^ hop) for i in range(n_scen)])
        hop //= 2
    return pl.pallas_call(
        value_kernel,
        out_shape=(jax.ShapeDtypeStruct((scenarios, trades), F32),) * 3,
        in_specs=[VMEM] * 4,
        out_specs=(VMEM,) * 3,
        compiler_params=params(8192),
    )(partial_levels, rest, shift_level, prepared)


def solution(mesh):
    in_specs = (
        P("trade", None),
        P("trade"),
        P(),
        P("scen"),
        P("trade"),
        P("trade", None),
        P("trade"),
        P("trade"),
        P("trade"),
        P("trade"),
        P("trade"),
        P("trade"),
        P("trade"),
    )
    out_specs = (P("scen", "trade"), P("scen", "trade"), P("scen", "trade"))
    return jax.shard_map(shards, mesh=mesh, in_specs=in_specs, out_specs=out_specs, check_vma=False)
```

time: 41.1 us -> 27.8 us (0.68)
  the two profiles are of different devices: /device:TPU:0 before, /device:TPU:27 now
where the time goes in v2:
time: 27.8 us; the launch traced here: 27.4 us
  Pallas kernels  11.5 us (41%)
  starting transfers between devices  10.8 us (39%)
  waiting for transfers between devices  2.56 us (9%)
  local copies, waits for them, and re-layouts  1.9 us (7%)
  between operations  0.7 us (3%)
    ppermute x2, starting transfers between devices, shards(): lax.ppermute(partial_levels, 'scen', [(i, i ^ hop) for i in range(n_scen)])  6.65 us
    pallas_call x2, Pallas kernels, shards(): pl.pallas_call(functools.partial(surface_kernel, k, owned, SURFACE_STEP),...  4.77 us
    ppermute x2, starting transfers between devices, shards(): received[k] = lax.ppermute(message, ('trade', 'scen'), pairs)  4.11 us
    pallas_call x1, Pallas kernels, shards(): pl.pallas_call(functools.partial(prepare_kernel, n_trade, n_scen, owned,...  4.1 us
    ppermute x2, waiting for transfers between devices, shards(): lax.ppermute(partial_levels, 'scen', [(i, i ^ hop) for i in range(n_scen)])  2.56 us
    unnamed x4, local copies, waits for them, and re-layouts  1.9 us
    pallas_call x1, Pallas kernels, shards(): pl.pallas_call(pack_kernel, out_shape=jax.ShapeDtypeStruct((WIDE + EXTRA,...  1.81 us
    pallas_call x1, Pallas kernels, shards(): pl.pallas_call(value_kernel, out_shape=(jax.ShapeDtypeStruct((scenarios,...  0.79 us
  transfers between devices with their start and end apart: 4, of which 2 were waited for; matrix products, arithmetic and copies ran while one was open for 0% of the time, Pallas kernels for 24%

profile of v2, /device:TPU:27, one launch (start us, length us, event | category | flops | bytes accessed | tf_op | source)
XLA Modules:
  0.0 27.4 jit_solution(10369509968478330571)
XLA Ops:
  0.6 1.8 %shard_map.148 = bf16[272,256]{1,0:T(8,128)(2,1)} custom-call(s32[2]{0:T(128)} %hot_in.1, f32[32,2048]{1,0:T(8,128)} %log_vol_in.1, f32[1,32]{1,0:T(1,128)} %bitcast.17), custom_call_target="tpu_custom_call" | custom-call | tf_op jit(solution)/shard_map/pallas_call | solution.py:337
  2.5 3.0 %collective-permute-start.1 = (bf16[272,256]{1,0:T(8,128)(2,1)}, bf16[272,256]{1,0:T(8,128)(2,1)S(1)}, u32[]{:S(2)}, u32[]{:S(2)}) collective-permute-start(bf16[272,256]{1,0:T(8,128)(2,1)} %shard_map.148), channel_id=1, source_target_pairs={{0,0},{5,1},{10,2},{15,3},{4,4},{1,5},{14,6},{11,7},{8,8},{13,9},{... | collective-permute-start | bytes 417800 | tf_op jit(solution)/shard_map/ppermute | solution.py:359
  5.5 1.1 %collective-permute-start = (bf16[272,256]{1,0:T(8,128)(2,1)}, bf16[272,256]{1,0:T(8,128)(2,1)S(1)}, u32[]{:S(2)}, u32[]{:S(2)}) collective-permute-start(bf16[272,256]{1,0:T(8,128)(2,1)} %shard_map.148), channel_id=1, source_target_pairs={{16,0},{21,1},{26,2},{31,3},{20,4},{17,5},{30,6},{27,7},{24,8},{29... | collective-permute-start | bytes 417800 | tf_op jit(solution)/shard_map/ppermute | solution.py:359
  6.6 4.1 %shard_map.149 = (f32[18,64,128]{2,1,0:T(8,128)}, f32[2,64,128]{2,1,0:T(8,128)}) custom-call(s32[2]{0:T(128)} %scen_in.1, bf16[512,2048]{1,0:T(8,128)(2,1)} %shock_ref.1, s32[64,128]{1,0:T(8,128)} %bitcast.9, s32[64,128]{1,0:T(8,128)} %bitcast.10, s32[64,128]{1,0:T(8,128)} %bitcast.11, s32[64,128]{1,0:T(8,128)} %bitcast.12, f32[64,128]{1,0:T(8,128)} %bitcast.13, ...), custom_call_target="tpu_custom_call" | custom-call | flops 40000000 | bytes 6000000 | tf_op jit(solution)/shard_map/pallas_call | solution.py:374
  10.7 0.0 collective-permute-done.1.message_ref
  10.7 0.0 copy-start
  10.7 1.1 %copy-done = f32[18,64,128]{2,1,0:T(8,128)S(1)} copy-done((f32[18,64,128]{2,1,0:T(8,128)S(1)}, f32[18,64,128]{2,1,0:T(8,128)}, u32[]{:S(2)}) %copy-start) | copy-done | bytes 589848
  11.8 2.4 %shard_map.150.refs_0_ = f32[128,128]{1,0:T(8,128)S(1)} custom-call(bf16[272,256]{1,0:T(8,128)(2,1)S(1)} %collective-permute-done.1.message_ref, f32[18,64,128]{2,1,0:T(8,128)S(1)} %copy-done), custom_call_target="tpu_custom_call" | custom-call | tf_op jit(solution)/shard_map/pallas_call | solution.py:398
  14.1 0.0 collective-permute-done.message_ref
  14.1 2.4 %shard_map.151 = f32[128,128]{1,0:T(8,128)S(1)} custom-call(bf16[272,256]{1,0:T(8,128)(2,1)S(1)} %collective-permute-done.message_ref, f32[18,64,128]{2,1,0:T(8,128)S(1)} %copy-done, f32[128,128]{1,0:T(8,128)S(1)} %shard_map.150.refs_0_), custom_call_target="tpu_custom_call" | custom-call | tf_op jit(solution)/shard_map/pallas_call | solution.py:398
  16.6 1.7 %collective-permute-start.2 = (f32[128,128]{1,0:T(8,128)S(1)}, f32[128,128]{1,0:T(8,128)S(1)}, u32[]{:S(2)}, u32[]{:S(2)}) collective-permute-start(f32[128,128]{1,0:T(8,128)S(1)} %shard_map.151), channel_id=1, source_target_pairs={{0,2},{1,3},{2,0},{3,1},{4,6},{5,7},{6,4},{7,5},{8,10},{9,11},{10,... | collective-permute-start | bytes 196616 | tf_op jit(solution)/shard_map/ppermute | solution.py:415
  18.2 1.7 %collective-permute-done.2 = f32[128,128]{1,0:T(8,128)S(1)} collective-permute-done((f32[128,128]{1,0:T(8,128)S(1)}, f32[128,128]{1,0:T(8,128)S(1)}, u32[]{:S(2)}, u32[]{:S(2)}) %collective-permute-start.2) | collective-permute-done | bytes 65568 | tf_op jit(solution)/shard_map/ppermute | solution.py:415
  19.9 5.0 %collective-permute-start.3 = (f32[128,128]{1,0:T(8,128)S(1)}, f32[128,128]{1,0:T(8,128)S(1)}, u32[]{:S(2)}, u32[]{:S(2)}) collective-permute-start(f32[128,128]{1,0:T(8,128)S(1)} %add.3.part_ref), channel_id=1, source_target_pairs={{0,1},{1,0},{2,3},{3,2},{4,5},{5,4},{6,7},{7,6},{8,9},{9,8},{10,11... | collective-permute-start | bytes 196616 | tf_op jit(solution)/shard_map/ppermute | solution.py:415
  24.9 0.9 %collective-permute-done.3.rest_ref = f32[128,128]{1,0:T(8,128)S(1)} collective-permute-done((f32[128,128]{1,0:T(8,128)S(1)}, f32[128,128]{1,0:T(8,128)S(1)}, u32[]{:S(2)}, u32[]{:S(2)}) %collective-permute-start.3) | collective-permute-done | bytes 65568 | tf_op jit(solution)/shard_map/ppermute | solution.py:415
  25.8 0.0 copy-start.1
  25.8 0.8 %copy-done.1 = f32[2,64,128]{2,1,0:T(8,128)S(1)} copy-done((f32[2,64,128]{2,1,0:T(8,128)S(1)}, f32[2,64,128]{2,1,0:T(8,128)}, u32[]{:S(2)}) %copy-start.1) | copy-done | bytes 65560
  26.6 0.8 %shard_map.152 = (f32[2,8192]{1,0:T(2,128)}, f32[2,8192]{1,0:T(2,128)}, f32[2,8192]{1,0:T(2,128)}) custom-call(f32[128,128]{1,0:T(8,128)S(1)} %add.3.part_ref, f32[128,128]{1,0:T(8,128)S(1)} %collective-permute-done.3.rest_ref, f32[2,64,128]{2,1,0:T(8,128)S(1)} %copy-done.1, f32[18,64,128]{2,1,0:T(8,128)S(1)} %copy-done), custom_call_target="tpu_custom_call" | custom-call | tf_op jit(solution)/shard_map/pallas_call | solution.py:417
  (1 shorter events, 0.0 us)
Async XLA Ops:
  2.5 8.2 %collective-permute-start.1 = (bf16[272,256]{1,0:T(8,128)(2,1)}, bf16[272,256]{1,0:T(8,128)(2,1)S(1)}, u32[]{:S(2)}, u32[]{:S(2)}) collective-permute-start(bf16[272,256]{1,0:T(8,128)(2,1)} %shard_map.148), channel_id=1, source_target_pairs={{0,0},{5,1},{10,2},{15,3},{4,4},{1,5},{14,6},{11,7},{8,8},{13,9},{... | collective-permute-start | bytes 417800 | tf_op jit(solution)/shard_map/ppermute | solution.py:359
  5.5 8.6 %collective-permute-start = (bf16[272,256]{1,0:T(8,128)(2,1)}, bf16[272,256]{1,0:T(8,128)(2,1)S(1)}, u32[]{:S(2)}, u32[]{:S(2)}) collective-permute-start(bf16[272,256]{1,0:T(8,128)(2,1)} %shard_map.148), channel_id=1, source_target_pairs={{16,0},{21,1},{26,2},{31,3},{20,4},{17,5},{30,6},{27,7},{24,8},{29... | collective-permute-start | bytes 417800 | tf_op jit(solution)/shard_map/ppermute | solution.py:359
  10.7 1.1 %copy-start = (f32[18,64,128]{2,1,0:T(8,128)S(1)}, f32[18,64,128]{2,1,0:T(8,128)}, u32[]{:S(2)}) copy-start(f32[18,64,128]{2,1,0:T(8,128)} %get-tuple-element.5.pre_ref) | copy-start | bytes 1769476
  16.6 3.3 %collective-permute-start.2 = (f32[128,128]{1,0:T(8,128)S(1)}, f32[128,128]{1,0:T(8,128)S(1)}, u32[]{:S(2)}, u32[]{:S(2)}) collective-permute-start(f32[128,128]{1,0:T(8,128)S(1)} %shard_map.151), channel_id=1, source_target_pairs={{0,2},{1,3},{2,0},{3,1},{4,6},{5,7},{6,4},{7,5},{8,10},{9,11},{10,... | collective-permute-start | bytes 196616 | tf_op jit(solution)/shard_map/ppermute | solution.py:415
  19.9 5.9 %collective-permute-start.3 = (f32[128,128]{1,0:T(8,128)S(1)}, f32[128,128]{1,0:T(8,128)S(1)}, u32[]{:S(2)}, u32[]{:S(2)}) collective-permute-start(f32[128,128]{1,0:T(8,128)S(1)} %add.3.part_ref), channel_id=1, source_target_pairs={{0,1},{1,0},{2,3},{3,2},{4,5},{5,4},{6,7},{7,6},{8,9},{9,8},{10,11... | collective-permute-start | bytes 196616 | tf_op jit(solution)/shard_map/ppermute | solution.py:415
  25.8 0.8 %copy-start.1 = (f32[2,64,128]{2,1,0:T(8,128)S(1)}, f32[2,64,128]{2,1,0:T(8,128)}, u32[]{:S(2)}) copy-start(f32[2,64,128]{2,1,0:T(8,128)} %get-tuple-element.6.shift_ref) | copy-start | bytes 196612

commit v3 on v2

--- a/solution.py
+++ b/solution.py
@@ -44,6 +44,10 @@
         0.5 * (4.0 * square - 3.0 * offset_cube + offset),
         0.5 * (offset_cube - square),
     )
+
+
+def in_hbm(*arrays):
+    return [pltpu.with_memory_space_constraint(x, pltpu.HBM) if x.size > 1 else x for x in arrays]
 
 
 def params(kilobytes):
@@ -336,7 +340,7 @@
 
     message = pl.pallas_call(
         pack_kernel,
-        out_shape=jax.ShapeDtypeStruct((WIDE + EXTRA, BLOCKS * owned), BF16),
+        out_shape=pltpu.VMEM((WIDE + EXTRA, BLOCKS * owned), BF16),
         in_specs=[HBM] * 3,
         out_specs=VMEM,
         scratch_shapes=[
@@ -346,8 +350,8 @@
             pltpu.SemaphoreType.DMA((BLOCKS * owned // LANES,)),
             pltpu.SemaphoreType.DMA((2,)),
         ],
-        compiler_params=params(60000),
-    )(hot_index, log_vol, beta.reshape(1, owned))
+        compiler_params=params(16384),
+    )(*in_hbm(hot_index, log_vol, beta.reshape(1, owned)))
 
     received = [None] * slots
     for k in reversed(range(slots)):
@@ -374,8 +378,8 @@
     prepared, shift_level = pl.pallas_call(
         functools.partial(prepare_kernel, n_trade, n_scen, owned, PREPARE_STEP),
         out_shape=(
-            jax.ShapeDtypeStruct((PREPARED, groups, LANES), F32),
-            jax.ShapeDtypeStruct((scenarios, groups, LANES), F32),
+            pltpu.VMEM((PREPARED, groups, LANES), F32),
+            pltpu.VMEM((scenarios, groups, LANES), F32),
         ),
         in_specs=[HBM] * 10,
         out_specs=(VMEM, VMEM),
@@ -389,8 +393,8 @@
             pltpu.SemaphoreType.DMA((scenarios,)),
         ],
         cost_estimate=pl.CostEstimate(flops=40_000_000, bytes_accessed=6_000_000, transcendentals=0),
-        compiler_params=params(60000),
-    )(scen_ids, shock_table, *dense)
+        compiler_params=params(16384),
+    )(*in_hbm(scen_ids, shock_table, *dense))
 
     partial_levels = None
     for k in range(slots):

time: 27.8 us -> 25.2 us (0.906)
  the two profiles are of different devices: /device:TPU:27 before, /device:TPU:0 now
where the time goes in v3:
time: 25.2 us; the launch traced here: 25 us
  starting transfers between devices  10.4 us (41%)
  Pallas kernels  10.2 us (40%)
  waiting for transfers between devices  3.63 us (14%)
  between operations  0.69 us (3%)
    ppermute x2, starting transfers between devices, shards(): lax.ppermute(partial_levels, 'scen', [(i, i ^ hop) for i in range(n_scen)])  5.63 us
    pallas_call x2, Pallas kernels, shards(): pl.pallas_call(functools.partial(surface_kernel, k, owned, SURFACE_STEP),...  4.78 us
    ppermute x2, starting transfers between devices, shards(): received[k] = lax.ppermute(message, ('trade', 'scen'), pairs)  4.77 us
    ppermute x2, waiting for transfers between devices, shards(): lax.ppermute(partial_levels, 'scen', [(i, i ^ hop) for i in range(n_scen)])  3.49 us
    pallas_call x1, Pallas kernels, shards(): pl.pallas_call(functools.partial(prepare_kernel, n_trade, n_scen, owned,...  3.47 us
    pallas_call x1, Pallas kernels, shards(): pl.pallas_call(pack_kernel, out_shape=pltpu.VMEM((WIDE + EXTRA, BLOCKS *...  1.17 us
    pallas_call x1, Pallas kernels, shards(): pl.pallas_call(value_kernel, out_shape=(jax.ShapeDtypeStruct((scenarios,...  0.8 us
  transfers between devices with their start and end apart: 4, of which 3 were waited for; matrix products, arithmetic and copies ran while one was open for 0% of the time, Pallas kernels for 23%

profile of v3, /device:TPU:0, one launch (start us, length us, event | category | flops | bytes accessed | tf_op | source)
XLA Modules:
  0.0 25.0 jit_solution(5391996162829236931)
XLA Ops:
  0.6 1.2 %shard_map.148 = bf16[272,256]{1,0:T(8,128)(2,1)S(1)} custom-call(s32[2]{0:T(128)} %hot_in.1, f32[32,2048]{1,0:T(8,128)} %log_vol_in.1, f32[1,32]{1,0:T(1,128)} %bitcast.17), custom_call_target="tpu_custom_call" | custom-call | tf_op jit(solution)/shard_map/pallas_call | solution.py:341
  1.8 0.7 %collective-permute-start.1 = (bf16[272,256]{1,0:T(8,128)(2,1)S(1)}, bf16[272,256]{1,0:T(8,128)(2,1)S(1)}, u32[]{:S(2)}, u32[]{:S(2)}) collective-permute-start(bf16[272,256]{1,0:T(8,128)(2,1)S(1)} %shard_map.148), channel_id=1, source_target_pairs={{0,0},{5,1},{10,2},{15,3},{4,4},{1,5},{14,6},{11,7},{8,8},{13,9},{... | collective-permute-start | bytes 417800 | tf_op jit(solution)/shard_map/ppermute | solution.py:363
  2.5 4.1 %collective-permute-start = (bf16[272,256]{1,0:T(8,128)(2,1)S(1)}, bf16[272,256]{1,0:T(8,128)(2,1)S(1)}, u32[]{:S(2)}, u32[]{:S(2)}) collective-permute-start(bf16[272,256]{1,0:T(8,128)(2,1)S(1)} %shard_map.148), channel_id=1, source_target_pairs={{16,0},{21,1},{26,2},{31,3},{20,4},{17,5},{30,6},{27,7},{24,8},{29... | collective-permute-start | bytes 417800 | tf_op jit(solution)/shard_map/ppermute | solution.py:363
  6.6 3.5 %shard_map.149 = (f32[18,64,128]{2,1,0:T(8,128)S(1)}, f32[2,64,128]{2,1,0:T(8,128)S(1)}) custom-call(s32[2]{0:T(128)} %scen_in.1, bf16[512,2048]{1,0:T(8,128)(2,1)} %shock_ref.1, s32[64,128]{1,0:T(8,128)} %bitcast.9, s32[64,128]{1,0:T(8,128)} %bitcast.10, s32[64,128]{1,0:T(8,128)} %bitcast.11, s32[64,128]{1,0:T(8,128)} %bitcast.12, f32[64,128]{1,0:T(8,128)} %bitcast.13, ...), custom_call_target="tpu_custom_call" | custom-call | flops 40000000 | bytes 6000000 | tf_op jit(solution)/shard_map/pallas_call | solution.py:378
  10.1 0.0 collective-permute-done.1.message_ref
  10.1 2.4 %shard_map.150.refs_0_ = f32[128,128]{1,0:T(8,128)S(1)} custom-call(bf16[272,256]{1,0:T(8,128)(2,1)S(1)} %collective-permute-done.1.message_ref, f32[18,64,128]{2,1,0:T(8,128)S(1)} %get-tuple-element.5.pre_ref), custom_call_target="tpu_custom_call" | custom-call | tf_op jit(solution)/shard_map/pallas_call | solution.py:402
  12.5 0.1 collective-permute-done.message_ref
  12.6 2.4 %shard_map.151 = f32[128,128]{1,0:T(8,128)S(1)} custom-call(bf16[272,256]{1,0:T(8,128)(2,1)S(1)} %collective-permute-done.message_ref, f32[18,64,128]{2,1,0:T(8,128)S(1)} %get-tuple-element.5.pre_ref, f32[128,128]{1,0:T(8,128)S(1)} %shard_map.150.refs_0_), custom_call_target="tpu_custom_call" | custom-call | tf_op jit(solution)/shard_map/pallas_call | solution.py:402
  15.0 5.6 %collective-permute-start.2 = (f32[128,128]{1,0:T(8,128)S(1)}, f32[128,128]{1,0:T(8,128)S(1)}, u32[]{:S(2)}, u32[]{:S(2)}) collective-permute-start(f32[128,128]{1,0:T(8,128)S(1)} %shard_map.151), channel_id=1, source_target_pairs={{0,2},{1,3},{2,0},{3,1},{4,6},{5,7},{6,4},{7,5},{8,10},{9,11},{10,... | collective-permute-start | bytes 196616 | tf_op jit(solution)/shard_map/ppermute | solution.py:419
  20.6 2.2 %collective-permute-done.2 = f32[128,128]{1,0:T(8,128)S(1)} collective-permute-done((f32[128,128]{1,0:T(8,128)S(1)}, f32[128,128]{1,0:T(8,128)S(1)}, u32[]{:S(2)}, u32[]{:S(2)}) %collective-permute-start.2) | collective-permute-done | bytes 65568 | tf_op jit(solution)/shard_map/ppermute | solution.py:419
  22.8 0.1 collective-permute-start.3
  22.9 1.2 %collective-permute-done.3.rest_ref = f32[128,128]{1,0:T(8,128)S(1)} collective-permute-done((f32[128,128]{1,0:T(8,128)S(1)}, f32[128,128]{1,0:T(8,128)S(1)}, u32[]{:S(2)}, u32[]{:S(2)}) %collective-permute-start.3) | collective-permute-done | bytes 65568 | tf_op jit(solution)/shard_map/ppermute | solution.py:419
  24.2 0.8 %shard_map.152 = (f32[2,8192]{1,0:T(2,128)}, f32[2,8192]{1,0:T(2,128)}, f32[2,8192]{1,0:T(2,128)}) custom-call(f32[128,128]{1,0:T(8,128)S(1)} %add.3.part_ref, f32[128,128]{1,0:T(8,128)S(1)} %collective-permute-done.3.rest_ref, f32[2,64,128]{2,1,0:T(8,128)S(1)} %get-tuple-element.6.shift_ref, f32[18,64,128]{2,1,0:T(8,128)S(1)} %get-tuple-element.5.pre_ref), custom_call_target="tpu_custom_call" | custom-call | tf_op jit(solution)/shard_map/pallas_call | solution.py:421
  (1 shorter events, 0.0 us)
Async XLA Ops:
  1.8 8.3 %collective-permute-start.1 = (bf16[272,256]{1,0:T(8,128)(2,1)S(1)}, bf16[272,256]{1,0:T(8,128)(2,1)S(1)}, u32[]{:S(2)}, u32[]{:S(2)}) collective-permute-start(bf16[272,256]{1,0:T(8,128)(2,1)S(1)} %shard_map.148), channel_id=1, source_target_pairs={{0,0},{5,1},{10,2},{15,3},{4,4},{1,5},{14,6},{11,7},{8,8},{13,9},{... | collective-permute-start | bytes 417800 | tf_op jit(solution)/shard_map/ppermute | solution.py:363
  2.5 10.1 %collective-permute-start = (bf16[272,256]{1,0:T(8,128)(2,1)S(1)}, bf16[272,256]{1,0:T(8,128)(2,1)S(1)}, u32[]{:S(2)}, u32[]{:S(2)}) collective-permute-start(bf16[272,256]{1,0:T(8,128)(2,1)S(1)} %shard_map.148), channel_id=1, source_target_pairs={{16,0},{21,1},{26,2},{31,3},{20,4},{17,5},{30,6},{27,7},{24,8},{29... | collective-permute-start | bytes 417800 | tf_op jit(solution)/shard_map/ppermute | solution.py:363
  15.0 7.8 %collective-permute-start.2 = (f32[128,128]{1,0:T(8,128)S(1)}, f32[128,128]{1,0:T(8,128)S(1)}, u32[]{:S(2)}, u32[]{:S(2)}) collective-permute-start(f32[128,128]{1,0:T(8,128)S(1)} %shard_map.151), channel_id=1, source_target_pairs={{0,2},{1,3},{2,0},{3,1},{4,6},{5,7},{6,4},{7,5},{8,10},{9,11},{10,... | collective-permute-start | bytes 196616 | tf_op jit(solution)/shard_map/ppermute | solution.py:419
  22.8 1.3 %collective-permute-start.3 = (f32[128,128]{1,0:T(8,128)S(1)}, f32[128,128]{1,0:T(8,128)S(1)}, u32[]{:S(2)}, u32[]{:S(2)}) collective-permute-start(f32[128,128]{1,0:T(8,128)S(1)} %add.3.part_ref), channel_id=1, source_target_pairs={{0,1},{1,0},{2,3},{3,2},{4,5},{5,4},{6,7},{7,6},{8,9},{9,8},{10,11... | collective-permute-start | bytes 196616 | tf_op jit(solution)/shard_map/ppermute | solution.py:419

commit v4 on v3

--- a/solution.py
+++ b/solution.py
@@ -18,8 +18,9 @@
 REACH = BAND + 3
 EXTRA = 16
 CENTRE = 1.4
-PREPARE_STEP = 16
-SURFACE_STEP = 16
+PREPARE_STEP = 8
+SHIFT_STEP = 32
+SURFACE_STEP = 64
 
 RATE = 0.03
 INV_ROOT_TWO = 0.7071067811865476
@@ -30,9 +31,9 @@
 F32 = jnp.float32
 BF16 = jnp.bfloat16
 
-(WE, WK, ROW, COL, BLK, SLOT, PICK) = (0, 4, 8, 9, 10, 11, 12)
-(ROOT, MONEY, GROWTH, CASH, VALUE) = (13, 14, 15, 16, 17)
-PREPARED = 18
+(WE, FIRST, BLK, SLOT, PICK, BIAS) = (0, 4, 5, 6, 7, 8)
+(ROOT, MONEY, GROWTH, CASH, VALUE) = (9, 10, 11, 12, 13)
+PREPARED = 14
 
 
 def spline_weights(offset):
@@ -117,9 +118,10 @@
     *refs,
 ):
     whole, reals = refs[:4], refs[4:8]
-    out_ref, shift_ref, scen_ref, whole_ref, real_ref, rows_ref, matrix_ref, sems, sem = refs[8:]
+    out_ref, mix_ref, coef_ref, matrix_ref = refs[8:12]
+    scen_ref, whole_ref, real_ref, rows_ref, wide_ref, row_ref, tap_ref, sems, sem = refs[12:]
     groups = out_ref.shape[1]
-    scenarios = shift_ref.shape[0]
+    scenarios = rows_ref.shape[0]
     ids = pltpu.make_async_copy(scen_in, scen_ref, sems.at[8])
     ids.start()
     columns = []
@@ -140,17 +142,21 @@
         copy.wait()
     dest, pick, expiry, strike = [whole_ref[i] for i in range(4)]
     frac_e, frac_k, notional, forward = [real_ref[i] for i in range(4)]
-    weights = spline_weights(frac_e)
+    weights = [w.astype(BF16).astype(F32) for w in spline_weights(frac_e)]
     for tap in range(4):
-        out_ref[WE + tap] = weights[tap].astype(BF16).astype(F32)
-    weights = spline_weights(frac_k)
+        out_ref[WE + tap] = weights[tap]
+    taps = spline_weights(frac_k)
     for tap in range(4):
-        out_ref[WK + tap] = weights[tap]
+        tap_ref[tap] = taps[tap]
+    out_ref[BIAS] = CENTRE * (
+        (weights[0] + weights[1] + weights[2] + weights[3]) * (taps[0] + taps[1] + taps[2] + taps[3])
+    )
     first_row = expiry - 1
     block = lax.shift_right_logical(first_row, BAND.bit_length() - 1)
-    out_ref[ROW] = (first_row - block * BAND).astype(F32)
+    row_ref[0] = (first_row - block * BAND).astype(F32)
+    row_ref[1] = (strike - 1).astype(F32)
+    out_ref[FIRST] = first_row.astype(F32)
     out_ref[BLK] = block.astype(F32)
-    out_ref[COL] = (strike - 1).astype(F32)
     hot = pick - owned
     step = jnp.where(hot < 0, 0, jnp.where(hot < HOT, device_count - 1, 1))
     owner = (dest + step) & (device_count - 1)
@@ -168,6 +174,23 @@
     out_ref[GROWTH] = jnp.exp(moneyness)
     out_ref[CASH] = scaled
     out_ref[VALUE] = scaled * forward
+
+    strikes = lax.broadcasted_iota(jnp.int32, (NK, LANES), 0).astype(F32)
+    expiries = lax.broadcasted_iota(jnp.int32, (2 * BAND, LANES), 0).astype(F32)
+
+    def some(i, carry):
+        for part in range(per_step):
+            g = i * per_step + part
+            columns = pl.ds(pl.multiple_of(g * LANES, LANES), LANES)
+            taps = [out_ref[WE + tap, pl.ds(g, 1), :] for tap in range(4)]
+            mix_ref[:, columns] = placed(
+                expiries, taps, row_ref[0, pl.ds(g, 1), :], (2 * BAND, LANES)
+            )
+            taps = [tap_ref[tap, pl.ds(g, 1), :] for tap in range(4)]
+            coef_ref[:, columns] = placed(strikes, taps, row_ref[1, pl.ds(g, 1), :], (NK, LANES))
+        return carry
+
+    lax.fori_loop(0, groups // per_step, some, 0)
 
     tiles = NE * NK // LANES
     in_tile = LANES // NK
@@ -181,28 +204,34 @@
         )
         turned = jnp.transpose(stacked)
         for i in range(in_tile):
-            matrix_ref[s * NK : (s + 1) * NK, i * tiles : (i + 1) * tiles] = turned[
+            wide_ref[s * NK : (s + 1) * NK, i * tiles : (i + 1) * tiles] = turned[
                 i * NK : (i + 1) * NK, :
             ]
-    shift = matrix_ref[...].astype(BF16)
+    matrix_ref[...] = wide_ref[...].astype(BF16)
+
+
+def shift_kernel(per_step, matrix_ref, pre_ref, coef_ref, after_ref, shift_ref):
+    scenarios, groups = shift_ref.shape[0], shift_ref.shape[1]
+    tiles = NE * NK // LANES
+    in_tile = LANES // NK
+    shift = matrix_ref[...]
     place = lax.broadcasted_iota(jnp.int32, (NE, LANES), 0)
     expiries = (
         (place & (tiles - 1)) * in_tile + lax.shift_right_logical(place, tiles.bit_length() - 1)
     ).astype(F32)
-    strikes = lax.broadcasted_iota(jnp.int32, (NK, LANES), 0).astype(F32)
 
     def some(i, carry):
         sides = []
         for part in range(per_step):
             g = i * per_step + part
-            first = out_ref[BLK, pl.ds(g, 1), :] * float(BAND) + out_ref[ROW, pl.ds(g, 1), :]
-            taps = [out_ref[WE + tap, pl.ds(g, 1), :] for tap in range(4)]
-            sides.append(placed(expiries, taps, first, (NE, LANES)).astype(BF16))
+            taps = [pre_ref[WE + tap, pl.ds(g, 1), :] for tap in range(4)]
+            sides.append(
+                placed(expiries, taps, pre_ref[FIRST, pl.ds(g, 1), :], (NE, LANES)).astype(BF16)
+            )
         mixed = jnp.dot(shift, jnp.concatenate(sides, axis=1), preferred_element_type=F32)
         for part in range(per_step):
             g = i * per_step + part
-            taps = [out_ref[WK + tap, pl.ds(g, 1), :] for tap in range(4)]
-            coefs = placed(strikes, taps, out_ref[COL, pl.ds(g, 1), :], (NK, LANES))
+            coefs = coef_ref[:, pl.ds(pl.multiple_of(g * LANES, LANES), LANES)]
             for s in range(scenarios):
                 piece = mixed[s * NK : (s + 1) * NK, part * LANES : (part + 1) * LANES]
                 shift_ref[s, pl.ds(g, 1), :] = jnp.sum(piece * coefs, axis=0, keepdims=True)
@@ -211,7 +240,7 @@
     lax.fori_loop(0, groups // per_step, some, 0)
 
 
-def surface_kernel(slot, owned, per_step, message_ref, pre_ref, *refs):
+def surface_kernel(slot, owned, per_step, message_ref, pre_ref, mix_ref, coef_ref, *refs):
     before_ref = refs[0] if len(refs) == 4 else None
     out_ref, table_ref, index_ref = refs[-3:]
     groups = pre_ref.shape[1]
@@ -241,8 +270,6 @@
         out_ref[later, :] = jnp.where(held, looked, other)
 
     underlyings = lax.broadcasted_iota(jnp.int32, (owned, LANES), 0).astype(F32)
-    strikes = lax.broadcasted_iota(jnp.int32, (NK, LANES), 0).astype(F32)
-    expiries = lax.broadcasted_iota(jnp.int32, (2 * BAND, LANES), 0).astype(F32)
     zero = jnp.zeros((owned, LANES), BF16)
 
     def some(i, carry):
@@ -267,20 +294,16 @@
         for part in range(per_step):
             g = i * per_step + part
             columns = slice(part * LANES, (part + 1) * LANES)
-            taps = [pre_ref[WE + tap, pl.ds(g, 1), :] for tap in range(4)]
-            mix = placed(expiries, taps, pre_ref[ROW, pl.ds(g, 1), :], (2 * BAND, LANES))
+            here = pl.ds(pl.multiple_of(g * LANES, LANES), LANES)
+            mix = mix_ref[:, here]
             curve = jnp.zeros((NK, LANES), F32)
             for a in range(REACH):
                 curve = curve + product[a * NK : (a + 1) * NK, columns] * mix[a : a + 1, :]
-            taps_k = [pre_ref[WK + tap, pl.ds(g, 1), :] for tap in range(4)]
-            coefs = placed(strikes, taps_k, pre_ref[COL, pl.ds(g, 1), :], (NK, LANES))
-            level = jnp.sum(curve * coefs, axis=0, keepdims=True)
-            weight = (taps[0] + taps[1] + taps[2] + taps[3]) * (
-                taps_k[0] + taps_k[1] + taps_k[2] + taps_k[3]
-            )
+            level = jnp.sum(curve * coef_ref[:, here], axis=0, keepdims=True)
+            level = level - pre_ref[BIAS, pl.ds(g, 1), :]
             held = index_ref[pl.ds(g, 1), :] >= 0.0
             other = 0.0 if before_ref is None else before_ref[pl.ds(g, 1), :]
-            out_ref[pl.ds(g, 1), :] = jnp.where(held, level - CENTRE * weight, other)
+            out_ref[pl.ds(g, 1), :] = jnp.where(held, level, other)
         return carry
 
     lax.fori_loop(0, groups // per_step, some, 0)
@@ -375,20 +398,24 @@
             forward,
         )
     ]
-    prepared, shift_level = pl.pallas_call(
+    prepared, mix, coefs, matrix = pl.pallas_call(
         functools.partial(prepare_kernel, n_trade, n_scen, owned, PREPARE_STEP),
         out_shape=(
             pltpu.VMEM((PREPARED, groups, LANES), F32),
-            pltpu.VMEM((scenarios, groups, LANES), F32),
+            pltpu.VMEM((2 * BAND, trades), F32),
+            pltpu.VMEM((NK, trades), F32),
+            pltpu.VMEM((scenarios * NK, NE), BF16),
         ),
         in_specs=[HBM] * 10,
-        out_specs=(VMEM, VMEM),
+        out_specs=(VMEM,) * 4,
         scratch_shapes=[
             pltpu.SMEM(scen_ids.shape, jnp.int32),
             pltpu.VMEM((4, groups, LANES), jnp.int32),
             pltpu.VMEM((4, groups, LANES), F32),
             pltpu.VMEM((scenarios, 16, NE * NK), BF16),
             pltpu.VMEM((scenarios * NK, NE), F32),
+            pltpu.VMEM((2, groups, LANES), F32),
+            pltpu.VMEM((4, groups, LANES), F32),
             pltpu.SemaphoreType.DMA((9,)),
             pltpu.SemaphoreType.DMA((scenarios,)),
         ],
@@ -397,25 +424,36 @@
     )(*in_hbm(scen_ids, shock_table, *dense))
 
     partial_levels = None
-    for k in range(slots):
+    for k in reversed(range(slots)):
         before = [] if partial_levels is None else [partial_levels]
         partial_levels = pl.pallas_call(
             functools.partial(surface_kernel, k, owned, SURFACE_STEP),
             out_shape=jax.ShapeDtypeStruct((2 * groups, LANES), F32),
-            in_specs=[VMEM] * (2 + len(before)),
+            in_specs=[VMEM] * (4 + len(before)),
             out_specs=VMEM,
             scratch_shapes=[
                 pltpu.VMEM((WIDE + 3 * NK, BLOCKS * owned), BF16),
                 pltpu.VMEM((groups, LANES), F32),
             ],
-            compiler_params=params(24576),
-        )(received[k], prepared, *before)
+            compiler_params=params(32768),
+        )(received[k], prepared, mix, coefs, *before)
+
+    shift_level = pl.pallas_call(
+        functools.partial(shift_kernel, SHIFT_STEP),
+        out_shape=pltpu.VMEM((scenarios, groups, LANES), F32),
+        in_specs=[VMEM] * 3 + [pl.BlockSpec(memory_space=pl.ANY)],
+        out_specs=VMEM,
+        cost_estimate=pl.CostEstimate(flops=40_000_000, bytes_accessed=2_000_000, transcendentals=0),
+        compiler_params=params(16384),
+    )(matrix, prepared, coefs, partial_levels)
 
     rest = jnp.zeros_like(partial_levels) if n_scen == 1 else None
     hop = n_scen // 2
     while hop:
         if rest is not None:
-            partial_levels = partial_levels + rest
+            partial_levels, shift_level = lax.optimization_barrier(
+                (partial_levels + rest, shift_level)
+            )
         rest = lax.ppermute(partial_levels, "scen", [(i, i ^ hop) for i in range(n_scen)])
         hop //= 2
     return pl.pallas_call(

time: 25.2 us -> 23.5 us (0.933)
  starting transfers between devices: 10.4 us -> 6.21 us
  waiting for transfers between devices: 3.63 us -> 7.72 us
  Pallas kernels: 10.2 us -> 8.56 us
    ppermute x2, waiting for transfers between devices: 0.14 us -> 4.65 us  [shards(): received[k] = lax.ppermute(message, ('trade', 'scen'), pairs)]
    ppermute x2, starting transfers between devices: 5.63 us -> 1.45 us  [shards(): lax.ppermute(partial_levels, 'scen', [(i, i ^ hop) for i in range(n_scen)])]
    pallas_call x1, Pallas kernels: 3.47 us -> 2.04 us  [shards(): pl.pallas_call(functools.partial(prepare_kernel, n_trade, n_scen, owned,...]
    pallas_call x2, Pallas kernels: 4.78 us -> 3.45 us  [shards(): pl.pallas_call(functools.partial(surface_kernel, k, owned, SURFACE_STEP),...]
    pallas_call x0 -> x1, Pallas kernels: none -> 1.11 us  [shards(): pl.pallas_call(functools.partial(shift_kernel, SHIFT_STEP), out_shape=plt...]
    ppermute x2, waiting for transfers between devices: 3.49 us -> 3.08 us  [shards(): lax.ppermute(partial_levels, 'scen', [(i, i ^ hop) for i in range(n_scen)])]
  transfers between devices with their start and end apart: 4 -> 4, of which waited for: 3 -> 3; matrix products, arithmetic and copies ran while one was open for 0% -> 0% of each run, Pallas kernels for 23% -> 21%
where the time goes in v4:
time: 23.5 us; the launch traced here: 23.2 us
  Pallas kernels  8.56 us (36%)
  waiting for transfers between devices  7.72 us (33%)
  starting transfers between devices  6.21 us (26%)
  between operations  0.7 us (3%)
    ppermute x2, starting transfers between devices, shards(): received[k] = lax.ppermute(message, ('trade', 'scen'), pairs)  4.76 us
    ppermute x2, waiting for transfers between devices, shards(): received[k] = lax.ppermute(message, ('trade', 'scen'), pairs)  4.65 us
    pallas_call x2, Pallas kernels, shards(): pl.pallas_call(functools.partial(surface_kernel, k, owned, SURFACE_STEP),...  3.45 us
    ppermute x2, waiting for transfers between devices, shards(): lax.ppermute(partial_levels, 'scen', [(i, i ^ hop) for i in range(n_scen)])  3.08 us
    pallas_call x1, Pallas kernels, shards(): pl.pallas_call(functools.partial(prepare_kernel, n_trade, n_scen, owned,...  2.04 us
    ppermute x2, starting transfers between devices, shards(): lax.ppermute(partial_levels, 'scen', [(i, i ^ hop) for i in range(n_scen)])  1.45 us
    pallas_call x1, Pallas kernels, shards(): pl.pallas_call(pack_kernel, out_shape=pltpu.VMEM((WIDE + EXTRA, BLOCKS *...  1.17 us
    pallas_call x1, Pallas kernels, shards(): pl.pallas_call(functools.partial(shift_kernel, SHIFT_STEP), out_shape=plt...  1.11 us
  transfers between devices with their start and end apart: 4, of which 3 were waited for; matrix products, arithmetic and copies ran while one was open for 0% of the time, Pallas kernels for 21%

profile of v4, /device:TPU:0, one launch (start us, length us, event | category | flops | bytes accessed | tf_op | source)
XLA Modules:
  0.0 23.2 jit_solution(5343702496323567522)
XLA Ops:
  0.6 1.2 %shard_map.148 = bf16[272,256]{1,0:T(8,128)(2,1)S(1)} custom-call(s32[2]{0:T(128)} %hot_in.1, f32[32,2048]{1,0:T(8,128)} %log_vol_in.1, f32[1,32]{1,0:T(1,128)} %bitcast.17), custom_call_target="tpu_custom_call" | custom-call | tf_op jit(solution)/shard_map/pallas_call | solution.py:364
  1.8 4.1 %collective-permute-start.1 = (bf16[272,256]{1,0:T(8,128)(2,1)S(1)}, bf16[272,256]{1,0:T(8,128)(2,1)S(1)}, u32[]{:S(2)}, u32[]{:S(2)}) collective-permute-start(bf16[272,256]{1,0:T(8,128)(2,1)S(1)} %shard_map.148), channel_id=1, source_target_pairs={{16,0},{21,1},{26,2},{31,3},{20,4},{17,5},{30,6},{27,7},{24,8},{29... | collective-permute-start | bytes 417800 | tf_op jit(solution)/shard_map/ppermute | solution.py:386
  5.9 0.7 %collective-permute-start = (bf16[272,256]{1,0:T(8,128)(2,1)S(1)}, bf16[272,256]{1,0:T(8,128)(2,1)S(1)}, u32[]{:S(2)}, u32[]{:S(2)}) collective-permute-start(bf16[272,256]{1,0:T(8,128)(2,1)S(1)} %shard_map.148), channel_id=1, source_target_pairs={{0,0},{5,1},{10,2},{15,3},{4,4},{1,5},{14,6},{11,7},{8,8},{13,9},{... | collective-permute-start | bytes 417800 | tf_op jit(solution)/shard_map/ppermute | solution.py:386
  6.6 2.0 %shard_map.149 = (f32[14,64,128]{2,1,0:T(8,128)S(1)}, f32[16,8192]{1,0:T(8,128)S(1)}, f32[32,8192]{1,0:T(8,128)S(1)}, bf16[64,64]{1,0:T(8,128)(2,1)S(1)}) custom-call(s32[2]{0:T(128)} %scen_in.1, bf16[512,2048]{1,0:T(8,128)(2,1)} %shock_ref.1, s32[64,128]{1,0:T(8,128)} %bitcast.9, s32[64,128]{1,0:T(8,128)} %bitcast.10, s32[64,128]{1,0:T(8,128)} %bitcast.11, ...), custom_call_target="tpu_custom_call" | custom-call | flops 40000000 | bytes 6000000 | tf_op jit(solution)/shard_map/pallas_call | solution.py:401
  8.6 4.6 %collective-permute-done.1.message_ref = bf16[272,256]{1,0:T(8,128)(2,1)S(1)} collective-permute-done((bf16[272,256]{1,0:T(8,128)(2,1)S(1)}, bf16[272,256]{1,0:T(8,128)(2,1)S(1)}, u32[]{:S(2)}, u32[]{:S(2)}) %collective-permute-start.1) | collective-permute-done | bytes 139296 | tf_op jit(solution)/shard_map/ppermute | solution.py:386
  13.3 1.7 %shard_map.150.refs_0_ = f32[128,128]{1,0:T(8,128)S(1)} custom-call(bf16[272,256]{1,0:T(8,128)(2,1)S(1)} %collective-permute-done.1.message_ref, f32[14,64,128]{2,1,0:T(8,128)S(1)} %get-tuple-element.9.pre_ref, f32[16,8192]{1,0:T(8,128)S(1)} %get-tuple-element.10.mix_ref, f32[32,8192]{1,0:T(8,128)S(1)} %get-tuple-element.11.coef_ref), custom_call_target="tpu_custom_call" | custom-call | tf_op jit(solution)/shard_map/pallas_call | solution.py:429
  15.0 0.0 collective-permute-done.message_ref
  15.0 1.7 %shard_map.151.after_ref = f32[128,128]{1,0:T(8,128)S(1)} custom-call(bf16[272,256]{1,0:T(8,128)(2,1)S(1)} %collective-permute-done.message_ref, f32[14,64,128]{2,1,0:T(8,128)S(1)} %get-tuple-element.9.pre_ref, f32[16,8192]{1,0:T(8,128)S(1)} %get-tuple-element.10.mix_ref, f32[32,8192]{1,0:T(8,128)S(1)} %get-tuple-element.11.coef_ref, ...), custom_call_target="tpu_custom_call" | custom-call | tf_op jit(solution)/shard_map/pallas_call | solution.py:429
  16.7 1.4 %collective-permute-start.2 = (f32[128,128]{1,0:T(8,128)S(1)}, f32[128,128]{1,0:T(8,128)S(1)}, u32[]{:S(2)}, u32[]{:S(2)}) collective-permute-start(f32[128,128]{1,0:T(8,128)S(1)} %shard_map.151.after_ref), channel_id=1, source_target_pairs={{0,2},{1,3},{2,0},{3,1},{4,6},{5,7},{6,4},{7,5},{8,10},{9,11},{10,... | collective-permute-start | bytes 196616 | tf_op jit(solution)/shard_map/ppermute | solution.py:457
  18.1 1.1 %shard_map.152.shift_ref = f32[2,64,128]{2,1,0:T(8,128)S(1)} custom-call(bf16[64,64]{1,0:T(8,128)(2,1)S(1)} %get-tuple-element.12.matrix_ref, f32[14,64,128]{2,1,0:T(8,128)S(1)} %get-tuple-element.9.pre_ref, f32[32,8192]{1,0:T(8,128)S(1)} %get-tuple-element.11.coef_ref, f32[128,128]{1,0:T(8,128)S(1)} %shard_map.151.after_ref), custom_call_target="tpu_custom_call" | custom-call | flops 40000000 | bytes 2000000 | tf_op jit(solution)/shard_map/pallas_call | solution.py:441
  19.2 1.8 %collective-permute-done.2 = f32[128,128]{1,0:T(8,128)S(1)} collective-permute-done((f32[128,128]{1,0:T(8,128)S(1)}, f32[128,128]{1,0:T(8,128)S(1)}, u32[]{:S(2)}, u32[]{:S(2)}) %collective-permute-start.2) | collective-permute-done | bytes 65568 | tf_op jit(solution)/shard_map/ppermute | solution.py:457
  21.1 0.1 collective-permute-start.3
  21.2 1.2 %collective-permute-done.3.rest_ref = f32[128,128]{1,0:T(8,128)S(1)} collective-permute-done((f32[128,128]{1,0:T(8,128)S(1)}, f32[128,128]{1,0:T(8,128)S(1)}, u32[]{:S(2)}, u32[]{:S(2)}) %collective-permute-start.3) | collective-permute-done | bytes 65568 | tf_op jit(solution)/shard_map/ppermute | solution.py:457
  22.4 0.8 %shard_map.153 = (f32[2,8192]{1,0:T(2,128)}, f32[2,8192]{1,0:T(2,128)}, f32[2,8192]{1,0:T(2,128)}) custom-call(f32[128,128]{1,0:T(8,128)S(1)} %add.3.part_ref, f32[128,128]{1,0:T(8,128)S(1)} %collective-permute-done.3.rest_ref, f32[2,64,128]{2,1,0:T(8,128)S(1)} %shard_map.152.shift_ref, f32[14,64,128]{2,1,0:T(8,128)S(1)} %get-tuple-element.9.pre_ref), custom_call_target="tpu_custom_call" | custom-call | tf_op jit(solution)/shard_map/pallas_call | solution.py:459
  (1 shorter events, 0.0 us)
Async XLA Ops:
  1.8 11.5 %collective-permute-start.1 = (bf16[272,256]{1,0:T(8,128)(2,1)S(1)}, bf16[272,256]{1,0:T(8,128)(2,1)S(1)}, u32[]{:S(2)}, u32[]{:S(2)}) collective-permute-start(bf16[272,256]{1,0:T(8,128)(2,1)S(1)} %shard_map.148), channel_id=1, source_target_pairs={{16,0},{21,1},{26,2},{31,3},{20,4},{17,5},{30,6},{27,7},{24,8},{29... | collective-permute-start | bytes 417800 | tf_op jit(solution)/shard_map/ppermute | solution.py:386
  5.9 9.1 %collective-permute-start = (bf16[272,256]{1,0:T(8,128)(2,1)S(1)}, bf16[272,256]{1,0:T(8,128)(2,1)S(1)}, u32[]{:S(2)}, u32[]{:S(2)}) collective-permute-start(bf16[272,256]{1,0:T(8,128)(2,1)S(1)} %shard_map.148), channel_id=1, source_target_pairs={{0,0},{5,1},{10,2},{15,3},{4,4},{1,5},{14,6},{11,7},{8,8},{13,9},{... | collective-permute-start | bytes 417800 | tf_op jit(solution)/shard_map/ppermute | solution.py:386
  16.7 4.3 %collective-permute-start.2 = (f32[128,128]{1,0:T(8,128)S(1)}, f32[128,128]{1,0:T(8,128)S(1)}, u32[]{:S(2)}, u32[]{:S(2)}) collective-permute-start(f32[128,128]{1,0:T(8,128)S(1)} %shard_map.151.after_ref), channel_id=1, source_target_pairs={{0,2},{1,3},{2,0},{3,1},{4,6},{5,7},{6,4},{7,5},{8,10},{9,11},{10,... | collective-permute-start | bytes 196616 | tf_op jit(solution)/shard_map/ppermute | solution.py:457
  21.1 1.3 %collective-permute-start.3 = (f32[128,128]{1,0:T(8,128)S(1)}, f32[128,128]{1,0:T(8,128)S(1)}, u32[]{:S(2)}, u32[]{:S(2)}) collective-permute-start(f32[128,128]{1,0:T(8,128)S(1)} %add.3.part_ref), channel_id=1, source_target_pairs={{0,1},{1,0},{2,3},{3,2},{4,5},{5,4},{6,7},{7,6},{8,9},{9,8},{10,11... | collective-permute-start | bytes 196616 | tf_op jit(solution)/shard_map/ppermute | solution.py:457

commit v5 on v4

--- a/solution.py
+++ b/solution.py
@@ -161,8 +161,10 @@
     step = jnp.where(hot < 0, 0, jnp.where(hot < HOT, device_count - 1, 1))
     owner = (dest + step) & (device_count - 1)
     offset = owner ^ lax.axis_index("trade")
-    mine = (offset & (n_scen - 1)) == lax.axis_index("scen")
-    slot = lax.shift_right_logical(offset, n_scen.bit_length() - 1)
+    scen_place = lax.axis_index("scen")
+    ring = lax.shift_right_logical(offset, n_scen.bit_length() - 1)
+    mine = ((offset & (n_scen - 1)) ^ ((ring & 1) * (n_scen // 2))) == scen_place
+    slot = ring ^ (scen_place & (device_count // n_scen - 1) & 1)
     out_ref[SLOT] = jnp.where(mine, slot, -1).astype(F32)
     out_ref[PICK] = jnp.where(hot < HOT, pick, pick - HOT).astype(F32)
 
@@ -378,11 +380,12 @@
 
     received = [None] * slots
     for k in reversed(range(slots)):
-        pairs = [
-            ((d ^ (q + k * n_scen)) * n_scen + q, d * n_scen + q)
-            for d in range(n_trade)
-            for q in range(n_scen)
-        ]
+        pairs = []
+        for d in range(n_trade):
+            for q in range(n_scen):
+                ring = k ^ (q & (slots - 1) & 1)
+                offset = ring * n_scen + (q ^ ((ring & 1) * (n_scen // 2)))
+                pairs.append(((d ^ offset) * n_scen + q, d * n_scen + q))
         received[k] = lax.ppermute(message, ("trade", "scen"), pairs)
 
     dense = [

time: 23.5 us -> 22.6 us (0.962)
  waiting for transfers between devices: 7.72 us -> 3.39 us
  starting transfers between devices: 6.21 us -> 9.64 us
    ppermute x2, waiting for transfers between devices: 4.65 us -> 0.42 us  [shards(): received[k] = lax.ppermute(message, ('trade', 'scen'), pairs)]
    ppermute x2, starting transfers between devices: 1.45 us -> 3.87 us  [shards(): lax.ppermute(partial_levels, 'scen', [(i, i ^ hop) for i in range(n_scen)])]
    ppermute x2, starting transfers between devices: 4.76 us -> 5.77 us  [shards(): received[k] = lax.ppermute(message, ('trade', 'scen'), pairs)]
  transfers between devices with their start and end apart: 4 -> 4, of which waited for: 3 -> 3; matrix products, arithmetic and copies ran while one was open for 0% -> 0% of each run, Pallas kernels for 21% -> 22%
where the time goes in v5:
time: 22.6 us; the launch traced here: 22.3 us
  starting transfers between devices  9.64 us (43%)
  Pallas kernels  8.56 us (38%)
  waiting for transfers between devices  3.39 us (15%)
  between operations  0.69 us (3%)
    ppermute x2, starting transfers between devices, shards(): received[k] = lax.ppermute(message, ('trade', 'scen'), pairs)  5.77 us
    ppermute x2, starting transfers between devices, shards(): lax.ppermute(partial_levels, 'scen', [(i, i ^ hop) for i in range(n_scen)])  3.87 us
    pallas_call x2, Pallas kernels, shards(): pl.pallas_call(functools.partial(surface_kernel, k, owned, SURFACE_STEP),...  3.45 us
    ppermute x2, waiting for transfers between devices, shards(): lax.ppermute(partial_levels, 'scen', [(i, i ^ hop) for i in range(n_scen)])  2.97 us
    pallas_call x1, Pallas kernels, shards(): pl.pallas_call(functools.partial(prepare_kernel, n_trade, n_scen, owned,...  2.04 us
    pallas_call x1, Pallas kernels, shards(): pl.pallas_call(pack_kernel, out_shape=pltpu.VMEM((WIDE + EXTRA, BLOCKS *...  1.17 us
    pallas_call x1, Pallas kernels, shards(): pl.pallas_call(functools.partial(shift_kernel, SHIFT_STEP), out_shape=plt...  1.11 us
    pallas_call x1, Pallas kernels, shards(): pl.pallas_call(value_kernel, out_shape=(jax.ShapeDtypeStruct((scenarios,...  0.8 us
  transfers between devices with their start and end apart: 4, of which 3 were waited for; matrix products, arithmetic and copies ran while one was open for 0% of the time, Pallas kernels for 22%

profile of v5, /device:TPU:0, one launch (start us, length us, event | category | flops | bytes accessed | tf_op | source)
XLA Modules:
  0.0 22.3 jit_solution(1048235213114891962)
XLA Ops:
  0.6 1.2 %shard_map.148 = bf16[272,256]{1,0:T(8,128)(2,1)S(1)} custom-call(s32[2]{0:T(128)} %hot_in.1, f32[32,2048]{1,0:T(8,128)} %log_vol_in.1, f32[1,32]{1,0:T(1,128)} %bitcast.17), custom_call_target="tpu_custom_call" | custom-call | tf_op jit(solution)/shard_map/pallas_call | solution.py:366
  1.8 5.1 %collective-permute-start.1 = (bf16[272,256]{1,0:T(8,128)(2,1)S(1)}, bf16[272,256]{1,0:T(8,128)(2,1)S(1)}, u32[]{:S(2)}, u32[]{:S(2)}) collective-permute-start(bf16[272,256]{1,0:T(8,128)(2,1)S(1)} %shard_map.148), channel_id=1, source_target_pairs={{24,0},{5,1},{18,2},{15,3},{28,4},{1,5},{22,6},{11,7},{16,8},{13,9... | collective-permute-start | bytes 417800 | tf_op jit(solution)/shard_map/ppermute | solution.py:389
  6.9 0.7 %collective-permute-start = (bf16[272,256]{1,0:T(8,128)(2,1)S(1)}, bf16[272,256]{1,0:T(8,128)(2,1)S(1)}, u32[]{:S(2)}, u32[]{:S(2)}) collective-permute-start(bf16[272,256]{1,0:T(8,128)(2,1)S(1)} %shard_map.148), channel_id=1, source_target_pairs={{0,0},{29,1},{10,2},{23,3},{4,4},{25,5},{14,6},{19,7},{8,8},{21,9}... | collective-permute-start | bytes 417800 | tf_op jit(solution)/shard_map/ppermute | solution.py:389
  7.6 2.0 %shard_map.149 = (f32[14,64,128]{2,1,0:T(8,128)S(1)}, f32[16,8192]{1,0:T(8,128)S(1)}, f32[32,8192]{1,0:T(8,128)S(1)}, bf16[64,64]{1,0:T(8,128)(2,1)S(1)}) custom-call(s32[2]{0:T(128)} %scen_in.1, bf16[512,2048]{1,0:T(8,128)(2,1)} %shock_ref.1, s32[64,128]{1,0:T(8,128)} %bitcast.9, s32[64,128]{1,0:T(8,128)} %bitcast.10, s32[64,128]{1,0:T(8,128)} %bitcast.11, ...), custom_call_target="tpu_custom_call" | custom-call | flops 40000000 | bytes 6000000 | tf_op jit(solution)/shard_map/pallas_call | solution.py:404
  9.6 0.4 %collective-permute-done.1.message_ref = bf16[272,256]{1,0:T(8,128)(2,1)S(1)} collective-permute-done((bf16[272,256]{1,0:T(8,128)(2,1)S(1)}, bf16[272,256]{1,0:T(8,128)(2,1)S(1)}, u32[]{:S(2)}, u32[]{:S(2)}) %collective-permute-start.1) | collective-permute-done | bytes 139296 | tf_op jit(solution)/shard_map/ppermute | solution.py:389
  10.1 1.7 %shard_map.150.refs_0_ = f32[128,128]{1,0:T(8,128)S(1)} custom-call(bf16[272,256]{1,0:T(8,128)(2,1)S(1)} %collective-permute-done.1.message_ref, f32[14,64,128]{2,1,0:T(8,128)S(1)} %get-tuple-element.9.pre_ref, f32[16,8192]{1,0:T(8,128)S(1)} %get-tuple-element.10.mix_ref, f32[32,8192]{1,0:T(8,128)S(1)} %get-tuple-element.11.coef_ref), custom_call_target="tpu_custom_call" | custom-call | tf_op jit(solution)/shard_map/pallas_call | solution.py:432
  11.8 0.0 collective-permute-done.message_ref
  11.8 1.7 %shard_map.151.after_ref = f32[128,128]{1,0:T(8,128)S(1)} custom-call(bf16[272,256]{1,0:T(8,128)(2,1)S(1)} %collective-permute-done.message_ref, f32[14,64,128]{2,1,0:T(8,128)S(1)} %get-tuple-element.9.pre_ref, f32[16,8192]{1,0:T(8,128)S(1)} %get-tuple-element.10.mix_ref, f32[32,8192]{1,0:T(8,128)S(1)} %get-tuple-element.11.coef_ref, ...), custom_call_target="tpu_custom_call" | custom-call | tf_op jit(solution)/shard_map/pallas_call | solution.py:432
  13.5 3.8 %collective-permute-start.2 = (f32[128,128]{1,0:T(8,128)S(1)}, f32[128,128]{1,0:T(8,128)S(1)}, u32[]{:S(2)}, u32[]{:S(2)}) collective-permute-start(f32[128,128]{1,0:T(8,128)S(1)} %shard_map.151.after_ref), channel_id=1, source_target_pairs={{0,2},{1,3},{2,0},{3,1},{4,6},{5,7},{6,4},{7,5},{8,10},{9,11},{10,... | collective-permute-start | bytes 196616 | tf_op jit(solution)/shard_map/ppermute | solution.py:460
  17.3 1.1 %shard_map.152.shift_ref = f32[2,64,128]{2,1,0:T(8,128)S(1)} custom-call(bf16[64,64]{1,0:T(8,128)(2,1)S(1)} %get-tuple-element.12.matrix_ref, f32[14,64,128]{2,1,0:T(8,128)S(1)} %get-tuple-element.9.pre_ref, f32[32,8192]{1,0:T(8,128)S(1)} %get-tuple-element.11.coef_ref, f32[128,128]{1,0:T(8,128)S(1)} %shard_map.151.after_ref), custom_call_target="tpu_custom_call" | custom-call | flops 40000000 | bytes 2000000 | tf_op jit(solution)/shard_map/pallas_call | solution.py:444
  18.4 1.7 %collective-permute-done.2 = f32[128,128]{1,0:T(8,128)S(1)} collective-permute-done((f32[128,128]{1,0:T(8,128)S(1)}, f32[128,128]{1,0:T(8,128)S(1)}, u32[]{:S(2)}, u32[]{:S(2)}) %collective-permute-start.2) | collective-permute-done | bytes 65568 | tf_op jit(solution)/shard_map/ppermute | solution.py:460
  20.2 0.1 collective-permute-start.3
  20.3 1.2 %collective-permute-done.3.rest_ref = f32[128,128]{1,0:T(8,128)S(1)} collective-permute-done((f32[128,128]{1,0:T(8,128)S(1)}, f32[128,128]{1,0:T(8,128)S(1)}, u32[]{:S(2)}, u32[]{:S(2)}) %collective-permute-start.3) | collective-permute-done | bytes 65568 | tf_op jit(solution)/shard_map/ppermute | solution.py:460
  21.5 0.8 %shard_map.153 = (f32[2,8192]{1,0:T(2,128)}, f32[2,8192]{1,0:T(2,128)}, f32[2,8192]{1,0:T(2,128)}) custom-call(f32[128,128]{1,0:T(8,128)S(1)} %add.3.part_ref, f32[128,128]{1,0:T(8,128)S(1)} %collective-permute-done.3.rest_ref, f32[2,64,128]{2,1,0:T(8,128)S(1)} %shard_map.152.shift_ref, f32[14,64,128]{2,1,0:T(8,128)S(1)} %get-tuple-element.9.pre_ref), custom_call_target="tpu_custom_call" | custom-call | tf_op jit(solution)/shard_map/pallas_call | solution.py:462
  (1 shorter events, 0.0 us)
Async XLA Ops:
  1.8 8.2 %collective-permute-start.1 = (bf16[272,256]{1,0:T(8,128)(2,1)S(1)}, bf16[272,256]{1,0:T(8,128)(2,1)S(1)}, u32[]{:S(2)}, u32[]{:S(2)}) collective-permute-start(bf16[272,256]{1,0:T(8,128)(2,1)S(1)} %shard_map.148), channel_id=1, source_target_pairs={{24,0},{5,1},{18,2},{15,3},{28,4},{1,5},{22,6},{11,7},{16,8},{13,9... | collective-permute-start | bytes 417800 | tf_op jit(solution)/shard_map/ppermute | solution.py:389
  6.9 4.9 %collective-permute-start = (bf16[272,256]{1,0:T(8,128)(2,1)S(1)}, bf16[272,256]{1,0:T(8,128)(2,1)S(1)}, u32[]{:S(2)}, u32[]{:S(2)}) collective-permute-start(bf16[272,256]{1,0:T(8,128)(2,1)S(1)} %shard_map.148), channel_id=1, source_target_pairs={{0,0},{29,1},{10,2},{23,3},{4,4},{25,5},{14,6},{19,7},{8,8},{21,9}... | collective-permute-start | bytes 417800 | tf_op jit(solution)/shard_map/ppermute | solution.py:389
  13.5 6.6 %collective-permute-start.2 = (f32[128,128]{1,0:T(8,128)S(1)}, f32[128,128]{1,0:T(8,128)S(1)}, u32[]{:S(2)}, u32[]{:S(2)}) collective-permute-start(f32[128,128]{1,0:T(8,128)S(1)} %shard_map.151.after_ref), channel_id=1, source_target_pairs={{0,2},{1,3},{2,0},{3,1},{4,6},{5,7},{6,4},{7,5},{8,10},{9,11},{10,... | collective-permute-start | bytes 196616 | tf_op jit(solution)/shard_map/ppermute | solution.py:460
  20.2 1.3 %collective-permute-start.3 = (f32[128,128]{1,0:T(8,128)S(1)}, f32[128,128]{1,0:T(8,128)S(1)}, u32[]{:S(2)}, u32[]{:S(2)}) collective-permute-start(f32[128,128]{1,0:T(8,128)S(1)} %add.3.part_ref), channel_id=1, source_target_pairs={{0,1},{1,0},{2,3},{3,2},{4,5},{5,4},{6,7},{7,6},{8,9},{9,8},{10,11... | collective-permute-start | bytes 196616 | tf_op jit(solution)/shard_map/ppermute | solution.py:460

commit v6 on v5

--- a/solution.py
+++ b/solution.py
@@ -243,9 +243,11 @@
 
 
 def surface_kernel(slot, owned, per_step, message_ref, pre_ref, mix_ref, coef_ref, *refs):
-    before_ref = refs[0] if len(refs) == 4 else None
-    out_ref, table_ref, index_ref = refs[-3:]
+    before_ref = refs[0] if len(refs) == 5 else None
+    out_ref, total_ref, table_ref, index_ref = refs[-4:]
     groups = pre_ref.shape[1]
+    if before_ref is not None:
+        total_ref[...] = before_ref[...].astype(F32)
     table_ref[0:WIDE, :] = message_ref[0:WIDE, :]
     table_ref[WIDE : WIDE + 3 * NK, :] = pltpu.roll(
         message_ref[0 : 3 * NK, :].astype(F32), (BLOCKS - 1) * owned, 1
@@ -268,8 +270,8 @@
         )
         index_ref[rows, :] = jnp.where(held, local, -1.0)
         later = pl.ds(groups + i * sub, sub)
-        other = 0.0 if before_ref is None else before_ref[later, :]
-        out_ref[later, :] = jnp.where(held, looked, other)
+        other = 0.0 if before_ref is None else total_ref[later, :]
+        total_ref[later, :] = jnp.where(held, looked, other)
 
     underlyings = lax.broadcasted_iota(jnp.int32, (owned, LANES), 0).astype(F32)
     zero = jnp.zeros((owned, LANES), BF16)
@@ -302,23 +304,26 @@
             for a in range(REACH):
                 curve = curve + product[a * NK : (a + 1) * NK, columns] * mix[a : a + 1, :]
             level = jnp.sum(curve * coef_ref[:, here], axis=0, keepdims=True)
-            level = level - pre_ref[BIAS, pl.ds(g, 1), :]
             held = index_ref[pl.ds(g, 1), :] >= 0.0
-            other = 0.0 if before_ref is None else before_ref[pl.ds(g, 1), :]
-            out_ref[pl.ds(g, 1), :] = jnp.where(held, level, other)
+            other = 0.0 if before_ref is None else total_ref[pl.ds(g, 1), :]
+            total_ref[pl.ds(g, 1), :] = jnp.where(held, level, other)
         return carry
 
     lax.fori_loop(0, groups // per_step, some, 0)
-
-
-def value_kernel(part_ref, rest_ref, shift_ref, pre_ref, price_ref, vega_ref, delta_ref):
+    out_ref[...] = total_ref[...].astype(BF16)
+
+
+def value_kernel(
+    part_ref, rest_ref, shift_ref, pre_ref, price_ref, vega_ref, delta_ref, total_ref
+):
+    total_ref[...] = part_ref[...].astype(F32) + rest_ref[...].astype(F32)
     scenarios, groups = shift_ref.shape[0], shift_ref.shape[1]
     sub = 8
     for i in range(groups // sub):
         rows = pl.ds(i * sub, sub)
         later = pl.ds(groups + i * sub, sub)
-        level = part_ref[rows, :] + rest_ref[rows, :]
-        slope = part_ref[later, :] + rest_ref[later, :]
+        level = total_ref[rows, :] - pre_ref[BIAS, rows, :]
+        slope = total_ref[later, :]
         root_time = pre_ref[ROOT, rows, :]
         moneyness = pre_ref[MONEY, rows, :]
         growth = pre_ref[GROWTH, rows, :]
@@ -431,10 +436,11 @@
         before = [] if partial_levels is None else [partial_levels]
         partial_levels = pl.pallas_call(
             functools.partial(surface_kernel, k, owned, SURFACE_STEP),
-            out_shape=jax.ShapeDtypeStruct((2 * groups, LANES), F32),
+            out_shape=jax.ShapeDtypeStruct((2 * groups, LANES), BF16),
             in_specs=[VMEM] * (4 + len(before)),
             out_specs=VMEM,
             scratch_shapes=[
+                pltpu.VMEM((2 * groups, LANES), F32),
                 pltpu.VMEM((WIDE + 3 * NK, BLOCKS * owned), BF16),
                 pltpu.VMEM((groups, LANES), F32),
             ],
@@ -464,6 +470,7 @@
         out_shape=(jax.ShapeDtypeStruct((scenarios, trades), F32),) * 3,
         in_specs=[VMEM] * 4,
         out_specs=(VMEM,) * 3,
+        scratch_shapes=[pltpu.VMEM((2 * groups, LANES), F32)],
         compiler_params=params(8192),
     )(partial_levels, rest, shift_level, prepared)
 

time: 22.6 us -> 22 us (0.973)
  waiting for transfers between devices: 3.39 us -> 2.64 us
    ppermute x2, waiting for transfers between devices: 2.97 us -> 2.22 us  [shards(): lax.ppermute(partial_levels, 'scen', [(i, i ^ hop) for i in range(n_scen)])]
  transfers between devices with their start and end apart: 4 -> 4, of which waited for: 3 -> 3; matrix products, arithmetic and copies ran while one was open for 0% -> 0% of each run, Pallas kernels for 22% -> 23%
where the time goes in v6:
time: 22 us; the launch traced here: 21.6 us
  starting transfers between devices  9.64 us (44%)
  Pallas kernels  8.57 us (39%)
  waiting for transfers between devices  2.64 us (12%)
  between operations  0.68 us (3%)
    ppermute x2, starting transfers between devices, shards(): received[k] = lax.ppermute(message, ('trade', 'scen'), pairs)  5.77 us
    ppermute x2, starting transfers between devices, shards(): lax.ppermute(partial_levels, 'scen', [(i, i ^ hop) for i in range(n_scen)])  3.87 us
    pallas_call x2, Pallas kernels, shards(): pl.pallas_call(functools.partial(surface_kernel, k, owned, SURFACE_STEP),...  3.45 us
    ppermute x2, waiting for transfers between devices, shards(): lax.ppermute(partial_levels, 'scen', [(i, i ^ hop) for i in range(n_scen)])  2.22 us
    pallas_call x1, Pallas kernels, shards(): pl.pallas_call(functools.partial(prepare_kernel, n_trade, n_scen, owned,...  2.04 us
    pallas_call x1, Pallas kernels, shards(): pl.pallas_call(pack_kernel, out_shape=pltpu.VMEM((WIDE + EXTRA, BLOCKS *...  1.17 us
    pallas_call x1, Pallas kernels, shards(): pl.pallas_call(functools.partial(shift_kernel, SHIFT_STEP), out_shape=plt...  1.11 us
    pallas_call x1, Pallas kernels, shards(): pl.pallas_call(value_kernel, out_shape=(jax.ShapeDtypeStruct((scenarios,...  0.8 us
  transfers between devices with their start and end apart: 4, of which 3 were waited for; matrix products, arithmetic and copies ran while one was open for 0% of the time, Pallas kernels for 23%

profile of v6, /device:TPU:0, one launch (start us, length us, event | category | flops | bytes accessed | tf_op | source)
XLA Modules:
  0.0 21.6 jit_solution(1614319956761014129)
XLA Ops:
  0.6 1.2 %shard_map.148 = bf16[272,256]{1,0:T(8,128)(2,1)S(1)} custom-call(s32[2]{0:T(128)} %hot_in.1, f32[32,2048]{1,0:T(8,128)} %log_vol_in.1, f32[1,32]{1,0:T(1,128)} %bitcast.17), custom_call_target="tpu_custom_call" | custom-call | tf_op jit(solution)/shard_map/pallas_call | solution.py:371
  1.8 5.1 %collective-permute-start.1 = (bf16[272,256]{1,0:T(8,128)(2,1)S(1)}, bf16[272,256]{1,0:T(8,128)(2,1)S(1)}, u32[]{:S(2)}, u32[]{:S(2)}) collective-permute-start(bf16[272,256]{1,0:T(8,128)(2,1)S(1)} %shard_map.148), channel_id=1, source_target_pairs={{24,0},{5,1},{18,2},{15,3},{28,4},{1,5},{22,6},{11,7},{16,8},{13,9... | collective-permute-start | bytes 417800 | tf_op jit(solution)/shard_map/ppermute | solution.py:394
  6.9 0.7 %collective-permute-start = (bf16[272,256]{1,0:T(8,128)(2,1)S(1)}, bf16[272,256]{1,0:T(8,128)(2,1)S(1)}, u32[]{:S(2)}, u32[]{:S(2)}) collective-permute-start(bf16[272,256]{1,0:T(8,128)(2,1)S(1)} %shard_map.148), channel_id=1, source_target_pairs={{0,0},{29,1},{10,2},{23,3},{4,4},{25,5},{14,6},{19,7},{8,8},{21,9}... | collective-permute-start | bytes 417800 | tf_op jit(solution)/shard_map/ppermute | solution.py:394
  7.6 2.0 %shard_map.149 = (f32[14,64,128]{2,1,0:T(8,128)S(1)}, f32[16,8192]{1,0:T(8,128)S(1)}, f32[32,8192]{1,0:T(8,128)S(1)}, bf16[64,64]{1,0:T(8,128)(2,1)S(1)}) custom-call(s32[2]{0:T(128)} %scen_in.1, bf16[512,2048]{1,0:T(8,128)(2,1)} %shock_ref.1, s32[64,128]{1,0:T(8,128)} %bitcast.9, s32[64,128]{1,0:T(8,128)} %bitcast.10, s32[64,128]{1,0:T(8,128)} %bitcast.11, ...), custom_call_target="tpu_custom_call" | custom-call | flops 40000000 | bytes 6000000 | tf_op jit(solution)/shard_map/pallas_call | solution.py:409
  9.6 0.4 %collective-permute-done.1.message_ref = bf16[272,256]{1,0:T(8,128)(2,1)S(1)} collective-permute-done((bf16[272,256]{1,0:T(8,128)(2,1)S(1)}, bf16[272,256]{1,0:T(8,128)(2,1)S(1)}, u32[]{:S(2)}, u32[]{:S(2)}) %collective-permute-start.1) | collective-permute-done | bytes 139296 | tf_op jit(solution)/shard_map/ppermute | solution.py:394
  10.1 1.7 %shard_map.150.refs_0_ = bf16[128,128]{1,0:T(8,128)(2,1)S(1)} custom-call(bf16[272,256]{1,0:T(8,128)(2,1)S(1)} %collective-permute-done.1.message_ref, f32[14,64,128]{2,1,0:T(8,128)S(1)} %get-tuple-element.9.pre_ref, f32[16,8192]{1,0:T(8,128)S(1)} %get-tuple-element.10.mix_ref, f32[32,8192]{1,0:T(8,128)S(1)} %get-tuple-element.11.coef_ref), custom_call_target="tpu_custom_call" | custom-call | tf_op jit(solution)/shard_map/pallas_call | solution.py:437
  11.8 0.0 collective-permute-done.message_ref
  11.8 1.7 %shard_map.151.after_ref = bf16[128,128]{1,0:T(8,128)(2,1)S(1)} custom-call(bf16[272,256]{1,0:T(8,128)(2,1)S(1)} %collective-permute-done.message_ref, f32[14,64,128]{2,1,0:T(8,128)S(1)} %get-tuple-element.9.pre_ref, f32[16,8192]{1,0:T(8,128)S(1)} %get-tuple-element.10.mix_ref, f32[32,8192]{1,0:T(8,128)S(1)} %get-tuple-element.11.coef_ref, ...), custom_call_target="tpu_custom_call" | custom-call | tf_op jit(solution)/shard_map/pallas_call | solution.py:437
  13.5 3.8 %collective-permute-start.2 = (bf16[128,128]{1,0:T(8,128)(2,1)S(1)}, bf16[128,128]{1,0:T(8,128)(2,1)S(1)}, u32[]{:S(2)}, u32[]{:S(2)}) collective-permute-start(bf16[128,128]{1,0:T(8,128)(2,1)S(1)} %shard_map.151.after_ref), channel_id=1, source_target_pairs={{0,2},{1,3},{2,0},{3,1},{4,6},{5,7},{6,4},{7,5},{8,10},{9,11},{10,... | collective-permute-start | bytes 98312 | tf_op jit(solution)/shard_map/ppermute | solution.py:466
  17.3 1.1 %shard_map.152.shift_ref = f32[2,64,128]{2,1,0:T(8,128)S(1)} custom-call(bf16[64,64]{1,0:T(8,128)(2,1)S(1)} %get-tuple-element.12.matrix_ref, f32[14,64,128]{2,1,0:T(8,128)S(1)} %get-tuple-element.9.pre_ref, f32[32,8192]{1,0:T(8,128)S(1)} %get-tuple-element.11.coef_ref, bf16[128,128]{1,0:T(8,128)(2,1)S(1)} %shard_map.151.after_ref), custom_call_target="tpu_custom_call" | custom-call | flops 40000000 | bytes 2000000 | tf_op jit(solution)/shard_map/pallas_call | solution.py:450
  18.4 1.0 %collective-permute-done.2 = bf16[128,128]{1,0:T(8,128)(2,1)S(1)} collective-permute-done((bf16[128,128]{1,0:T(8,128)(2,1)S(1)}, bf16[128,128]{1,0:T(8,128)(2,1)S(1)}, u32[]{:S(2)}, u32[]{:S(2)}) %collective-permute-start.2) | collective-permute-done | bytes 32800 | tf_op jit(solution)/shard_map/ppermute | solution.py:466
  19.5 0.1 collective-permute-start.3
  19.6 1.2 %collective-permute-done.3.rest_ref = bf16[128,128]{1,0:T(8,128)(2,1)S(1)} collective-permute-done((bf16[128,128]{1,0:T(8,128)(2,1)S(1)}, bf16[128,128]{1,0:T(8,128)(2,1)S(1)}, u32[]{:S(2)}, u32[]{:S(2)}) %collective-permute-start.3) | collective-permute-done | bytes 32800 | tf_op jit(solution)/shard_map/ppermute | solution.py:466
  20.8 0.8 %shard_map.153 = (f32[2,8192]{1,0:T(2,128)}, f32[2,8192]{1,0:T(2,128)}, f32[2,8192]{1,0:T(2,128)}) custom-call(bf16[128,128]{1,0:T(8,128)(2,1)S(1)} %add.3.part_ref, bf16[128,128]{1,0:T(8,128)(2,1)S(1)} %collective-permute-done.3.rest_ref, f32[2,64,128]{2,1,0:T(8,128)S(1)} %shard_map.152.shift_ref, f32[14,64,128]{2,1,0:T(8,128)S(1)} %get-tuple-element.9.pre_ref), custom_call_target="tpu_custom_call" | custom-call | tf_op jit(solution)/shard_map/pallas_call | solution.py:468
  (1 shorter events, 0.0 us)
Async XLA Ops:
  1.8 8.2 %collective-permute-start.1 = (bf16[272,256]{1,0:T(8,128)(2,1)S(1)}, bf16[272,256]{1,0:T(8,128)(2,1)S(1)}, u32[]{:S(2)}, u32[]{:S(2)}) collective-permute-start(bf16[272,256]{1,0:T(8,128)(2,1)S(1)} %shard_map.148), channel_id=1, source_target_pairs={{24,0},{5,1},{18,2},{15,3},{28,4},{1,5},{22,6},{11,7},{16,8},{13,9... | collective-permute-start | bytes 417800 | tf_op jit(solution)/shard_map/ppermute | solution.py:394
  6.9 4.9 %collective-permute-start = (bf16[272,256]{1,0:T(8,128)(2,1)S(1)}, bf16[272,256]{1,0:T(8,128)(2,1)S(1)}, u32[]{:S(2)}, u32[]{:S(2)}) collective-permute-start(bf16[272,256]{1,0:T(8,128)(2,1)S(1)} %shard_map.148), channel_id=1, source_target_pairs={{0,0},{29,1},{10,2},{23,3},{4,4},{25,5},{14,6},{19,7},{8,8},{21,9}... | collective-permute-start | bytes 417800 | tf_op jit(solution)/shard_map/ppermute | solution.py:394
  13.5 5.9 %collective-permute-start.2 = (bf16[128,128]{1,0:T(8,128)(2,1)S(1)}, bf16[128,128]{1,0:T(8,128)(2,1)S(1)}, u32[]{:S(2)}, u32[]{:S(2)}) collective-permute-start(bf16[128,128]{1,0:T(8,128)(2,1)S(1)} %shard_map.151.after_ref), channel_id=1, source_target_pairs={{0,2},{1,3},{2,0},{3,1},{4,6},{5,7},{6,4},{7,5},{8,10},{9,11},{10,... | collective-permute-start | bytes 98312 | tf_op jit(solution)/shard_map/ppermute | solution.py:466
  19.5 1.3 %collective-permute-start.3 = (bf16[128,128]{1,0:T(8,128)(2,1)S(1)}, bf16[128,128]{1,0:T(8,128)(2,1)S(1)}, u32[]{:S(2)}, u32[]{:S(2)}) collective-permute-start(bf16[128,128]{1,0:T(8,128)(2,1)S(1)} %add.3.part_ref), channel_id=1, source_target_pairs={{0,1},{1,0},{2,3},{3,2},{4,5},{5,4},{6,7},{7,6},{8,9},{9,8},{10,11... | collective-permute-start | bytes 98312 | tf_op jit(solution)/shard_map/ppermute | solution.py:466

commit v7 on v6

--- a/solution.py
+++ b/solution.py
@@ -457,14 +457,12 @@
     )(matrix, prepared, coefs, partial_levels)
 
     rest = jnp.zeros_like(partial_levels) if n_scen == 1 else None
-    hop = n_scen // 2
-    while hop:
+    hop = 1
+    while hop < n_scen:
         if rest is not None:
-            partial_levels, shift_level = lax.optimization_barrier(
-                (partial_levels + rest, shift_level)
-            )
+            partial_levels = partial_levels + rest
         rest = lax.ppermute(partial_levels, "scen", [(i, i ^ hop) for i in range(n_scen)])
-        hop //= 2
+        hop *= 2
     return pl.pallas_call(
         value_kernel,
         out_shape=(jax.ShapeDtypeStruct((scenarios, trades), F32),) * 3,

time: 22 us -> 21.8 us (level)
  waiting for transfers between devices: 2.64 us -> 2.07 us
  starting transfers between devices: 9.64 us -> 10.2 us
    ppermute x2, starting transfers between devices: 3.87 us -> 4.45 us  [shards(): lax.ppermute(partial_levels, 'scen', [(i, i ^ hop) for i in range(n_scen)])]
    ppermute x2, waiting for transfers between devices: 2.22 us -> 1.64 us  [shards(): lax.ppermute(partial_levels, 'scen', [(i, i ^ hop) for i in range(n_scen)])]
where the time goes in v7:
time: 21.8 us; the launch traced here: 21.6 us
  starting transfers between devices  10.2 us (47%)
  Pallas kernels  8.57 us (39%)
  waiting for transfers between devices  2.07 us (9%)
  between operations  0.68 us (3%)
    ppermute x2, starting transfers between devices, shards(): received[k] = lax.ppermute(message, ('trade', 'scen'), pairs)  5.77 us
    ppermute x2, starting transfers between devices, shards(): lax.ppermute(partial_levels, 'scen', [(i, i ^ hop) for i in range(n_scen)])  4.45 us
    pallas_call x2, Pallas kernels, shards(): pl.pallas_call(functools.partial(surface_kernel, k, owned, SURFACE_STEP),...  3.45 us
    pallas_call x1, Pallas kernels, shards(): pl.pallas_call(functools.partial(prepare_kernel, n_trade, n_scen, owned,...  2.04 us
    ppermute x2, waiting for transfers between devices, shards(): lax.ppermute(partial_levels, 'scen', [(i, i ^ hop) for i in range(n_scen)])  1.64 us
    pallas_call x1, Pallas kernels, shards(): pl.pallas_call(pack_kernel, out_shape=pltpu.VMEM((WIDE + EXTRA, BLOCKS *...  1.17 us
    pallas_call x1, Pallas kernels, shards(): pl.pallas_call(functools.partial(shift_kernel, SHIFT_STEP), out_shape=plt...  1.11 us
    pallas_call x1, Pallas kernels, shards(): pl.pallas_call(value_kernel, out_shape=(jax.ShapeDtypeStruct((scenarios,...  0.8 us
  transfers between devices with their start and end apart: 4, of which 3 were waited for; matrix products, arithmetic and copies ran while one was open for 0% of the time, Pallas kernels for 23%

profile of v7, /device:TPU:0, one launch (start us, length us, event | category | flops | bytes accessed | tf_op | source)
XLA Modules:
  0.0 21.6 jit_solution(11910925346124557261)
XLA Ops:
  0.6 1.2 %shard_map.148 = bf16[272,256]{1,0:T(8,128)(2,1)S(1)} custom-call(s32[2]{0:T(128)} %hot_in.1, f32[32,2048]{1,0:T(8,128)} %log_vol_in.1, f32[1,32]{1,0:T(1,128)} %bitcast.17), custom_call_target="tpu_custom_call" | custom-call | tf_op jit(solution)/shard_map/pallas_call | solution.py:371
  1.8 5.1 %collective-permute-start.1 = (bf16[272,256]{1,0:T(8,128)(2,1)S(1)}, bf16[272,256]{1,0:T(8,128)(2,1)S(1)}, u32[]{:S(2)}, u32[]{:S(2)}) collective-permute-start(bf16[272,256]{1,0:T(8,128)(2,1)S(1)} %shard_map.148), channel_id=1, source_target_pairs={{24,0},{5,1},{18,2},{15,3},{28,4},{1,5},{22,6},{11,7},{16,8},{13,9... | collective-permute-start | bytes 417800 | tf_op jit(solution)/shard_map/ppermute | solution.py:394
  6.9 0.7 %collective-permute-start = (bf16[272,256]{1,0:T(8,128)(2,1)S(1)}, bf16[272,256]{1,0:T(8,128)(2,1)S(1)}, u32[]{:S(2)}, u32[]{:S(2)}) collective-permute-start(bf16[272,256]{1,0:T(8,128)(2,1)S(1)} %shard_map.148), channel_id=1, source_target_pairs={{0,0},{29,1},{10,2},{23,3},{4,4},{25,5},{14,6},{19,7},{8,8},{21,9}... | collective-permute-start | bytes 417800 | tf_op jit(solution)/shard_map/ppermute | solution.py:394
  7.6 2.0 %shard_map.149 = (f32[14,64,128]{2,1,0:T(8,128)S(1)}, f32[16,8192]{1,0:T(8,128)S(1)}, f32[32,8192]{1,0:T(8,128)S(1)}, bf16[64,64]{1,0:T(8,128)(2,1)S(1)}) custom-call(s32[2]{0:T(128)} %scen_in.1, bf16[512,2048]{1,0:T(8,128)(2,1)} %shock_ref.1, s32[64,128]{1,0:T(8,128)} %bitcast.9, s32[64,128]{1,0:T(8,128)} %bitcast.10, s32[64,128]{1,0:T(8,128)} %bitcast.11, ...), custom_call_target="tpu_custom_call" | custom-call | flops 40000000 | bytes 6000000 | tf_op jit(solution)/shard_map/pallas_call | solution.py:409
  9.6 0.4 %collective-permute-done.1.message_ref = bf16[272,256]{1,0:T(8,128)(2,1)S(1)} collective-permute-done((bf16[272,256]{1,0:T(8,128)(2,1)S(1)}, bf16[272,256]{1,0:T(8,128)(2,1)S(1)}, u32[]{:S(2)}, u32[]{:S(2)}) %collective-permute-start.1) | collective-permute-done | bytes 139296 | tf_op jit(solution)/shard_map/ppermute | solution.py:394
  10.1 1.7 %shard_map.150.refs_0_ = bf16[128,128]{1,0:T(8,128)(2,1)S(1)} custom-call(bf16[272,256]{1,0:T(8,128)(2,1)S(1)} %collective-permute-done.1.message_ref, f32[14,64,128]{2,1,0:T(8,128)S(1)} %get-tuple-element.7.pre_ref, f32[16,8192]{1,0:T(8,128)S(1)} %get-tuple-element.8.mix_ref, f32[32,8192]{1,0:T(8,128)S(1)} %get-tuple-element.9.coef_ref), custom_call_target="tpu_custom_call" | custom-call | tf_op jit(solution)/shard_map/pallas_call | solution.py:437
  11.8 0.0 collective-permute-done.message_ref
  11.8 1.7 %shard_map.151.after_ref = bf16[128,128]{1,0:T(8,128)(2,1)S(1)} custom-call(bf16[272,256]{1,0:T(8,128)(2,1)S(1)} %collective-permute-done.message_ref, f32[14,64,128]{2,1,0:T(8,128)S(1)} %get-tuple-element.7.pre_ref, f32[16,8192]{1,0:T(8,128)S(1)} %get-tuple-element.8.mix_ref, f32[32,8192]{1,0:T(8,128)S(1)} %get-tuple-element.9.coef_ref, ...), custom_call_target="tpu_custom_call" | custom-call | tf_op jit(solution)/shard_map/pallas_call | solution.py:437
  13.5 1.6 %collective-permute-start.2 = (bf16[128,128]{1,0:T(8,128)(2,1)S(1)}, bf16[128,128]{1,0:T(8,128)(2,1)S(1)}, u32[]{:S(2)}, u32[]{:S(2)}) collective-permute-start(bf16[128,128]{1,0:T(8,128)(2,1)S(1)} %shard_map.151.after_ref), channel_id=1, source_target_pairs={{0,1},{1,0},{2,3},{3,2},{4,5},{5,4},{6,7},{7,6},{8,9},{9,8},{10,11... | collective-permute-start | bytes 98312 | tf_op jit(solution)/shard_map/ppermute | solution.py:464
  15.2 0.9 %collective-permute-done.2 = bf16[128,128]{1,0:T(8,128)(2,1)S(1)} collective-permute-done((bf16[128,128]{1,0:T(8,128)(2,1)S(1)}, bf16[128,128]{1,0:T(8,128)(2,1)S(1)}, u32[]{:S(2)}, u32[]{:S(2)}) %collective-permute-start.2) | collective-permute-done | bytes 32800 | tf_op jit(solution)/shard_map/ppermute | solution.py:464
  16.0 2.8 %collective-permute-start.3 = (bf16[128,128]{1,0:T(8,128)(2,1)S(1)}, bf16[128,128]{1,0:T(8,128)(2,1)S(1)}, u32[]{:S(2)}, u32[]{:S(2)}) collective-permute-start(bf16[128,128]{1,0:T(8,128)(2,1)S(1)} %add.3.part_ref), channel_id=1, source_target_pairs={{0,2},{1,3},{2,0},{3,1},{4,6},{5,7},{6,4},{7,5},{8,10},{9,11},{10,... | collective-permute-start | bytes 98312 | tf_op jit(solution)/shard_map/ppermute | solution.py:464
  18.8 1.1 %shard_map.152.shift_ref = f32[2,64,128]{2,1,0:T(8,128)S(1)} custom-call(bf16[64,64]{1,0:T(8,128)(2,1)S(1)} %get-tuple-element.10.matrix_ref, f32[14,64,128]{2,1,0:T(8,128)S(1)} %get-tuple-element.7.pre_ref, f32[32,8192]{1,0:T(8,128)S(1)} %get-tuple-element.9.coef_ref, bf16[128,128]{1,0:T(8,128)(2,1)S(1)} %shard_map.151.after_ref), custom_call_target="tpu_custom_call" | custom-call | flops 40000000 | bytes 2000000 | tf_op jit(solution)/shard_map/pallas_call | solution.py:450
  20.0 0.8 %collective-permute-done.3.rest_ref = bf16[128,128]{1,0:T(8,128)(2,1)S(1)} collective-permute-done((bf16[128,128]{1,0:T(8,128)(2,1)S(1)}, bf16[128,128]{1,0:T(8,128)(2,1)S(1)}, u32[]{:S(2)}, u32[]{:S(2)}) %collective-permute-start.3) | collective-permute-done | bytes 32800 | tf_op jit(solution)/shard_map/ppermute | solution.py:464
  20.8 0.8 %shard_map.153 = (f32[2,8192]{1,0:T(2,128)}, f32[2,8192]{1,0:T(2,128)}, f32[2,8192]{1,0:T(2,128)}) custom-call(bf16[128,128]{1,0:T(8,128)(2,1)S(1)} %add.3.part_ref, bf16[128,128]{1,0:T(8,128)(2,1)S(1)} %collective-permute-done.3.rest_ref, f32[2,64,128]{2,1,0:T(8,128)S(1)} %shard_map.152.shift_ref, f32[14,64,128]{2,1,0:T(8,128)S(1)} %get-tuple-element.7.pre_ref), custom_call_target="tpu_custom_call" | custom-call | tf_op jit(solution)/shard_map/pallas_call | solution.py:466
  (1 shorter events, 0.0 us)
Async XLA Ops:
  1.8 8.2 %collective-permute-start.1 = (bf16[272,256]{1,0:T(8,128)(2,1)S(1)}, bf16[272,256]{1,0:T(8,128)(2,1)S(1)}, u32[]{:S(2)}, u32[]{:S(2)}) collective-permute-start(bf16[272,256]{1,0:T(8,128)(2,1)S(1)} %shard_map.148), channel_id=1, source_target_pairs={{24,0},{5,1},{18,2},{15,3},{28,4},{1,5},{22,6},{11,7},{16,8},{13,9... | collective-permute-start | bytes 417800 | tf_op jit(solution)/shard_map/ppermute | solution.py:394
  6.9 4.9 %collective-permute-start = (bf16[272,256]{1,0:T(8,128)(2,1)S(1)}, bf16[272,256]{1,0:T(8,128)(2,1)S(1)}, u32[]{:S(2)}, u32[]{:S(2)}) collective-permute-start(bf16[272,256]{1,0:T(8,128)(2,1)S(1)} %shard_map.148), channel_id=1, source_target_pairs={{0,0},{29,1},{10,2},{23,3},{4,4},{25,5},{14,6},{19,7},{8,8},{21,9}... | collective-permute-start | bytes 417800 | tf_op jit(solution)/shard_map/ppermute | solution.py:394
  13.5 2.5 %collective-permute-start.2 = (bf16[128,128]{1,0:T(8,128)(2,1)S(1)}, bf16[128,128]{1,0:T(8,128)(2,1)S(1)}, u32[]{:S(2)}, u32[]{:S(2)}) collective-permute-start(bf16[128,128]{1,0:T(8,128)(2,1)S(1)} %shard_map.151.after_ref), channel_id=1, source_target_pairs={{0,1},{1,0},{2,3},{3,2},{4,5},{5,4},{6,7},{7,6},{8,9},{9,8},{10,11... | collective-permute-start | bytes 98312 | tf_op jit(solution)/shard_map/ppermute | solution.py:464
  16.0 4.7 %collective-permute-start.3 = (bf16[128,128]{1,0:T(8,128)(2,1)S(1)}, bf16[128,128]{1,0:T(8,128)(2,1)S(1)}, u32[]{:S(2)}, u32[]{:S(2)}) collective-permute-start(bf16[128,128]{1,0:T(8,128)(2,1)S(1)} %add.3.part_ref), channel_id=1, source_target_pairs={{0,2},{1,3},{2,0},{3,1},{4,6},{5,7},{6,4},{7,5},{8,10},{9,11},{10,... | collective-permute-start | bytes 98312 | tf_op jit(solution)/shard_map/ppermute | solution.py:464

commit v8 on v7

--- a/solution.py
+++ b/solution.py
@@ -108,6 +108,10 @@
     return result
 
 
+def parity(value, count):
+    return sum((value >> i) & 1 for i in range(count.bit_length() - 1)) & 1
+
+
 def prepare_kernel(
     device_count,
     n_scen,
@@ -164,7 +168,7 @@
     scen_place = lax.axis_index("scen")
     ring = lax.shift_right_logical(offset, n_scen.bit_length() - 1)
     mine = ((offset & (n_scen - 1)) ^ ((ring & 1) * (n_scen // 2))) == scen_place
-    slot = ring ^ (scen_place & (device_count // n_scen - 1) & 1)
+    slot = ring ^ (parity(scen_place, n_scen) & (device_count // n_scen - 1))
     out_ref[SLOT] = jnp.where(mine, slot, -1).astype(F32)
     out_ref[PICK] = jnp.where(hot < HOT, pick, pick - HOT).astype(F32)
 
@@ -388,7 +392,7 @@
         pairs = []
         for d in range(n_trade):
             for q in range(n_scen):
-                ring = k ^ (q & (slots - 1) & 1)
+                ring = k ^ (parity(q, n_scen) & (slots - 1))
                 offset = ring * n_scen + (q ^ ((ring & 1) * (n_scen // 2)))
                 pairs.append(((d ^ offset) * n_scen + q, d * n_scen + q))
         received[k] = lax.ppermute(message, ("trade", "scen"), pairs)

time: 21.8 us -> 21.3 us (0.977)
  starting transfers between devices: 10.2 us -> 9.7 us
    ppermute x2, starting transfers between devices: 4.45 us -> 3.92 us  [shards(): lax.ppermute(partial_levels, 'scen', [(i, i ^ hop) for i in range(n_scen)])]
where the time goes in v8:
time: 21.3 us; the launch traced here: 21 us
  starting transfers between devices  9.7 us (46%)
  Pallas kernels  8.57 us (40%)
  waiting for transfers between devices  2.07 us (10%)
  between operations  0.68 us (3%)
    ppermute x2, starting transfers between devices, shards(): received[k] = lax.ppermute(message, ('trade', 'scen'), pairs)  5.77 us
    ppermute x2, starting transfers between devices, shards(): lax.ppermute(partial_levels, 'scen', [(i, i ^ hop) for i in range(n_scen)])  3.92 us
    pallas_call x2, Pallas kernels, shards(): pl.pallas_call(functools.partial(surface_kernel, k, owned, SURFACE_STEP),...  3.45 us
    pallas_call x1, Pallas kernels, shards(): pl.pallas_call(functools.partial(prepare_kernel, n_trade, n_scen, owned,...  2.04 us
    ppermute x2, waiting for transfers between devices, shards(): lax.ppermute(partial_levels, 'scen', [(i, i ^ hop) for i in range(n_scen)])  1.64 us
    pallas_call x1, Pallas kernels, shards(): pl.pallas_call(pack_kernel, out_shape=pltpu.VMEM((WIDE + EXTRA, BLOCKS *...  1.17 us
    pallas_call x1, Pallas kernels, shards(): pl.pallas_call(functools.partial(shift_kernel, SHIFT_STEP), out_shape=plt...  1.11 us
    pallas_call x1, Pallas kernels, shards(): pl.pallas_call(value_kernel, out_shape=(jax.ShapeDtypeStruct((scenarios,...  0.8 us
  transfers between devices with their start and end apart: 4, of which 3 were waited for; matrix products, arithmetic and copies ran while one was open for 0% of the time, Pallas kernels for 23%

profile of v8, /device:TPU:0, one launch (start us, length us, event | category | flops | bytes accessed | tf_op | source)
XLA Modules:
  0.0 21.0 jit_solution(7289936938742699821)
XLA Ops:
  0.6 1.2 %shard_map.148 = bf16[272,256]{1,0:T(8,128)(2,1)S(1)} custom-call(s32[2]{0:T(128)} %hot_in.1, f32[32,2048]{1,0:T(8,128)} %log_vol_in.1, f32[1,32]{1,0:T(1,128)} %bitcast.17), custom_call_target="tpu_custom_call" | custom-call | tf_op jit(solution)/shard_map/pallas_call | solution.py:375
  1.8 5.1 %collective-permute-start.1 = (bf16[272,256]{1,0:T(8,128)(2,1)S(1)}, bf16[272,256]{1,0:T(8,128)(2,1)S(1)}, u32[]{:S(2)}, u32[]{:S(2)}) collective-permute-start(bf16[272,256]{1,0:T(8,128)(2,1)S(1)} %shard_map.148), channel_id=1, source_target_pairs={{24,0},{5,1},{10,2},{23,3},{28,4},{1,5},{14,6},{19,7},{16,8},{13,9... | collective-permute-start | bytes 417800 | tf_op jit(solution)/shard_map/ppermute | solution.py:398
  6.9 0.7 %collective-permute-start = (bf16[272,256]{1,0:T(8,128)(2,1)S(1)}, bf16[272,256]{1,0:T(8,128)(2,1)S(1)}, u32[]{:S(2)}, u32[]{:S(2)}) collective-permute-start(bf16[272,256]{1,0:T(8,128)(2,1)S(1)} %shard_map.148), channel_id=1, source_target_pairs={{0,0},{29,1},{18,2},{15,3},{4,4},{25,5},{22,6},{11,7},{8,8},{21,9}... | collective-permute-start | bytes 417800 | tf_op jit(solution)/shard_map/ppermute | solution.py:398
  7.6 2.0 %shard_map.149 = (f32[14,64,128]{2,1,0:T(8,128)S(1)}, f32[16,8192]{1,0:T(8,128)S(1)}, f32[32,8192]{1,0:T(8,128)S(1)}, bf16[64,64]{1,0:T(8,128)(2,1)S(1)}) custom-call(s32[2]{0:T(128)} %scen_in.1, bf16[512,2048]{1,0:T(8,128)(2,1)} %shock_ref.1, s32[64,128]{1,0:T(8,128)} %bitcast.9, s32[64,128]{1,0:T(8,128)} %bitcast.10, s32[64,128]{1,0:T(8,128)} %bitcast.11, ...), custom_call_target="tpu_custom_call" | custom-call | flops 40000000 | bytes 6000000 | tf_op jit(solution)/shard_map/pallas_call | solution.py:413
  9.6 0.4 %collective-permute-done.1.message_ref = bf16[272,256]{1,0:T(8,128)(2,1)S(1)} collective-permute-done((bf16[272,256]{1,0:T(8,128)(2,1)S(1)}, bf16[272,256]{1,0:T(8,128)(2,1)S(1)}, u32[]{:S(2)}, u32[]{:S(2)}) %collective-permute-start.1) | collective-permute-done | bytes 139296 | tf_op jit(solution)/shard_map/ppermute | solution.py:398
  10.1 1.7 %shard_map.150.refs_0_ = bf16[128,128]{1,0:T(8,128)(2,1)S(1)} custom-call(bf16[272,256]{1,0:T(8,128)(2,1)S(1)} %collective-permute-done.1.message_ref, f32[14,64,128]{2,1,0:T(8,128)S(1)} %get-tuple-element.7.pre_ref, f32[16,8192]{1,0:T(8,128)S(1)} %get-tuple-element.8.mix_ref, f32[32,8192]{1,0:T(8,128)S(1)} %get-tuple-element.9.coef_ref), custom_call_target="tpu_custom_call" | custom-call | tf_op jit(solution)/shard_map/pallas_call | solution.py:441
  11.8 0.0 collective-permute-done.message_ref
  11.8 1.7 %shard_map.151.after_ref = bf16[128,128]{1,0:T(8,128)(2,1)S(1)} custom-call(bf16[272,256]{1,0:T(8,128)(2,1)S(1)} %collective-permute-done.message_ref, f32[14,64,128]{2,1,0:T(8,128)S(1)} %get-tuple-element.7.pre_ref, f32[16,8192]{1,0:T(8,128)S(1)} %get-tuple-element.8.mix_ref, f32[32,8192]{1,0:T(8,128)S(1)} %get-tuple-element.9.coef_ref, ...), custom_call_target="tpu_custom_call" | custom-call | tf_op jit(solution)/shard_map/pallas_call | solution.py:441
  13.5 1.6 %collective-permute-start.2 = (bf16[128,128]{1,0:T(8,128)(2,1)S(1)}, bf16[128,128]{1,0:T(8,128)(2,1)S(1)}, u32[]{:S(2)}, u32[]{:S(2)}) collective-permute-start(bf16[128,128]{1,0:T(8,128)(2,1)S(1)} %shard_map.151.after_ref), channel_id=1, source_target_pairs={{0,1},{1,0},{2,3},{3,2},{4,5},{5,4},{6,7},{7,6},{8,9},{9,8},{10,11... | collective-permute-start | bytes 98312 | tf_op jit(solution)/shard_map/ppermute | solution.py:468
  15.2 0.9 %collective-permute-done.2 = bf16[128,128]{1,0:T(8,128)(2,1)S(1)} collective-permute-done((bf16[128,128]{1,0:T(8,128)(2,1)S(1)}, bf16[128,128]{1,0:T(8,128)(2,1)S(1)}, u32[]{:S(2)}, u32[]{:S(2)}) %collective-permute-start.2) | collective-permute-done | bytes 32800 | tf_op jit(solution)/shard_map/ppermute | solution.py:468
  16.0 2.3 %collective-permute-start.3 = (bf16[128,128]{1,0:T(8,128)(2,1)S(1)}, bf16[128,128]{1,0:T(8,128)(2,1)S(1)}, u32[]{:S(2)}, u32[]{:S(2)}) collective-permute-start(bf16[128,128]{1,0:T(8,128)(2,1)S(1)} %add.3.part_ref), channel_id=1, source_target_pairs={{0,2},{1,3},{2,0},{3,1},{4,6},{5,7},{6,4},{7,5},{8,10},{9,11},{10,... | collective-permute-start | bytes 98312 | tf_op jit(solution)/shard_map/ppermute | solution.py:468
  18.3 1.1 %shard_map.152.shift_ref = f32[2,64,128]{2,1,0:T(8,128)S(1)} custom-call(bf16[64,64]{1,0:T(8,128)(2,1)S(1)} %get-tuple-element.10.matrix_ref, f32[14,64,128]{2,1,0:T(8,128)S(1)} %get-tuple-element.7.pre_ref, f32[32,8192]{1,0:T(8,128)S(1)} %get-tuple-element.9.coef_ref, bf16[128,128]{1,0:T(8,128)(2,1)S(1)} %shard_map.151.after_ref), custom_call_target="tpu_custom_call" | custom-call | flops 40000000 | bytes 2000000 | tf_op jit(solution)/shard_map/pallas_call | solution.py:454
  19.4 0.8 %collective-permute-done.3.rest_ref = bf16[128,128]{1,0:T(8,128)(2,1)S(1)} collective-permute-done((bf16[128,128]{1,0:T(8,128)(2,1)S(1)}, bf16[128,128]{1,0:T(8,128)(2,1)S(1)}, u32[]{:S(2)}, u32[]{:S(2)}) %collective-permute-start.3) | collective-permute-done | bytes 32800 | tf_op jit(solution)/shard_map/ppermute | solution.py:468
  20.2 0.8 %shard_map.153 = (f32[2,8192]{1,0:T(2,128)}, f32[2,8192]{1,0:T(2,128)}, f32[2,8192]{1,0:T(2,128)}) custom-call(bf16[128,128]{1,0:T(8,128)(2,1)S(1)} %add.3.part_ref, bf16[128,128]{1,0:T(8,128)(2,1)S(1)} %collective-permute-done.3.rest_ref, f32[2,64,128]{2,1,0:T(8,128)S(1)} %shard_map.152.shift_ref, f32[14,64,128]{2,1,0:T(8,128)S(1)} %get-tuple-element.7.pre_ref), custom_call_target="tpu_custom_call" | custom-call | tf_op jit(solution)/shard_map/pallas_call | solution.py:470
  (1 shorter events, 0.0 us)
Async XLA Ops:
  1.8 8.2 %collective-permute-start.1 = (bf16[272,256]{1,0:T(8,128)(2,1)S(1)}, bf16[272,256]{1,0:T(8,128)(2,1)S(1)}, u32[]{:S(2)}, u32[]{:S(2)}) collective-permute-start(bf16[272,256]{1,0:T(8,128)(2,1)S(1)} %shard_map.148), channel_id=1, source_target_pairs={{24,0},{5,1},{10,2},{23,3},{28,4},{1,5},{14,6},{19,7},{16,8},{13,9... | collective-permute-start | bytes 417800 | tf_op jit(solution)/shard_map/ppermute | solution.py:398
  6.9 4.9 %collective-permute-start = (bf16[272,256]{1,0:T(8,128)(2,1)S(1)}, bf16[272,256]{1,0:T(8,128)(2,1)S(1)}, u32[]{:S(2)}, u32[]{:S(2)}) collective-permute-start(bf16[272,256]{1,0:T(8,128)(2,1)S(1)} %shard_map.148), channel_id=1, source_target_pairs={{0,0},{29,1},{18,2},{15,3},{4,4},{25,5},{22,6},{11,7},{8,8},{21,9}... | collective-permute-start | bytes 417800 | tf_op jit(solution)/shard_map/ppermute | solution.py:398
  13.5 2.5 %collective-permute-start.2 = (bf16[128,128]{1,0:T(8,128)(2,1)S(1)}, bf16[128,128]{1,0:T(8,128)(2,1)S(1)}, u32[]{:S(2)}, u32[]{:S(2)}) collective-permute-start(bf16[128,128]{1,0:T(8,128)(2,1)S(1)} %shard_map.151.after_ref), channel_id=1, source_target_pairs={{0,1},{1,0},{2,3},{3,2},{4,5},{5,4},{6,7},{7,6},{8,9},{9,8},{10,11... | collective-permute-start | bytes 98312 | tf_op jit(solution)/shard_map/ppermute | solution.py:468
  16.0 4.2 %collective-permute-start.3 = (bf16[128,128]{1,0:T(8,128)(2,1)S(1)}, bf16[128,128]{1,0:T(8,128)(2,1)S(1)}, u32[]{:S(2)}, u32[]{:S(2)}) collective-permute-start(bf16[128,128]{1,0:T(8,128)(2,1)S(1)} %add.3.part_ref), channel_id=1, source_target_pairs={{0,2},{1,3},{2,0},{3,1},{4,6},{5,7},{6,4},{7,5},{8,10},{9,11},{10,... | collective-permute-start | bytes 98312 | tf_op jit(solution)/shard_map/ppermute | solution.py:468

commit v9 on v8

--- a/solution.py
+++ b/solution.py
@@ -18,7 +18,7 @@
 REACH = BAND + 3
 EXTRA = 16
 CENTRE = 1.4
-PREPARE_STEP = 8
+PREPARE_STEP = 32
 SHIFT_STEP = 32
 SURFACE_STEP = 64
 
@@ -78,8 +78,8 @@
             first = [((tile * per_tile + i) * TILES + half) * LANES for i in range(per_tile)]
             stacked = jnp.concatenate([log_vol_ref[:, c : c + LANES] for c in first], axis=0)
             out_ref[half * LANES : (half + 1) * LANES, tile * LANES : (tile + 1) * LANES] = (
-                jnp.transpose(stacked) + CENTRE
-            ).astype(BF16)
+                jnp.transpose((stacked + CENTRE).astype(BF16))
+            )
     copies[steps].wait()
     copies[steps + 1].wait()
     row = lax.broadcasted_iota(jnp.int32, (EXTRA, LANES), 0)

time: 21.3 us -> 21.2 us (level)
  no operation moved by 1% of the time
where the time goes in v9:
time: 21.2 us; the launch traced here: 21 us
  starting transfers between devices  9.69 us (46%)
  Pallas kernels  8.52 us (40%)
  waiting for transfers between devices  2.07 us (10%)
  between operations  0.68 us (3%)
    ppermute x2, starting transfers between devices, shards(): received[k] = lax.ppermute(message, ('trade', 'scen'), pairs)  5.77 us
    ppermute x2, starting transfers between devices, shards(): lax.ppermute(partial_levels, 'scen', [(i, i ^ hop) for i in range(n_scen)])  3.92 us
    pallas_call x2, Pallas kernels, shards(): pl.pallas_call(functools.partial(surface_kernel, k, owned, SURFACE_STEP),...  3.46 us
    pallas_call x1, Pallas kernels, shards(): pl.pallas_call(functools.partial(prepare_kernel, n_trade, n_scen, owned,...  2.04 us
    ppermute x2, waiting for transfers between devices, shards(): lax.ppermute(partial_levels, 'scen', [(i, i ^ hop) for i in range(n_scen)])  1.65 us
    pallas_call x1, Pallas kernels, shards(): pl.pallas_call(pack_kernel, out_shape=pltpu.VMEM((WIDE + EXTRA, BLOCKS *...  1.11 us
    pallas_call x1, Pallas kernels, shards(): pl.pallas_call(functools.partial(shift_kernel, SHIFT_STEP), out_shape=plt...  1.11 us
    pallas_call x1, Pallas kernels, shards(): pl.pallas_call(value_kernel, out_shape=(jax.ShapeDtypeStruct((scenarios,...  0.8 us
  transfers between devices with their start and end apart: 4, of which 3 were waited for; matrix products, arithmetic and copies ran while one was open for 0% of the time, Pallas kernels for 23%

profile of v9, /device:TPU:0, one launch (start us, length us, event | category | flops | bytes accessed | tf_op | source)
XLA Modules:
  0.0 21.0 jit_solution(3644168004405917809)
XLA Ops:
  0.6 1.1 %shard_map.148 = bf16[272,256]{1,0:T(8,128)(2,1)S(1)} custom-call(s32[2]{0:T(128)} %hot_in.1, f32[32,2048]{1,0:T(8,128)} %log_vol_in.1, f32[1,32]{1,0:T(1,128)} %bitcast.17), custom_call_target="tpu_custom_call" | custom-call | tf_op jit(solution)/shard_map/pallas_call | solution.py:375
  1.8 5.1 %collective-permute-start.1 = (bf16[272,256]{1,0:T(8,128)(2,1)S(1)}, bf16[272,256]{1,0:T(8,128)(2,1)S(1)}, u32[]{:S(2)}, u32[]{:S(2)}) collective-permute-start(bf16[272,256]{1,0:T(8,128)(2,1)S(1)} %shard_map.148), channel_id=1, source_target_pairs={{24,0},{5,1},{10,2},{23,3},{28,4},{1,5},{14,6},{19,7},{16,8},{13,9... | collective-permute-start | bytes 417800 | tf_op jit(solution)/shard_map/ppermute | solution.py:398
  6.9 0.7 %collective-permute-start = (bf16[272,256]{1,0:T(8,128)(2,1)S(1)}, bf16[272,256]{1,0:T(8,128)(2,1)S(1)}, u32[]{:S(2)}, u32[]{:S(2)}) collective-permute-start(bf16[272,256]{1,0:T(8,128)(2,1)S(1)} %shard_map.148), channel_id=1, source_target_pairs={{0,0},{29,1},{18,2},{15,3},{4,4},{25,5},{22,6},{11,7},{8,8},{21,9}... | collective-permute-start | bytes 417800 | tf_op jit(solution)/shard_map/ppermute | solution.py:398
  7.5 2.0 %shard_map.149 = (f32[14,64,128]{2,1,0:T(8,128)S(1)}, f32[16,8192]{1,0:T(8,128)S(1)}, f32[32,8192]{1,0:T(8,128)S(1)}, bf16[64,64]{1,0:T(8,128)(2,1)S(1)}) custom-call(s32[2]{0:T(128)} %scen_in.1, bf16[512,2048]{1,0:T(8,128)(2,1)} %shock_ref.1, s32[64,128]{1,0:T(8,128)} %bitcast.9, s32[64,128]{1,0:T(8,128)} %bitcast.10, s32[64,128]{1,0:T(8,128)} %bitcast.11, ...), custom_call_target="tpu_custom_call" | custom-call | flops 40000000 | bytes 6000000 | tf_op jit(solution)/shard_map/pallas_call | solution.py:413
  9.6 0.4 %collective-permute-done.1.message_ref = bf16[272,256]{1,0:T(8,128)(2,1)S(1)} collective-permute-done((bf16[272,256]{1,0:T(8,128)(2,1)S(1)}, bf16[272,256]{1,0:T(8,128)(2,1)S(1)}, u32[]{:S(2)}, u32[]{:S(2)}) %collective-permute-start.1) | collective-permute-done | bytes 139296 | tf_op jit(solution)/shard_map/ppermute | solution.py:398
  10.0 1.7 %shard_map.150.refs_0_ = bf16[128,128]{1,0:T(8,128)(2,1)S(1)} custom-call(bf16[272,256]{1,0:T(8,128)(2,1)S(1)} %collective-permute-done.1.message_ref, f32[14,64,128]{2,1,0:T(8,128)S(1)} %get-tuple-element.7.pre_ref, f32[16,8192]{1,0:T(8,128)S(1)} %get-tuple-element.8.mix_ref, f32[32,8192]{1,0:T(8,128)S(1)} %get-tuple-element.9.coef_ref), custom_call_target="tpu_custom_call" | custom-call | tf_op jit(solution)/shard_map/pallas_call | solution.py:441
  11.7 0.0 collective-permute-done.message_ref
  11.7 1.7 %shard_map.151.after_ref = bf16[128,128]{1,0:T(8,128)(2,1)S(1)} custom-call(bf16[272,256]{1,0:T(8,128)(2,1)S(1)} %collective-permute-done.message_ref, f32[14,64,128]{2,1,0:T(8,128)S(1)} %get-tuple-element.7.pre_ref, f32[16,8192]{1,0:T(8,128)S(1)} %get-tuple-element.8.mix_ref, f32[32,8192]{1,0:T(8,128)S(1)} %get-tuple-element.9.coef_ref, ...), custom_call_target="tpu_custom_call" | custom-call | tf_op jit(solution)/shard_map/pallas_call | solution.py:441
  13.5 1.6 %collective-permute-start.2 = (bf16[128,128]{1,0:T(8,128)(2,1)S(1)}, bf16[128,128]{1,0:T(8,128)(2,1)S(1)}, u32[]{:S(2)}, u32[]{:S(2)}) collective-permute-start(bf16[128,128]{1,0:T(8,128)(2,1)S(1)} %shard_map.151.after_ref), channel_id=1, source_target_pairs={{0,1},{1,0},{2,3},{3,2},{4,5},{5,4},{6,7},{7,6},{8,9},{9,8},{10,11... | collective-permute-start | bytes 98312 | tf_op jit(solution)/shard_map/ppermute | solution.py:468
  15.1 0.9 %collective-permute-done.2 = bf16[128,128]{1,0:T(8,128)(2,1)S(1)} collective-permute-done((bf16[128,128]{1,0:T(8,128)(2,1)S(1)}, bf16[128,128]{1,0:T(8,128)(2,1)S(1)}, u32[]{:S(2)}, u32[]{:S(2)}) %collective-permute-start.2) | collective-permute-done | bytes 32800 | tf_op jit(solution)/shard_map/ppermute | solution.py:468
  16.0 2.3 %collective-permute-start.3 = (bf16[128,128]{1,0:T(8,128)(2,1)S(1)}, bf16[128,128]{1,0:T(8,128)(2,1)S(1)}, u32[]{:S(2)}, u32[]{:S(2)}) collective-permute-start(bf16[128,128]{1,0:T(8,128)(2,1)S(1)} %add.3.part_ref), channel_id=1, source_target_pairs={{0,2},{1,3},{2,0},{3,1},{4,6},{5,7},{6,4},{7,5},{8,10},{9,11},{10,... | collective-permute-start | bytes 98312 | tf_op jit(solution)/shard_map/ppermute | solution.py:468
  18.3 1.1 %shard_map.152.shift_ref = f32[2,64,128]{2,1,0:T(8,128)S(1)} custom-call(bf16[64,64]{1,0:T(8,128)(2,1)S(1)} %get-tuple-element.10.matrix_ref, f32[14,64,128]{2,1,0:T(8,128)S(1)} %get-tuple-element.7.pre_ref, f32[32,8192]{1,0:T(8,128)S(1)} %get-tuple-element.9.coef_ref, bf16[128,128]{1,0:T(8,128)(2,1)S(1)} %shard_map.151.after_ref), custom_call_target="tpu_custom_call" | custom-call | flops 40000000 | bytes 2000000 | tf_op jit(solution)/shard_map/pallas_call | solution.py:454
  19.4 0.8 %collective-permute-done.3.rest_ref = bf16[128,128]{1,0:T(8,128)(2,1)S(1)} collective-permute-done((bf16[128,128]{1,0:T(8,128)(2,1)S(1)}, bf16[128,128]{1,0:T(8,128)(2,1)S(1)}, u32[]{:S(2)}, u32[]{:S(2)}) %collective-permute-start.3) | collective-permute-done | bytes 32800 | tf_op jit(solution)/shard_map/ppermute | solution.py:468
  20.2 0.8 %shard_map.153 = (f32[2,8192]{1,0:T(2,128)}, f32[2,8192]{1,0:T(2,128)}, f32[2,8192]{1,0:T(2,128)}) custom-call(bf16[128,128]{1,0:T(8,128)(2,1)S(1)} %add.3.part_ref, bf16[128,128]{1,0:T(8,128)(2,1)S(1)} %collective-permute-done.3.rest_ref, f32[2,64,128]{2,1,0:T(8,128)S(1)} %shard_map.152.shift_ref, f32[14,64,128]{2,1,0:T(8,128)S(1)} %get-tuple-element.7.pre_ref), custom_call_target="tpu_custom_call" | custom-call | tf_op jit(solution)/shard_map/pallas_call | solution.py:470
  (1 shorter events, 0.0 us)
Async XLA Ops:
  1.8 8.2 %collective-permute-start.1 = (bf16[272,256]{1,0:T(8,128)(2,1)S(1)}, bf16[272,256]{1,0:T(8,128)(2,1)S(1)}, u32[]{:S(2)}, u32[]{:S(2)}) collective-permute-start(bf16[272,256]{1,0:T(8,128)(2,1)S(1)} %shard_map.148), channel_id=1, source_target_pairs={{24,0},{5,1},{10,2},{23,3},{28,4},{1,5},{14,6},{19,7},{16,8},{13,9... | collective-permute-start | bytes 417800 | tf_op jit(solution)/shard_map/ppermute | solution.py:398
  6.9 4.9 %collective-permute-start = (bf16[272,256]{1,0:T(8,128)(2,1)S(1)}, bf16[272,256]{1,0:T(8,128)(2,1)S(1)}, u32[]{:S(2)}, u32[]{:S(2)}) collective-permute-start(bf16[272,256]{1,0:T(8,128)(2,1)S(1)} %shard_map.148), channel_id=1, source_target_pairs={{0,0},{29,1},{18,2},{15,3},{4,4},{25,5},{22,6},{11,7},{8,8},{21,9}... | collective-permute-start | bytes 417800 | tf_op jit(solution)/shard_map/ppermute | solution.py:398
  13.5 2.5 %collective-permute-start.2 = (bf16[128,128]{1,0:T(8,128)(2,1)S(1)}, bf16[128,128]{1,0:T(8,128)(2,1)S(1)}, u32[]{:S(2)}, u32[]{:S(2)}) collective-permute-start(bf16[128,128]{1,0:T(8,128)(2,1)S(1)} %shard_map.151.after_ref), channel_id=1, source_target_pairs={{0,1},{1,0},{2,3},{3,2},{4,5},{5,4},{6,7},{7,6},{8,9},{9,8},{10,11... | collective-permute-start | bytes 98312 | tf_op jit(solution)/shard_map/ppermute | solution.py:468
  16.0 4.2 %collective-permute-start.3 = (bf16[128,128]{1,0:T(8,128)(2,1)S(1)}, bf16[128,128]{1,0:T(8,128)(2,1)S(1)}, u32[]{:S(2)}, u32[]{:S(2)}) collective-permute-start(bf16[128,128]{1,0:T(8,128)(2,1)S(1)} %add.3.part_ref), channel_id=1, source_target_pairs={{0,2},{1,3},{2,0},{3,1},{4,6},{5,7},{6,4},{7,5},{8,10},{9,11},{10,... | collective-permute-start | bytes 98312 | tf_op jit(solution)/shard_map/ppermute | solution.py:468
